TPU v7x, 32 devices: a whole 2x2x4 slice. The times are simulated.
32 devices in a mesh: dp: 4 (over y, core), wide: 8 (over z, x).
Axes of the slice: x: 2, y: 2, z: 4, core: 2. Of those that a mesh axis runs over, the one named last changes fastest.
Arguments:
- block_in: bfloat16 [4, 4, 8192, 512], P(None, 'dp', 'wide'), may hold values from -6 to 6
- cotangent: bfloat16 [4, 4, 8192, 512], P(None, 'dp', 'wide'), may hold values from -6 to 6
- ln1_gain: bfloat16 [512], P('wide'), may hold values from 0.5 to 1.5
- ln1_bias: bfloat16 [512], P('wide'), may hold values from -1.5 to 1.5
- qkv_weight: bfloat16 [512, 1536], P('wide'), may hold values from -0.25 to 0.25
- out_weight: bfloat16 [512, 512], P('wide'), may hold values from -0.75 to 0.75
- ln2_gain: bfloat16 [512], P('wide'), may hold values from 0.5 to 1.5
- ln2_bias: bfloat16 [512], P('wide'), may hold values from -1.5 to 1.5
- up_weight: bfloat16 [512, 2048], P('wide'), may hold values from -0.25 to 0.25
- up_bias: bfloat16 [2048], P('wide'), may hold values from -1.5 to 1.5
- down_weight: bfloat16 [2048, 512], P('wide'), may hold values from -0.125 to 0.125
- down_bias: bfloat16 [512], P('wide'), may hold values from -1.5 to 1.5
- seq_lengths: int32 [4, 4, 8], P(None, 'dp'), may hold values from 1 to 8185, as said below
Outputs:
- block_out: bfloat16 [4, 4, 8192, 512], P(None, 'dp', 'wide')
- grad_input: float32 [4, 4, 8192, 512], P(None, 'dp', 'wide')
- grad_ln1_gain: float32 [512], P('wide')
- grad_ln1_bias: float32 [512], P('wide')
- grad_qkv_weight: float32 [512, 1536], P('wide')
- grad_out_weight: float32 [512, 512], P('wide')
- grad_ln2_gain: float32 [512], P('wide')
- grad_ln2_bias: float32 [512], P('wide')
- grad_up_weight: float32 [512, 2048], P('wide')
- grad_up_bias: float32 [2048], P('wide')
- grad_down_weight: float32 [2048, 512], P('wide')
- grad_down_bias: float32 [512], P('wide')
Inputs may be any that keep to these rules, and one draw needn't show every extreme that they name: `seq_lengths`: for each micro-batch and group, 8 lengths of 1 or more that sum to 8192; the fourth is the longest and begins within the group's first 1024 positions and ends within its last 1024; in every draw some group's fourth sequence is 8185 long.
All inputs are finite; a program needn't handle non-finite values.
Results may differ from a plain program's by a relative error of at most 0.019.
Values may be sent and summed in bfloat16 or wider, within the bound.
A program may use at most 320 MiB of HBM per device.

v0:
```python
import jax
import jax.numpy as jnp
from jax import lax
from jax.sharding import PartitionSpec as P

HEADS = 8


EPSILON = 1e-05


def entering(array, axis, combine, identity):
    count, index = (lax.axis_size(axis), lax.axis_index(axis))
    everything = jax.tree.map(
        lambda part, kind: lax.all_gather(part.astype(kind), axis),
        array,
        (jnp.bfloat16, jnp.bfloat16, jnp.bfloat16),
    )
    start = jax.tree.map(
        lambda part, zero: jnp.broadcast_to(jnp.asarray(zero, part.dtype), part.shape),
        array,
        identity,
    )

    def hop(k, before):
        reached = k < index
        new = combine(
            before, jax.tree.map(lambda part, own: part[k].astype(own.dtype), everything, array)
        )
        return jax.tree.map(lambda a, b: jnp.where(reached, a, b), new, before)

    return lax.fori_loop(0, count, hop, start)


def entering_2(array, axis, combine, identity):
    count, index = (lax.axis_size(axis), lax.axis_index(axis))
    everything = jax.tree.map(
        lambda part, kind: lax.all_gather(part.astype(kind), axis),
        array,
        jax.tree.map(lambda a: jnp.bfloat16 if a.dtype == jnp.float32 else a.dtype, array),
    )
    start = jax.tree.map(
        lambda part, zero: jnp.broadcast_to(jnp.asarray(zero, part.dtype), part.shape),
        array,
        identity,
    )

    def hop(k, before):
        at = count - 1 - k
        reached = at > index
        new = combine(
            before, jax.tree.map(lambda part, own: part[at].astype(own.dtype), everything, array)
        )
        return jax.tree.map(lambda a, b: jnp.where(reached, a, b), new, before)

    return lax.fori_loop(0, count, hop, start)


def layer_norm(values, gain, shift):
    average = jnp.mean(values, axis=-1, keepdims=True)
    centred = values - average
    spread = jnp.mean(centred * centred, axis=-1, keepdims=True)
    return centred * lax.rsqrt(spread + EPSILON) * gain + shift


def feature(values):
    return jax.nn.elu(values) + 1.0


def segment_starts(lengths, places):
    seq_ends = jnp.cumsum(lengths, axis=-1)
    closed = seq_ends[..., None, :] <= places[:, None]
    return jnp.sum(jnp.where(closed, lengths[..., None, :], 0), axis=-1)


def carry_on(earlier, following):
    early_state, early_norm, early_flag = earlier
    late_state, late_norm, late_flag = following
    through = 1.0 - late_flag
    return (
        late_state + through[:, None, None, None] * early_state,
        late_norm + through[:, None, None] * early_norm,
        jnp.maximum(early_flag, late_flag),
    )


def block_masks(starts, offset):
    block_rows = starts.shape[0]
    positions = jnp.arange(block_rows, dtype=jnp.int32)
    allowed = (positions[:, None] >= positions[None, :]) & (starts[:, None] == starts[None, :])
    sees_state = (starts < offset).astype(jnp.float32)
    return (allowed, sees_state)


def block_scores(query_part, key_part, allowed):
    scores = jnp.einsum("the,she->hts", query_part, key_part, preferred_element_type=jnp.float32)
    return jnp.where(allowed[None], scores, 0.0).astype(jnp.bfloat16)


def per_device(
    block_in,
    cotangent,
    ln1_gain,
    ln1_bias,
    qkv_weight,
    out_weight,
    ln2_gain,
    ln2_bias,
    up_weight,
    up_bias,
    down_weight,
    down_bias,
    seq_lengths,
):
    micro_count, token_count, model_width = (
        block_in.shape[0],
        block_in.shape[2],
        block_in.shape[3],
    )
    gathered = (
        lax.all_gather(ln1_gain, "wide", axis=0, tiled=True),
        lax.all_gather(ln1_bias, "wide", axis=0, tiled=True),
        lax.all_gather(qkv_weight, "wide", axis=0, tiled=True),
        lax.all_gather(out_weight, "wide", axis=0, tiled=True),
        lax.all_gather(ln2_gain, "wide", axis=0, tiled=True),
        lax.all_gather(ln2_bias, "wide", axis=0, tiled=True),
        lax.all_gather(up_weight, "wide", axis=0, tiled=True),
        lax.all_gather(up_bias, "wide", axis=0, tiled=True),
        lax.all_gather(down_weight, "wide", axis=0, tiled=True),
        lax.all_gather(down_bias, "wide", axis=0, tiled=True),
    )
    gain_one = gathered[0].astype(jnp.float32)
    bias_one = gathered[1].astype(jnp.float32)
    gain_two = gathered[4].astype(jnp.float32)
    bias_two = gathered[5].astype(jnp.float32)
    up_shift = gathered[7].astype(jnp.float32)
    down_shift = gathered[9].astype(jnp.float32)
    offset = lax.axis_index("wide") * token_count
    places = offset + jnp.arange(token_count, dtype=jnp.int32)
    starts = segment_starts(seq_lengths.reshape(micro_count, -1), places)
    tokens = block_in.reshape(micro_count * token_count, model_width).astype(jnp.float32)
    normed = layer_norm(tokens, gain_one, bias_one).astype(jnp.bfloat16)
    projected = jnp.dot(normed, gathered[2], preferred_element_type=jnp.float32).reshape(
        micro_count, token_count, 3, HEADS, -1
    )
    query_raw = projected[:, :, 0]
    key_raw = projected[:, :, 1]
    query_feat = feature(query_raw).astype(jnp.bfloat16)
    key_feat = feature(key_raw).astype(jnp.bfloat16)
    values = projected[:, :, 2].astype(jnp.bfloat16)
    final_start = starts[:, -1]
    in_last = starts == final_start[:, None]
    last_keys = jnp.where(in_last[:, :, None, None], key_feat, jnp.zeros_like(key_feat))
    local_state = jnp.einsum(
        "mthe,mthf->mhef", last_keys, values, preferred_element_type=jnp.float32
    )
    local_norm = jnp.sum(last_keys.astype(jnp.float32), axis=1)
    cut_flag = (final_start >= offset).astype(jnp.float32)
    identity = (jnp.zeros_like(local_state), jnp.zeros_like(local_norm), jnp.zeros_like(cut_flag))
    state_in, norm_in, _ = entering((local_state, local_norm, cut_flag), "wide", carry_on, identity)
    state_low = state_in.astype(jnp.bfloat16)

    def attend(block_items):
        query_part, key_part, value_part, start_part, state_part, norm_part = block_items
        allowed, sees_state = block_masks(start_part, offset)
        scores = block_scores(query_part, key_part, allowed)
        query_wide = query_part.astype(jnp.float32)
        numerator = jnp.einsum(
            "hts,shf->thf", scores, value_part, preferred_element_type=jnp.float32
        ) + sees_state[:, None, None] * jnp.einsum(
            "the,hef->thf", query_part, state_part, preferred_element_type=jnp.float32
        )
        denominator = jnp.sum(scores.astype(jnp.float32), axis=-1).T + sees_state[
            :, None
        ] * jnp.sum(query_wide * norm_part[None], axis=-1)
        return (numerator, denominator)

    numerator, denominator = lax.map(
        attend, (query_feat, key_feat, values, starts, state_low, norm_in)
    )
    mixed = (
        (numerator / denominator[..., None])
        .reshape(micro_count * token_count, model_width)
        .astype(jnp.bfloat16)
    )
    branch = jnp.dot(mixed, gathered[3], preferred_element_type=jnp.float32)
    middle = tokens + branch
    second = layer_norm(middle, gain_two, bias_two).astype(jnp.bfloat16)
    hidden = jnp.dot(second, gathered[6], preferred_element_type=jnp.float32) + up_shift
    active = jax.nn.gelu(hidden).astype(jnp.bfloat16)
    output = jnp.dot(active, gathered[8], preferred_element_type=jnp.float32) + down_shift
    result = (middle + output).astype(jnp.bfloat16).reshape(block_in.shape)
    weights_back = (
        lax.all_gather(ln1_gain, "wide", axis=0, tiled=True),
        lax.all_gather(ln1_bias, "wide", axis=0, tiled=True),
        lax.all_gather(qkv_weight, "wide", axis=0, tiled=True),
        lax.all_gather(out_weight, "wide", axis=0, tiled=True),
        lax.all_gather(ln2_gain, "wide", axis=0, tiled=True),
        lax.all_gather(ln2_bias, "wide", axis=0, tiled=True),
        lax.all_gather(up_weight, "wide", axis=0, tiled=True),
        lax.all_gather(up_bias, "wide", axis=0, tiled=True),
        lax.all_gather(down_weight, "wide", axis=0, tiled=True),
        lax.all_gather(down_bias, "wide", axis=0, tiled=True),
    )
    upstream = cotangent.reshape(micro_count * token_count, model_width).astype(jnp.float32)
    out_grad = cotangent.reshape(micro_count * token_count, model_width)
    grad_down = jnp.einsum("tf,td->fd", active, out_grad, preferred_element_type=jnp.float32)
    grad_down_bias = jnp.sum(upstream, axis=0)
    active_grad = jnp.einsum(
        "td,fd->tf", out_grad, weights_back[8], preferred_element_type=jnp.float32
    )
    _, gelu_pull = jax.vjp(jax.nn.gelu, hidden)
    hidden_grad = gelu_pull(active_grad)[0].astype(jnp.bfloat16)
    grad_up = jnp.einsum("td,tf->df", second, hidden_grad, preferred_element_type=jnp.float32)
    grad_up_bias = jnp.sum(hidden_grad.astype(jnp.float32), axis=0)
    second_grad = jnp.einsum(
        "tf,df->td", hidden_grad, weights_back[6], preferred_element_type=jnp.float32
    )
    _, norm_two_pull = jax.vjp(layer_norm, middle, gain_two, bias_two)
    middle_grad, grad_gain_two, grad_bias_two = norm_two_pull(second_grad)
    middle_grad = middle_grad + upstream
    branch_grad = middle_grad.astype(jnp.bfloat16)
    grad_out = jnp.einsum("td,te->de", mixed, branch_grad, preferred_element_type=jnp.float32)
    mixed_grad = jnp.einsum(
        "te,de->td", branch_grad, weights_back[3], preferred_element_type=jnp.float32
    ).reshape(micro_count, token_count, HEADS, -1)
    numer_grad = (mixed_grad / denominator[..., None]).astype(jnp.bfloat16)
    denom_grad = -jnp.sum(mixed_grad * numerator, axis=-1) / (denominator * denominator)
    sees_all = starts < offset
    query_seen = jnp.where(sees_all[:, :, None, None], query_feat, jnp.zeros_like(query_feat))
    use_state = jnp.einsum(
        "mthe,mthf->mhef", query_seen, numer_grad, preferred_element_type=jnp.float32
    )
    use_norm = jnp.sum(query_seen.astype(jnp.float32) * denom_grad[..., None], axis=1)
    state_out, norm_out, _ = entering_2((use_state, use_norm, cut_flag), "wide", carry_on, identity)
    state_out_low = state_out.astype(jnp.bfloat16)

    def attend_back(block_items):
        (
            query_part,
            key_part,
            value_part,
            start_part,
            state_part,
            norm_part,
            num_grad,
            den_grad,
            state_grad,
            norm_grad,
        ) = block_items
        allowed, sees_state = block_masks(start_part, offset)
        in_final = (start_part == start_part[-1]).astype(jnp.float32)
        scores = block_scores(query_part, key_part, allowed)
        score_grad = (
            jnp.einsum("thf,shf->hts", num_grad, value_part, preferred_element_type=jnp.float32)
            + den_grad.T[:, :, None]
        )
        score_grad = jnp.where(allowed[None], score_grad, 0.0).astype(jnp.bfloat16)
        query_grad = jnp.einsum(
            "hts,she->the", score_grad, key_part, preferred_element_type=jnp.float32
        ) + sees_state[:, None, None] * (
            jnp.einsum("thf,hef->the", num_grad, state_part, preferred_element_type=jnp.float32)
            + den_grad[:, :, None] * norm_part[None]
        )
        key_grad = jnp.einsum(
            "hts,the->she", score_grad, query_part, preferred_element_type=jnp.float32
        ) + in_final[:, None, None] * (
            jnp.einsum("thf,hef->the", value_part, state_grad, preferred_element_type=jnp.float32)
            + norm_grad[None]
        )
        value_grad = jnp.einsum(
            "hts,thf->shf", scores, num_grad, preferred_element_type=jnp.float32
        ) + in_final[:, None, None] * jnp.einsum(
            "the,hef->thf", key_part, state_grad, preferred_element_type=jnp.float32
        )
        return (query_grad, key_grad, value_grad)

    query_grad, key_grad, value_grad = lax.map(
        attend_back,
        (
            query_feat,
            key_feat,
            values,
            starts,
            state_low,
            norm_in,
            numer_grad,
            denom_grad,
            state_out_low,
            norm_out,
        ),
    )
    _, query_pull = jax.vjp(feature, query_raw)
    _, key_pull = jax.vjp(feature, key_raw)
    projected_grad = jnp.stack(
        [query_pull(query_grad)[0], key_pull(key_grad)[0], value_grad], axis=2
    )
    projected_grad = projected_grad.reshape(micro_count * token_count, 3 * model_width).astype(
        jnp.bfloat16
    )
    grad_qkv = jnp.einsum("td,tc->dc", normed, projected_grad, preferred_element_type=jnp.float32)
    normed_grad = jnp.einsum(
        "tc,dc->td", projected_grad, weights_back[2], preferred_element_type=jnp.float32
    )
    _, norm_one_pull = jax.vjp(layer_norm, tokens, gain_one, bias_one)
    input_grad, grad_gain_one, grad_bias_one = norm_one_pull(normed_grad)
    input_grad = (input_grad + middle_grad).reshape(block_in.shape)
    shares = (
        lax.psum_scatter(
            grad_gain_one.astype(jnp.bfloat16), "wide", scatter_dimension=0, tiled=True
        ).astype(jnp.float32),
        lax.psum_scatter(
            grad_bias_one.astype(jnp.bfloat16), "wide", scatter_dimension=0, tiled=True
        ).astype(jnp.float32),
        lax.psum_scatter(
            grad_qkv.astype(jnp.bfloat16), "wide", scatter_dimension=0, tiled=True
        ).astype(jnp.float32),
        lax.psum_scatter(
            grad_out.astype(jnp.bfloat16), "wide", scatter_dimension=0, tiled=True
        ).astype(jnp.float32),
        lax.psum_scatter(
            grad_gain_two.astype(jnp.bfloat16), "wide", scatter_dimension=0, tiled=True
        ).astype(jnp.float32),
        lax.psum_scatter(
            grad_bias_two.astype(jnp.bfloat16), "wide", scatter_dimension=0, tiled=True
        ).astype(jnp.float32),
        lax.psum_scatter(
            grad_up.astype(jnp.bfloat16), "wide", scatter_dimension=0, tiled=True
        ).astype(jnp.float32),
        lax.psum_scatter(
            grad_up_bias.astype(jnp.bfloat16), "wide", scatter_dimension=0, tiled=True
        ).astype(jnp.float32),
        lax.psum_scatter(
            grad_down.astype(jnp.bfloat16), "wide", scatter_dimension=0, tiled=True
        ).astype(jnp.float32),
        lax.psum_scatter(
            grad_down_bias.astype(jnp.bfloat16), "wide", scatter_dimension=0, tiled=True
        ).astype(jnp.float32),
    )
    shares = (
        lax.psum(shares[0].astype(jnp.bfloat16), "dp").astype(jnp.float32),
        lax.psum(shares[1].astype(jnp.bfloat16), "dp").astype(jnp.float32),
        lax.psum(shares[2].astype(jnp.bfloat16), "dp").astype(jnp.float32),
        lax.psum(shares[3].astype(jnp.bfloat16), "dp").astype(jnp.float32),
        lax.psum(shares[4].astype(jnp.bfloat16), "dp").astype(jnp.float32),
        lax.psum(shares[5].astype(jnp.bfloat16), "dp").astype(jnp.float32),
        lax.psum(shares[6].astype(jnp.bfloat16), "dp").astype(jnp.float32),
        lax.psum(shares[7].astype(jnp.bfloat16), "dp").astype(jnp.float32),
        lax.psum(shares[8].astype(jnp.bfloat16), "dp").astype(jnp.float32),
        lax.psum(shares[9].astype(jnp.bfloat16), "dp").astype(jnp.float32),
    )
    return (
        result,
        input_grad,
        shares[0],
        shares[1],
        shares[2],
        shares[3],
        shares[4],
        shares[5],
        shares[6],
        shares[7],
        shares[8],
        shares[9],
    )


def solution(mesh):
    return jax.shard_map(
        per_device,
        mesh=mesh,
        in_specs=(
            P(None, "dp", "wide", None),
            P(None, "dp", "wide", None),
            P("wide"),
            P("wide"),
            P("wide", None),
            P("wide", None),
            P("wide"),
            P("wide"),
            P("wide", None),
            P("wide"),
            P("wide", None),
            P("wide"),
            P(None, "dp", None),
        ),
        out_specs=(
            P(None, "dp", "wide", None),
            P(None, "dp", "wide", None),
            P("wide"),
            P("wide"),
            P("wide", None),
            P("wide", None),
            P("wide"),
            P("wide"),
            P("wide", None),
            P("wide"),
            P("wide", None),
            P("wide"),
        ),
        check_vma=False,
    )
```

profile of v0, /device:TPU:0, one launch (start us, length us, event | category | flops | bytes accessed | tf_op | source)
XLA Modules:
  0.0 1094.3 jit_solution(14036960306360957128)
XLA Ops:
  16.1 23.4 %all-reduce.13 = (bf16[512]{0:T(512)(128)(2,1)S(1)}, bf16[512]{0:T(512)(128)(2,1)S(1)}, bf16[32]{0:T(256)(128)(2,1)S(1)}, bf16[512]{0:T(512)(128)(2,1)S(1)}, bf16[512]{0:T(512)(128)(2,1)S(1)}) all-reduce(bf16[512]{0:T(512)(128)(2,1)S(1)} %dynamic-update-slice.1, ...), channel_id=1, replica_groups=mesh['dp'=4,'wide'=8] {'wide'}, use_global_device_ids=true, to_apply=%add.1 | all-reduce | flops 2080 | bytes 8320
  58.7 13.9 %fusion.102 = f32[4,1024,3,8,64]{1,4,3,2,0:T(8,128)} fusion(bf16[3,8,64,512,1]{3,2,1,0,4:T(8,128)(2,1)S(1)} %bitcast.391, bf16[4,1,1024,512]{3,2,1,0:T(8,128)(2,1)} %fusion.90), kind=kOutput, calls=%fused_computation.155 | convolution fusion | flops 6442450944 | bytes 30932992 | tf_op jit(solution)/shard_map/dot_general | solution.py:143
  90.7 33.0 %all_gather.70 = bf16[512,512]{1,0:T(8,128)(2,1)S(1)} all-gather(bf16[64,512]{1,0:T(8,128)(2,1)S(1)} %copy-done.26), channel_id=1, replica_groups=mesh['dp'=4,'wide'=8] {'wide'}, dimensions={0}, use_global_device_ids=true | all-gather | bytes 589824 | tf_op jit(solution)/shard_map/all_gather | solution.py:124
  123.7 18.9 %all-gather.5 = bf16[8,1,256]{2,1,0:T(2,128)(2,1)S(1)} all-gather(bf16[1,1,256]{2,1,0:T(2,128)(2,1)S(1)} %reshape.465), channel_id=1, replica_groups=mesh['dp'=4,'wide'=8] {'wide'}, dimensions={0}, use_global_device_ids=true | all-gather | bytes 4608 | tf_op jit(solution)/shard_map/all_gather | solution.py:128
  149.6 30.6 %all-gather.2 = bf16[32,8,64]{2,1,0:T(8,128)(2,1)S(1)} all-gather(bf16[4,8,64]{2,1,0:T(8,128)(2,1)S(1)} %get-tuple-element.745), channel_id=4, replica_groups=mesh['dp'=4,'wide'=8] {'wide'}, dimensions={0}, use_global_device_ids=true | all-gather | bytes 36864 | tf_op jit(solution)/shard_map/all_gather | solution.py:15
  180.2 12.4 %while.66 = (s32[]{:T(128)}, f32[4,8,64,64]{3,2,1,0:T(8,128)S(1)}, f32[4,8,64]{2,1,0:T(8,128)S(1)}, s32[]{:T(128)}, bf16[8,4,8,64,64]{4,3,2,1,0:T(8,128)(2,1)}, ...) while((s32[]{:T(128)}, f32[4,8,64,64]{3,2,1,0:T(8,128)S(1)}, ...), condition=%wide.region_6.7_spmd.clone.clone, body=%wide.region_5.6_spmd.clone.sunk.clone | while | flops 665612 | bytes 1331367 | solution.py:32
  193.2 257.8 %while.64 = (s32[]{:T(128)}, f32[4,1024,8,64]{1,0,3,2:T(4,128)}, f32[4,1024,8]{1,0,2:T(4,128)S(1)}, bf16[4,1024,8,64]{1,3,2,0:T(8,128)(2,1)}, s32[4,1024]{1,0:T(...) while((s32[]{:T(128)}, f32[4,1024,8,64]{1,0,3,2:T(4,128)}, ...), condition=%wide.region_10.11_spmd.clone, body=%wide.region_7.10_spmd.sunk.clone | while | flops 2253916160 | bytes 56038012 | solution.py:178
  217.0 38.8 %dynamic_update_slice.30 = f32[4,1024,8,64]{1,0,3,2:T(4,128)} dynamic-update-slice(f32[4,1024,8,64]{1,0,3,2:T(4,128)} %get-tuple-element.1164, f32[1,1024,8,64]{1,0,3,2:T(1,128)S(1)} %copy.124, s32[]{:T(128)} %get-tuple-element.1163, s32[]{:T(128)} %constant.176.clone.1..sunk.4, s32[]{:T(128)} %constant.176.clone.1..sunk.4, s32[]{:T(128)} %constant.176.clone.1..sunk.4) | dynamic-update-slice | bytes 4194308 | tf_op jit(solution)/shard_map/while/body/jit(dynamic_update_index_in_dim)/dynamic_update_slice | solution.py:178
  281.5 38.7 %dynamic_update_slice.30 = f32[4,1024,8,64]{1,0,3,2:T(4,128)} dynamic-update-slice(f32[4,1024,8,64]{1,0,3,2:T(4,128)} %get-tuple-element.1164, f32[1,1024,8,64]{1,0,3,2:T(1,128)S(1)} %copy.124, s32[]{:T(128)} %get-tuple-element.1163, s32[]{:T(128)} %constant.176.clone.1..sunk.4, s32[]{:T(128)} %constant.176.clone.1..sunk.4, s32[]{:T(128)} %constant.176.clone.1..sunk.4) | dynamic-update-slice | bytes 4194308 | tf_op jit(solution)/shard_map/while/body/jit(dynamic_update_index_in_dim)/dynamic_update_slice | solution.py:178
  345.8 38.7 %dynamic_update_slice.30 = f32[4,1024,8,64]{1,0,3,2:T(4,128)} dynamic-update-slice(f32[4,1024,8,64]{1,0,3,2:T(4,128)} %get-tuple-element.1164, f32[1,1024,8,64]{1,0,3,2:T(1,128)S(1)} %copy.124, s32[]{:T(128)} %get-tuple-element.1163, s32[]{:T(128)} %constant.176.clone.1..sunk.4, s32[]{:T(128)} %constant.176.clone.1..sunk.4, s32[]{:T(128)} %constant.176.clone.1..sunk.4) | dynamic-update-slice | bytes 4194308 | tf_op jit(solution)/shard_map/while/body/jit(dynamic_update_index_in_dim)/dynamic_update_slice | solution.py:178
  410.2 38.7 %dynamic_update_slice.30 = f32[4,1024,8,64]{1,0,3,2:T(4,128)} dynamic-update-slice(f32[4,1024,8,64]{1,0,3,2:T(4,128)} %get-tuple-element.1164, f32[1,1024,8,64]{1,0,3,2:T(1,128)S(1)} %copy.124, s32[]{:T(128)} %get-tuple-element.1163, s32[]{:T(128)} %constant.176.clone.1..sunk.4, s32[]{:T(128)} %constant.176.clone.1..sunk.4, s32[]{:T(128)} %constant.176.clone.1..sunk.4) | dynamic-update-slice | bytes 4194308 | tf_op jit(solution)/shard_map/while/body/jit(dynamic_update_index_in_dim)/dynamic_update_slice | solution.py:178
  466.8 25.9 %multiply_convert_fusion = (bf16[4096,2048]{1,0:T(8,128)(2,1)}, f32[4096,2048]{1,0:T(8,128)}) fusion(f32[2048]{0:T(1024)S(1)} %bitcast.402, bf16[512,2048]{1,0:T(8,128)(2,1)} %all-gather.14.cloned.1.call-done, f32[4096,512]{1,0:T(8,128)} %copy-done.4, f32[512]{0:T(512)S(1)} %convert_element_type.377, f32[512]{0:T(512)S(1)} %convert_element_type.376, ...), kind=kOutput, calls=%fused_computation.107 | convolution fusion | flops 8684306432 | bytes 60862464 | tf_op jit(solution)/shard_map/dot_general | solution.py:189
  492.7 35.0 %fusion.129 = (bf16[2048]{0:T(1024)(128)(2,1)}, bf16[4096,2048]{1,0:T(8,128)(2,1)}) fusion(f32[4096,2048]{1,0:T(8,128)} %get-tuple-element.772, f32[2048]{0:T(1024)S(1)} %bitcast.403, bf16[4096,512]{1,0:T(8,128)(2,1)} %bitcast.374, bf16[2048,512]{1,0:T(8,128)(2,1)} %all-gather.16.cloned.1.call-done), kind=kOutput, calls=%fused_computation.204 | convolution fusion | flops 8774481920 | bytes 56635392 | tf_op jit(solution)/shard_map/td,fd->tf/dot_general | solution.py:209
  527.7 18.3 %multiply_reduce_fusion.1 = (bf16[512]{0:T(512)(128)(2,1)}, f32[4096]{0:T(1024)S(1)}, bf16[512]{0:T(512)(128)(2,1)}, f32[4096,512]{1,0:T(8,128)}) fusion(f32[4096,512]{1,0:T(8,128)S(1)} %copy-done.5, f32[4096]{0:T(1024)S(1)} %fusion.114, f32[4096]{0:T(1024)S(1)} %broadcast_multiply_fusion, f32[512]{0:T(512)S(1)} %convert_element_type.376, ...), kind=kOutput, calls=%fused_computation.130 | convolution fusion | flops 8606707712 | bytes 35704832 | tf_op jit(solution)/shard_map/tf,df->td/dot_general | solution.py:216
  563.0 10.9 reshape.435
  594.9 18.9 %convolution_convert_fusion.2 = bf16[512,2048]{1,0:T(8,128)(2,1)} fusion(bf16[4096,2048]{1,0:T(8,128)(2,1)} %get-tuple-element.776, f32[4096,512]{1,0:T(8,128)} %copy-done.4, f32[512]{0:T(512)S(1)} %convert_element_type.377, f32[512]{0:T(512)S(1)} %convert_element_type.376, f32[4096]{0:T(1024)S(1)} %fusion.114, f32[4096]{0:T(1024)S(1)} %broadcast_multiply_fusion), kind=kOutput, calls=%fused_computation.164 | convolution fusion | flops 8601468928 | bytes 27299840 | tf_op jit(solution)/shard_map/td,tf->df/dot_general | solution.py:214
  634.7 30.7 %all-gather.4 = bf16[32,8,64]{2,1,0:T(8,128)(2,1)S(1)} all-gather(bf16[4,8,64]{2,1,0:T(8,128)(2,1)S(1)} %multiply_reduce_fusion.2), channel_id=6, replica_groups=mesh['dp'=4,'wide'=8] {'wide'}, dimensions={0}, use_global_device_ids=true | all-gather | bytes 36864 | tf_op jit(solution)/shard_map/all_gather | solution.py:38
  665.4 13.5 %convolution_convert_fusion.1 = bf16[2048,512]{1,0:T(8,128)(2,1)} fusion(bf16[4096,2048]{1,0:T(8,128)(2,1)} %get-tuple-element.771, bf16[4096,512]{1,0:T(8,128)(2,1)S(1)} %bitcast.375), kind=kOutput, calls=%fused_computation.163 | convolution fusion | flops 8590983168 | bytes 23068672 | tf_op jit(solution)/shard_map/tf,td->fd/dot_general | solution.py:207
  679.0 17.3 %while.67 = (s32[]{:T(128)}, f32[4,8,64,64]{3,2,1,0:T(8,128)S(1)}, f32[4,8,64]{2,1,0:T(8,128)S(1)}, s32[]{:T(128)}, bf16[8,4,8,64,64]{4,3,2,1,0:T(8,128)(2,1)}, ...) while((s32[]{:T(128)}, f32[4,8,64,64]{3,2,1,0:T(8,128)S(1)}, ...), condition=%wide.region_18.19_spmd.clone.clone, body=%wide.region_17.18_spmd.clone.sunk.clone | while | flops 665616 | bytes 1331413 | solution.py:56
  697.3 216.3 %while.65 = (s32[]{:T(128)}, f32[4,1024,8,64]{1,3,2,0:T(8,128)}, f32[4,1024,8,64]{1,3,2,0:T(8,128)}, bf16[4,1024,8,64]{1,3,2,0:T(8,128)(2,1)}, bf16[4,1024,8,64]...) while((s32[]{:T(128)}, f32[4,1024,8,64]{1,3,2,0:T(8,128)}, ...), condition=%wide.region_20.21_spmd.clone, body=%wide.region_19.20_spmd.sunk.clone | while | flops 5619847168 | bytes 83452088 | solution.py:278
  698.8 10.6 select_convert_fusion.9
  724.2 11.3 %fusion.243 = f32[8,64,1024]{2,1,0:T(8,128)S(1)} fusion(bf16[8,1024,1024]{2,1,0:T(8,128)(2,1)} %select_convert_fusion.9, bf16[4,1024,8,64]{1,3,2,0:T(8,128)(2,1)} %get-tuple-element.1238, s32[]{:T(128)} %get-tuple-element.1219), kind=kOutput, calls=%fused_computation.49.clone.1.clone | convolution fusion | flops 1073741824 | bytes 19923456 | tf_op jit(solution)/shard_map/while/body/eval_jaxpr/hts,she->the/dot_general | solution.py:259
  752.7 10.6 select_convert_fusion.9
  778.2 11.5 %fusion.243 = f32[8,64,1024]{2,1,0:T(8,128)S(1)} fusion(bf16[8,1024,1024]{2,1,0:T(8,128)(2,1)} %select_convert_fusion.9, bf16[4,1024,8,64]{1,3,2,0:T(8,128)(2,1)} %get-tuple-element.1238, s32[]{:T(128)} %get-tuple-element.1219), kind=kOutput, calls=%fused_computation.49.clone.1.clone | convolution fusion | flops 1073741824 | bytes 19923456 | tf_op jit(solution)/shard_map/while/body/eval_jaxpr/hts,she->the/dot_general | solution.py:259
  832.3 11.4 %fusion.243 = f32[8,64,1024]{2,1,0:T(8,128)S(1)} fusion(bf16[8,1024,1024]{2,1,0:T(8,128)(2,1)} %select_convert_fusion.9, bf16[4,1024,8,64]{1,3,2,0:T(8,128)(2,1)} %get-tuple-element.1238, s32[]{:T(128)} %get-tuple-element.1219), kind=kOutput, calls=%fused_computation.49.clone.1.clone | convolution fusion | flops 1073741824 | bytes 19923456 | tf_op jit(solution)/shard_map/while/body/eval_jaxpr/hts,she->the/dot_general | solution.py:259
  886.1 11.3 %fusion.243 = f32[8,64,1024]{2,1,0:T(8,128)S(1)} fusion(bf16[8,1024,1024]{2,1,0:T(8,128)(2,1)} %select_convert_fusion.9, bf16[4,1024,8,64]{1,3,2,0:T(8,128)(2,1)} %get-tuple-element.1238, s32[]{:T(128)} %get-tuple-element.1219), kind=kOutput, calls=%fused_computation.49.clone.1.clone | convolution fusion | flops 1073741824 | bytes 19923456 | tf_op jit(solution)/shard_map/while/body/eval_jaxpr/hts,she->the/dot_general | solution.py:259
  913.5 13.3 %add_bitcast_fusion.2 = (bf16[4,1024,1,8,64]{1,4,3,0,2:T(8,128)(2,1)S(1)}, bf16[4,1024,1,8,64]{1,4,3,0,2:T(8,128)(2,1)S(1)}) fusion(f32[4,1024,8,64]{1,3,2,0:T(8,128)} %get-tuple-element.452, f32[4,1024,3,8,64]{1,4,3,2,0:T(8,128)} %fusion.102, f32[4,1024,8,64]{1,3,2,0:T(8,128)} %get-tuple-element.453), kind=kLoop, calls=%fused_computation.138 | loop fusion | flops 33554432 | bytes 41943040 | tf_op jit(solution)/shard_map/stack | solution.py:295
  930.8 27.6 %copy.81 = bf16[4,1024,3,8,64]{1,0,4,3,2:T(4,128)(2,1)S(1)} copy(bf16[4,1024,3,8,64]{1,4,3,0,2:T(8,128)(2,1)S(1)} %maximum_convert_fusion) | data formatting | bytes 25165824 | tf_op jit(solution)/shard_map/convert_element_type | solution.py:298
  975.7 15.3 %fusion.124 = (bf16[512]{0:T(512)(128)(2,1)S(1)}, f32[4096]{0:T(1024)S(1)}, f32[4096,512]{1,0:T(8,128)S(1)}) fusion(f32[512]{0:T(512)S(1)} %copy-done.30, f32[4096]{0:T(1024)S(1)} %bitcast.397, bf16[4,1,1024,512]{3,2,1,0:T(8,128)(2,1)} %param.21, bf16[4096,1536]{0,1:T(8,128)(2,1)} %bitcast.381, bf16[512,1536]{1,0:T(8,128)(2,1)S(1)} %copy-done.18), kind=kOutput, calls=%fused_computation.200 | convolution fusion | flops 6455029248 | bytes 26774528 | tf_op jit(solution)/shard_map/tc,dc->td/dot_general | solution.py:302
  995.5 34.5 %all-reduce.12 = (bf16[512]{0:T(512)(128)(2,1)S(1)}, bf16[512]{0:T(512)(128)(2,1)S(1)}, bf16[512]{0:T(512)(128)(2,1)S(1)}, bf16[512]{0:T(512)(128)(2,1)S(1)}, bf...) all-reduce(bf16[512]{0:T(512)(128)(2,1)S(1)} %copy-done.38, ...), channel_id=1, replica_groups=mesh['dp'=4,'wide'=8] {'wide'}, use_global_device_ids=true, to_apply=%add.5 | all-reduce | flops 5120 | bytes 20480
  1030.0 18.2 %add_convert_fusion = bf16[4096,512]{1,0:T(8,128)(2,1)} fusion(f32[4096,512]{1,0:T(8,128)} %copy-done.4, bf16[4096,2048]{1,0:T(8,128)(2,1)} %get-tuple-element.771, bf16[2048,512]{1,0:T(8,128)(2,1)} %all-gather.16.cloned.1.call-done, f32[512]{0:T(512)S(1)} %convert_element_type.381), kind=kOutput, calls=%fused_computation.148 | convolution fusion | flops 8596226048 | bytes 31459328 | tf_op jit(solution)/shard_map/dot_general | solution.py:191
  1048.3 12.6 %add_add_fusion.2 = f32[4096,512]{1,0:T(8,128)} fusion(f32[4096,512]{1,0:T(8,128)} %copy-done.6, f32[4096]{0:T(1024)S(1)} %negate_multiply_fusion, f32[4096]{0:T(1024)S(1)} %copy-done.24, bf16[4,1,1024,512]{3,2,1,0:T(8,128)(2,1)} %param.22, f32[4096]{0:T(1024)S(1)} %get-tuple-element.759, f32[4096]{0:T(1024)S(1)} %bitcast.399, ...), kind=kLoop, calls=%fused_computation.131 | loop fusion | flops 25165824 | bytes 33638400 | tf_op jit(solution)/shard_map/add | solution.py:307
  (345 shorter events, 459.0 us)
Async XLA Ops:
  7.2 49.8 %all-gather.12.cloned.1.call-start = ((), (), s32[]{:S(2)}) async-start(), calls=%async_computation.4 | async-start | bytes 1769472 | tf_op jit(solution)/shard_map/all_gather | solution.py:123
  7.9 172.3 %all-gather.18.cloned.1.call-start = ((), (), s32[]{:S(2)}) async-start(), calls=%async_computation.11 | async-start | bytes 4718592 | tf_op jit(solution)/shard_map/all_gather | solution.py:15
  39.5 8.5 copy-start
  39.5 8.5 copy-start.29
  76.7 8.5 copy-start.8
  85.1 38.6 %copy-start.39 = (bf16[256]{0:T(256)(128)(2,1)S(1)}, bf16[256]{0:T(256)(128)(2,1)}, u32[]{:S(2)}) copy-start(bf16[256]{0:T(256)(128)(2,1)} %param.30) | copy-start | bytes 1540
  89.2 377.6 %all-gather.14.cloned.1.call-start = ((), (), s32[]{:S(2)}) async-start(), calls=%async_computation.5 | async-start | bytes 2359296 | tf_op jit(solution)/shard_map/all_gather | solution.py:127
  90.0 402.7 %all-gather.16.cloned.1.call-start = ((), (), s32[]{:S(2)}) async-start(), calls=%async_computation.6 | async-start | bytes 2359296 | tf_op jit(solution)/shard_map/all_gather | solution.py:129
  90.6 588.5 %all-gather.20.cloned.1.call-start = ((), (), s32[]{:S(2)}) async-start(), calls=%async_computation.12 | async-start | bytes 4718592 | tf_op jit(solution)/shard_map/all_gather | solution.py:38
  451.0 8.1 copy-start.16
  451.0 8.1 copy-start.19
  451.0 8.1 copy-start.21
  451.0 8.1 copy-start.22
  451.0 8.1 copy-start.1
  492.7 35.0 %copy-start.5 = (f32[4096,512]{1,0:T(8,128)S(1)}, f32[4096,512]{1,0:T(8,128)}, u32[]{:S(2)}) copy-start(f32[4096,512]{1,0:T(8,128)} %copy-done.4) | copy-start | bytes 25165828
  563.0 10.9 copy-start.20
  573.9 10.6 copy-start.3
  573.9 10.6 copy-start.31
  588.1 460.1 %reduce-scatter.7.cloned.1.call-start = ((), (), s32[]{:S(2)}) async-start(), calls=%async_computation.8 | async-start | bytes 589824 | tf_op jit(solution)/shard_map/reduce_scatter | solution.py:318
  594.8 19.5 %copy-start.27 = (f32[1,8,4,128]{3,2,1,0:T(4,128)S(1)}, f32[1,8,4,128]{3,2,1,0:T(4,128)}, u32[]{:S(2)}) copy-start(f32[1,8,4,128]{3,2,1,0:T(4,128)} %get-tuple-element.763) | copy-start | bytes 49156
  594.8 24.8 %copy-start.40 = (bf16[64]{0:T(256)(128)(2,1)S(1)}, bf16[64]{0:T(256)(128)(2,1)}, u32[]{:S(2)}) copy-start(bf16[64]{0:T(256)(128)(2,1)} %param.32) | copy-start | bytes 388
  594.8 453.4 %reduce-scatter.9.cloned.1.call-start = ((), (), s32[]{:S(2)}) async-start(), calls=%async_computation.9 | async-start | bytes 2359296 | tf_op jit(solution)/shard_map/reduce_scatter | solution.py:327
  613.8 434.5 %reduce-scatter.11.cloned.1.call-start = ((), (), s32[]{:S(2)}) async-start(), calls=%async_computation.10 | async-start | bytes 2359296 | tf_op jit(solution)/shard_map/reduce_scatter | solution.py:333
  619.8 8.2 copy-start.37
  622.3 43.1 %copy-start.10 = (bf16[4,1,1024,512]{3,2,1,0:T(8,128)(2,1)S(1)}, bf16[4,1,1024,512]{3,2,1,0:T(8,128)(2,1)}, u32[]{:S(2)}) copy-start(bf16[4,1,1024,512]{3,2,1,0:T(8,128)(2,1)} %param.22) | copy-start | bytes 12582916
  679.0 369.3 %reduce-scatter.5.cloned.1.call-start = ((), (), s32[]{:S(2)}) async-start(), calls=%async_computation.7 | async-start | bytes 1769472 | tf_op jit(solution)/shard_map/reduce_scatter | solution.py:315
  958.5 9.2 copy-start.17
  967.7 8.0 copy-start.30
  975.6 104.9 %all-reduce.18.cloned.1.call-start = ((), (), s32[]{:S(2)}) async-start(), calls=%async_computation.13 | async-start | bytes 1572864 | tf_op jit(solution)/shard_map/psum | solution.py:343
  975.7 15.4 %copy-start.28 = (f32[1,8,4,128]{3,2,1,0:T(4,128)S(1)}, f32[1,8,4,128]{3,2,1,0:T(4,128)}, u32[]{:S(2)}) copy-start(f32[1,8,4,128]{3,2,1,0:T(4,128)} %get-tuple-element.761) | copy-start | bytes 49156
  975.7 15.5 %copy-start.2 = (bf16[4,1,1024,512]{3,2,1,0:T(8,128)(2,1)S(1)}, bf16[4,1,1024,512]{3,2,1,0:T(8,128)(2,1)}, u32[]{:S(2)}) copy-start(bf16[4,1,1024,512]{3,2,1,0:T(8,128)(2,1)} %param.21) | copy-start | bytes 12582916
  1030.0 18.3 %copy-start.24 = (f32[4096]{0:T(1024)S(1)}, f32[4096]{0:T(1024)}, u32[]{:S(2)}) copy-start(f32[4096]{0:T(1024)} %copy-done.23) | copy-start | bytes 49156
  (19 other events, 77.4 us)
Sparse Core Ops, SparseCore 0:
  10.2 46.7 all-gather.11
  89.4 75.9 all-gather.17
  167.5 47.5 all-gather.13
  217.1 47.7 all-gather.15
  588.3 71.6 all-gather.19
  663.1 60.1 reduce-scatter.6
  727.2 66.6 reduce-scatter.8
  797.9 66.6 reduce-scatter.10
  975.7 62.5 reduce-scatter.4
  1048.4 32.0 all-reduce.17
where the time goes:
time: 1110 us; the launch traced here: 1090 us
  matrix products  471 us (42%)
  local copies, waits for them, and re-layouts  255 us (23%)
  blocking collectives  177 us (16%)
  other arithmetic  153 us (14%)
  waiting for transfers between devices  18.4 us (2%)
  between operations  17.8 us (2%)
    dynamic_update_slice x16, local copies, waits for them, and re-layouts, per_device(): lax.map(attend, (query_feat, key_feat, values, starts, state_low, norm_in))  165 us
    unnamed x2, blocking collectives  57.9 us
    dot_general x4, matrix products, attend_back(): jnp.einsum('hts,she->the', score_grad, key_part, preferred_element_type=j...  45.5 us
    dot_general x4, matrix products, attend_back(): jnp.einsum('thf,shf->hts', num_grad, value_part, preferred_element_type=j...  42.2 us
    dot_general x4, matrix products, block_scores(): jnp.einsum('the,she->hts', query_part, key_part, preferred_element_type=j...  40.2 us
    dot_general x4, matrix products, attend_back(): jnp.einsum('hts,thf->shf', scores, num_grad, preferred_element_type=jnp.f...  39.1 us
    dot_general x4, matrix products, attend_back(): jnp.einsum('hts,the->she', score_grad, query_part, preferred_element_type...  36.9 us
    dot_general x4, matrix products, attend(): jnp.einsum('hts,shf->thf', scores, value_part, preferred_element_type=jnp...  36.6 us
  transfers between devices with their start and end apart: 10, of which 2 were waited for; matrix products, arithmetic and copies ran while one was open for 67% of the time, Pallas kernels for 0%

commit v1 on v0

v1 whole, which is shorter than its diff:
```python
import functools

import jax
import jax.numpy as jnp
from jax import lax
from jax.experimental import pallas as pl
from jax.experimental.pallas import tpu as pltpu
from jax.sharding import PartitionSpec as P

HEADS = 8
EPSILON = 1e-05
F32 = jnp.float32
BF16 = jnp.bfloat16
CHUNK = 128
TILE = 512
FF_TILE = 512
VMEM = 60 * 1024 * 1024


def nn(a, b):
    return lax.dot_general(a, b, (((1,), (0,)), ((), ())), preferred_element_type=F32)


def nt(a, b):
    return lax.dot_general(a, b, (((1,), (1,)), ((), ())), preferred_element_type=F32)


def rows_of(row, width):
    return jnp.concatenate([row] * (width // 128), axis=1)


def start_of(lens, m, place):
    start, end = jnp.zeros_like(place), 0
    for j in range(lens.shape[1]):
        end = end + lens[m, j]
        start = start + jnp.where(end <= place, lens[m, j], 0)
    return start


def place_rows(first, count):
    return first + lax.broadcasted_iota(jnp.int32, (count, 128), 0)


def flag(condition):
    return jnp.where(condition, 1.0, 0.0)


def normed(x):
    average = jnp.mean(x, axis=-1, keepdims=True)
    centred = x - average
    spread = jnp.mean(centred * centred, axis=-1, keepdims=True)
    scale = lax.rsqrt(spread + EPSILON)
    return centred * scale, scale


def norm_back(e, xhat, scale, gain):
    a = gain * e
    return scale * (
        a - jnp.mean(a, axis=-1, keepdims=True) - xhat * jnp.mean(a * xhat, axis=-1, keepdims=True)
    )


def feature(v):
    return jnp.where(v > 0.0, v + 1.0, jnp.exp(jnp.minimum(v, 0.0)))


def column_sum(a):
    return jnp.sum(a, axis=0, keepdims=True)


def by_group(fn, *arrays):
    return jnp.concatenate(
        [fn(g, *[a[:, 256 * g : 256 * g + 256] for a in arrays]) for g in range(2)], axis=1
    )


def lane_half(shape):
    return lax.broadcasted_iota(jnp.int32, shape, 1) < 64


def pack_state(state, norm, out):
    folded = []
    for s in state:
        y = s[:, :128] + s[:, 128:]
        folded.append(y + pltpu.roll(y, 64, 1))
    out[0:256, :] = jnp.where(lane_half((256, 128)), folded[0], folded[1]).astype(out.dtype)
    row = lax.broadcasted_iota(jnp.int32, (16, 128), 0)
    tail = jnp.zeros((16, 128), F32)
    for j in range(4):
        tail = jnp.where(row == j, norm[:, 128 * j : 128 * j + 128], tail)
    out[256:272, :] = tail.astype(out.dtype)
    if out.shape[0] > 272:
        out[272:, :] = jnp.zeros((out.shape[0] - 272, 128), out.dtype)


def unpack_state(packed, ones):
    z = packed[0:256, :]
    turned = pltpu.roll(z, 64, 1)
    half = lane_half((256, 128))
    groups = []
    for part in (jnp.where(half, z, turned), jnp.where(half, turned, z)):
        groups.append(jnp.concatenate([part, part], axis=1).astype(BF16) * ones)
    tail = packed[256:272, :]
    norm = jnp.concatenate([tail[j : j + 1, :] for j in range(4)], axis=1)
    return groups, norm


MESH = pl.DeviceIdType.MESH


def place():
    dp = lax.axis_index("dp")
    return lax.rem(dp, 2), dp // 2, lax.axis_index("wide"), lax.axis_size("dp") // 2, lax.axis_size("wide")


def others(count, fn):
    def body(o, carry):
        fn(o)
        return carry

    lax.fori_loop(1, count, body, 0)


def remote(src, dst, send, recv, dp, wide):
    return pltpu.make_async_remote_copy(
        src_ref=src, dst_ref=dst, send_sem=send, recv_sem=recv, device_id=(dp, wide), device_id_type=MESH
    )


def greet():
    core, y, me, ny, n = place()
    dp = 2 * y + core
    barrier = pltpu.get_barrier_semaphore()

    def signal(d, w):
        pl.semaphore_signal(barrier, inc=1, device_id=(d, w), device_id_type=MESH)

    others(n, lambda o: signal(dp, lax.rem(me + o, n)))
    others(ny, lambda o: signal(2 * lax.rem(y + o, ny) + core, me))
    signal(2 * y + 1 - core, me)
    pl.semaphore_wait(barrier, n - 1 + ny - 1 + 1)


class Gather:
    def __init__(self, src, dst, sems):
        self.src, self.dst = src, dst
        self.near, self.send, self.recv, self.y_send, self.y_recv, self.c_send, self.c_recv = sems
        self.core, self.y, self.me, self.ny, self.n = place()
        self.dp = 2 * self.y + self.core
        each = src.shape[0]
        self.split = split_of(each)
        part = each // self.split
        if self.split == 1:
            self.rows, self.half = pl.ds(0, each), None
        else:
            at = self.core * (each // 2) + self.y * part
            self.rows = pl.ds(pl.multiple_of(at, part), part)
            self.half = pl.ds(pl.multiple_of(self.core * (each // 2), each // 2), each // 2)

    def own(self):
        return pltpu.make_async_copy(self.src.at[self.rows], self.dst.at[self.me, self.rows], self.near)

    def out(self, o):
        to = lax.rem(self.me + o, self.n)
        return remote(self.src.at[self.rows], self.dst.at[self.me, self.rows], self.send.at[o], self.recv.at[self.me], self.dp, to)

    def back(self, o):
        frm = lax.rem(self.me + o, self.n)
        part = self.dst.at[frm, self.rows]
        return remote(part, part, self.send.at[o], self.recv.at[frm], self.dp, frm)

    def start_wide(self):
        self.own().start()
        others(self.n, lambda o: self.out(o).start())

    def finish_wide(self):
        self.own().wait()
        others(self.n, lambda o: self.out(o).wait_send())
        others(self.n, lambda o: self.back(o).wait_recv())

    def along_y(self, o):
        part = self.dst.at[:, self.rows]
        to = lax.rem(self.y + o, self.ny)
        return remote(part, part, self.y_send.at[o], self.y_recv.at[self.y], 2 * to + self.core, self.me)

    def along_y_back(self, o):
        frm = lax.rem(self.y + o, self.ny)
        each = self.src.shape[0]
        part = each // self.split
        at = self.core * (each // 2) + frm * part
        ref = self.dst.at[:, pl.ds(pl.multiple_of(at, part), part)]
        return remote(ref, ref, self.y_send.at[o], self.y_recv.at[frm], 2 * frm + self.core, self.me)

    def start_y(self):
        if self.split > 1:
            others(self.ny, lambda o: self.along_y(o).start())

    def finish_y(self):
        if self.split > 1:
            others(self.ny, lambda o: self.along_y(o).wait_send())
            others(self.ny, lambda o: self.along_y_back(o).wait_recv())

    def cross(self):
        part = self.dst.at[:, self.half]
        return remote(part, part, self.c_send, self.c_recv, 2 * self.y + 1 - self.core, self.me)

    def cross_back(self):
        each = self.src.shape[0]
        at = (1 - self.core) * (each // 2)
        part = self.dst.at[:, pl.ds(pl.multiple_of(at, each // 2), each // 2)]
        return remote(part, part, self.c_send, self.c_recv, 2 * self.y + 1 - self.core, self.me)

    def start_core(self):
        if self.split > 1:
            self.cross().start()

    def finish_core(self):
        if self.split > 1:
            self.cross().wait_send()
            self.cross_back().wait_recv()


def split_of(each):
    count = lax.axis_size("dp")
    return count if each % (16 * count) == 0 else 1


def gather_sems():
    n, ny = lax.axis_size("wide"), lax.axis_size("dp") // 2
    dma = pltpu.SemaphoreType.DMA
    return [dma, dma((n,)), dma((n,)), dma((ny,)), dma((ny,)), dma, dma]


HIGH = 4


def low_count():
    return lax.axis_size("wide") // HIGH


def state_rows():
    unit = 16 * low_count()
    return -(-272 // unit) * unit


class Running:
    def __init__(self, own, upward, refs):
        self.own, self.upward = own, upward
        (self.slots, self.group, self.high, self.mine, self.spread, self.result, self.near, self.send1, self.recv1,
         self.send2, self.recv2, self.send3, self.recv3) = refs
        _, _, self.me, _, _ = place()
        self.dp = lax.axis_index("dp")
        self.lo = low_count()
        self.h, self.l = self.me // self.lo, lax.rem(self.me, self.lo)
        self.part = state_rows() // self.lo

    def slice(self, l):
        return pl.ds(pl.multiple_of(l * self.part, self.part), self.part)

    def copy1(self, o, back=False):
        other = lax.rem(self.l + o, self.lo)
        slot = other if back else self.l
        return remote(self.own, self.slots.at[slot], self.send1.at[o], self.recv1.at[slot], self.dp, self.h * self.lo + other)

    def near1(self):
        return pltpu.make_async_copy(self.own, self.slots.at[self.l], self.near.at[0])

    def start1(self):
        self.near1().start()
        others(self.lo, lambda o: self.copy1(o).start())

    def before(self, a, b):
        return a < b if self.upward else a > b

    def finish1_start2(self):
        self.near1().wait()
        others(self.lo, lambda o: self.copy1(o).wait_send())
        others(self.lo, lambda o: self.copy1(o, True).wait_recv())
        every = jnp.zeros(self.own.shape, F32)
        inner = every
        for l in range(self.lo):
            part = self.slots[l].astype(F32)
            every = every + part
            inner = inner + jnp.where(self.before(l, self.l), part, 0.0)
        self.group[...] = every.astype(BF16)
        self.result[...] = inner

        def send(o):
            other = lax.rem(self.h + o, HIGH)

            @pl.when(self.before(self.h, other))
            def _():
                self.copy2(o).start()

        others(HIGH, send)

    def copy2(self, o, back=False):
        other = lax.rem(self.h + o, HIGH)
        slot = other if back else self.h
        return remote(
            self.group.at[:, self.slice(self.l)], self.high.at[slot], self.send2.at[o], self.recv2.at[slot],
            self.dp, other * self.lo + self.l,
        )

    def finish2_start3(self):
        def wait(o):
            other = lax.rem(self.h + o, HIGH)

            @pl.when(self.before(self.h, other))
            def _():
                self.copy2(o).wait_send()

            @pl.when(self.before(other, self.h))
            def _():
                self.copy2(o, True).wait_recv()

        others(HIGH, wait)
        total = jnp.zeros(self.mine.shape, F32)
        for h in range(HIGH):
            total = total + jnp.where(self.before(h, self.h), self.high[h].astype(F32), 0.0)
        self.mine[...] = total.astype(BF16)
        self.near3().start()
        others(self.lo, lambda o: self.copy3(o).start())

    def near3(self):
        return pltpu.make_async_copy(self.mine, self.spread.at[self.l], self.near.at[1])

    def copy3(self, o, back=False):
        other = lax.rem(self.l + o, self.lo)
        slot = other if back else self.l
        return remote(self.mine, self.spread.at[slot], self.send3.at[o], self.recv3.at[slot], self.dp, self.h * self.lo + other)

    def finish3(self):
        self.near3().wait()
        others(self.lo, lambda o: self.copy3(o).wait_send())
        others(self.lo, lambda o: self.copy3(o, True).wait_recv())
        for l in range(self.lo):
            rows = slice(l * self.part, (l + 1) * self.part)
            self.result[:, rows] = self.result[:, rows] + self.spread[l].astype(F32)


def running_scratch(micro):
    lo, rows = low_count(), state_rows()
    dma = pltpu.SemaphoreType.DMA
    return [
        pltpu.VMEM((lo, micro, rows, 128), BF16),
        pltpu.VMEM((micro, rows, 128), BF16),
        pltpu.VMEM((HIGH, micro, rows // lo, 128), BF16),
        pltpu.VMEM((micro, rows // lo, 128), BF16),
        pltpu.VMEM((lo, micro, rows // lo, 128), BF16),
        pltpu.VMEM((micro, rows, 128), F32),
        dma((2,)), dma((lo,)), dma((lo,)), dma((HIGH,)), dma((HIGH,)), dma((lo,)), dma((lo,)),
    ]


def vector_tile(vectors, each):
    row = lax.broadcasted_iota(jnp.int32, (16, 128), 0)

    def padded(piece):
        return jnp.concatenate([piece.astype(F32), jnp.zeros((1, 128 - each), F32)], axis=1)

    pieces = [padded(v[...]) for v in vectors[:5]]
    hidden = vectors[5][...]
    pieces += [padded(hidden[:, each * r : each * r + each]) for r in range(hidden.shape[1] // each)]
    tile = jnp.zeros((16, 128), F32)
    for j, piece in enumerate(pieces):
        tile = jnp.where(row == j, piece, tile)
    return tile.astype(BF16)


def spread_vectors(slots, out, each):
    n = slots.shape[0]
    d = each * n
    per = 4 * each
    row = lax.broadcasted_iota(jnp.int32, (16, 128), 0)
    blocks = [jnp.zeros((16, 128), F32) for _ in range(d // 128)]
    for w in range(n):
        tile = slots[w].astype(F32)
        at = each * w
        moved = pltpu.roll(tile, at % 128, 1) if at % 128 else tile
        blocks[at // 128] = blocks[at // 128] + jnp.where(row < 5, moved, 0.0)
        for r in range(4):
            at = per * w + each * r
            to_row, lane = 5 + at // d, at % d
            only = jnp.where(row == 5 + r, tile, 0.0)
            moved = pltpu.roll(only, lane % 128, 1) if lane % 128 else only
            if to_row != 5 + r:
                moved = pltpu.roll(moved, (to_row - 5 - r) % 16, 0)
            blocks[lane // 128] = blocks[lane // 128] + moved
    for j, block in enumerate(blocks):
        out[:, 128 * j : 128 * j + 128] = block


def first_kernel(
    lens, off, x, *refs
):
    (s_qkv, s_out, s_up, s_down, v0, v1, v2, v3, v4, v5, ones,
     q_out, k_out, v_out, num_out, kc_out, states_out, state_in, w_qkv, w_out, w_up, w_down, vec_out,
     w_ref, q_all, k_all, v_all, acc, zacc, state, norm, local, tile, tiles_ref, tile_near, tile_send, tile_recv,
     save_sem, *rest) = refs
    each = s_qkv.shape[0]
    running_refs, rest = rest[:13], rest[13:]
    jobs = []
    d = x.shape[1]
    for j in range(3):
        jobs.append(Gather(s_qkv.at[:, d * j : d * j + d], w_ref.at[j], rest[7 * j : 7 * j + 7]))
    for j, (src, dst) in enumerate(((s_out, w_out), (s_up, w_up), (s_down, w_down))):
        jobs.append(Gather(src, dst, rest[21 + 7 * j : 28 + 7 * j]))
    running = Running(local, True, running_refs)
    rows = x.shape[0]
    micro = local.shape[0]
    block_rows = num_out.shape[0]
    tiles = block_rows // rows
    steps = micro * tiles
    i = pl.program_id(0)
    core, y, me, ny, n = place()
    dp = 2 * y + core

    def vec_copy(o, back=False):
        other = lax.rem(me + o, n)
        slot = other if back else me
        return remote(tile, tiles_ref.at[slot], tile_send.at[o], tile_recv.at[slot], dp, other)

    def vec_near():
        return pltpu.make_async_copy(tile, tiles_ref.at[me], tile_near)

    def save(j):
        return pltpu.make_async_copy(w_ref.at[j], w_qkv.at[:, :, d * j : d * j + d], save_sem.at[j])

    @pl.when(i == 0)
    def _():
        tile[...] = vector_tile((v0, v1, v2, v3, v4, v5), each)
        greet()
        vec_near().start()
        others(n, lambda o: vec_copy(o).start())
        for job in jobs[:3]:
            job.start_wide()

    @pl.when(i < steps)
    def _():
        xhat, _ = normed(x[...].astype(F32))

        @pl.when(i == 0)
        def _():
            vec_near().wait()
            others(n, lambda o: vec_copy(o).wait_send())
            others(n, lambda o: vec_copy(o, True).wait_recv())
            spread_vectors(tiles_ref, vec_out, each)
            for job in jobs[:3]:
                job.finish_wide()
                job.start_y()
            for job in jobs[3:]:
                job.start_wide()
            for job in jobs[:3]:
                job.finish_y()
                job.start_core()
            jobs[0].finish_core()

        h1 = (xhat * vec_out[0:1, :] + vec_out[1:2, :]).astype(BF16)
        at = pl.ds(pl.multiple_of(i * rows, rows), rows)

        def weights(j):
            return w_ref[j].reshape(d, d)

        q = feature(nn(h1, weights(0))).astype(BF16)
        q_out[...] = q
        q_all[at, :] = q

        @pl.when(i == 0)
        def _():
            jobs[1].finish_core()

        k = feature(nn(h1, weights(1))).astype(BF16)
        k_out[...] = k
        k_all[at, :] = k

        @pl.when(i == 0)
        def _():
            jobs[2].finish_core()
            for j in range(3):
                save(j).start()

        v = nn(h1, weights(2)).astype(BF16)
        v_out[...] = v
        v_all[at, :] = v
        m, t = i // tiles, lax.rem(i, tiles)
        base = off[0]
        final = start_of(lens, m, base + block_rows - 1)
        last = flag(start_of(lens, m, place_rows(base + t * rows, rows)) == final)
        k_last = k * rows_of(last.astype(BF16), d)
        k_turned = k_last.T

        @pl.when(t == 0)
        def _():
            acc[...] = jnp.zeros_like(acc)
            zacc[...] = jnp.zeros_like(zacc)

        for g in range(2):
            acc[g] += nn(k_turned[256 * g : 256 * g + 256, :], v[:, 256 * g : 256 * g + 256])
        zacc[...] += column_sum(k_last.astype(F32))

        @pl.when(t == tiles - 1)
        def _():
            mask = ones[...].astype(F32)
            pack_state([acc[0] * mask, acc[1] * mask], zacc[...], local.at[m])

    @pl.when(i == steps - 1)
    def _():
        running.start1()

    @pl.when(i == steps)
    def _():
        for job in jobs[3:5]:
            job.finish_wide()
            job.start_y()

    @pl.when(i == steps + 1)
    def _():
        running.finish1_start2()
        jobs[5].finish_wide()
        jobs[5].start_y()

    @pl.when(i == steps + 2)
    def _():
        running.finish2_start3()
        for job in jobs[3:5]:
            job.finish_y()
            job.start_core()

    @pl.when(i >= steps)
    def _():
        m = i - steps
        at = pl.ds(pl.multiple_of(m * block_rows, block_rows), block_rows)
        attend(lens, m, off[0], q_all.at[at], k_all.at[at], v_all.at[at], ones, num_out, kc_out, states_out, state, norm)

    @pl.when(i == steps + micro - 1)
    def _():
        jobs[5].finish_y()
        jobs[5].start_core()
        running.finish3()
        state_in[...] = running.result[...]
        for job in jobs[3:]:
            job.finish_core()
        for j in range(3):
            save(j).wait()


def chunk_masks(lens, m, begin, size):
    by_row = start_of(lens, m, place_rows(begin, size))
    lane = begin + lax.broadcasted_iota(jnp.int32, (8, size), 1)
    by_column = start_of(lens, m, lane)[0:1, :]
    final = start_of(lens, m, begin + size - 1)
    return by_row, by_column, final


def pair_mask():
    return flag(lane_half((16, 128))).astype(BF16)[0:1, :]


def split_pair(a, low, high):
    return jnp.concatenate([a * low, a * high], axis=0)


def attend(lens, m, base, q_ref, k_ref, v_ref, ones, num_out, kc_out, states_out, state, norm):
    rows, d = q_ref.shape
    size = CHUNK
    state[...] = jnp.zeros_like(state)
    norm[...] = jnp.zeros_like(norm)
    half = lane_half((1, 128))
    low = flag(half).astype(BF16)
    high = flag(jnp.logical_not(half)).astype(BF16)

    def step(c, carry):
        at = pl.ds(pl.multiple_of(c * size, size), size)
        begin = base + c * size
        q, k, v = q_ref[at, :], k_ref[at, :], v_ref[at, :]
        by_row, by_column, final = chunk_masks(lens, m, begin, size)
        places = lax.broadcasted_iota(jnp.int32, (size, size), 0)
        columns = lax.broadcasted_iota(jnp.int32, (size, size), 1)
        allowed = flag((places >= columns) & (by_row[:, :size] == by_column)).astype(BF16)
        allowed2 = jnp.concatenate([allowed, allowed], axis=1)
        seen = flag(by_row < begin)
        last = flag(by_row == final).astype(BF16)
        keep = jnp.where(final < begin, 1.0, 0.0)
        kc_out[at, :] = (nn(allowed, k) + rows_of(seen, d) * norm[...]).astype(BF16)
        groups = [state[g].astype(BF16) for g in range(2)]
        for g in range(2):
            states_out[c, g] = groups[g]
        q_seen = q * rows_of(seen.astype(BF16), d)
        for p in range(4):
            cut = slice(128 * p, 128 * p + 128)
            s = nt(q[:, cut], split_pair(k[:, cut], low, high)).astype(BF16) * allowed2
            inside = nn(s, split_pair(v[:, cut], low, high))
            g, side = p // 2, 128 * (p % 2)
            before = nn(q_seen[:, 256 * g : 256 * g + 256], groups[g][:, side : side + 128])
            num_out[at, cut] = (inside + before).astype(BF16)
        k_last = k * rows_of(last, d)
        k_turned = k_last.T
        mask = ones[...].astype(F32)
        for g in range(2):
            cut = slice(256 * g, 256 * g + 256)
            state[g] = keep * state[g] + nn(k_turned[cut, :], v[:, cut]) * mask
        norm[...] = keep * norm[...] + column_sum(k_last.astype(F32))
        return carry

    lax.fori_loop(0, rows // size, step, 0)


def middle_kernel(
    lens, off, q_ref, num_ref, kc_ref, x_ref, cot_ref, state_in, ones,
    w_out, vec, w_up, w_down,
    block_out, gm_out, gnum_out, gden_out, use_out, g_out, g_up, g_down, g_bias, g_up_bias,
    groups, norm, use, use_norm, acc_out, acc_up, acc_down, total, e_total, h2_ref, h2t_ref, ct_ref,
):
    m, t, tiles = pl.program_id(0), pl.program_id(1), pl.num_programs(1)
    rows, d = x_ref.shape
    first = (m == 0) & (t == 0)
    final = (m == pl.num_programs(0) - 1) & (t == tiles - 1)
    base = off[0]

    @pl.when(first)
    def _():
        acc_out[...] = jnp.zeros_like(acc_out)
        acc_up[...] = jnp.zeros_like(acc_up)
        acc_down[...] = jnp.zeros_like(acc_down)
        g_bias[...] = jnp.zeros_like(g_bias)
        g_up_bias[...] = jnp.zeros_like(g_up_bias)

    @pl.when(t == 0)
    def _():
        parts, z = unpack_state(state_in[...], ones[...])
        for g in range(2):
            groups[g] = parts[g]
        norm[...] = z
        use[...] = jnp.zeros_like(use)
        use_norm[...] = jnp.zeros_like(use_norm)

    gain, bias, down_bias = vec[2:3, :], vec[3:4, :], vec[4:5, :]
    q = q_ref[...]
    seen = flag(start_of(lens, m, place_rows(base + t * rows, rows)) < base)
    q_seen = q * rows_of(seen.astype(BF16), d)
    num = num_ref[...].astype(F32) + by_group(lambda g, a: nn(a, groups[g]), q_seen)
    kc = kc_ref[...].astype(F32) + rows_of(seen, d) * norm[...]
    den = by_group(lambda g, a: nn(a, ones[...]), (q.astype(F32) * kc).astype(BF16))
    over = 1.0 / den
    mixed = (num * over).astype(BF16)
    middle = x_ref[...].astype(F32) + nn(mixed, w_out[...])
    xhat, scale = normed(middle)
    h2 = (xhat * gain + bias).astype(BF16)
    h2_ref[...] = h2
    h2t_ref[...] = h2.T
    ct_ref[...] = cot_ref[...].T
    total[...] = middle + down_bias
    e_total[...] = jnp.zeros_like(e_total)

    def ffn(f, carry):
        cut = pl.ds(pl.multiple_of(f * FF_TILE, FF_TILE), FF_TILE)
        hidden = nn(h2_ref[...], w_up[:, cut]) + vec[pl.ds(5 + f, 1), :]
        pulled = nt(cot_ref[...], w_down[cut, :])
        square = hidden * hidden
        c0, c1 = 0.7978845608028654, 0.044715
        th = jnp.tanh(hidden * (c0 + (c0 * c1) * square))
        half_up = 0.5 + 0.5 * th
        active = (hidden * half_up).astype(BF16)
        slope = half_up + (0.5 * hidden) * (1.0 - th * th) * (c0 + (3.0 * c0 * c1) * square)
        g_hidden = slope * pulled
        g_low = g_hidden.astype(BF16)
        total[...] += nn(active, w_down[cut, :])
        e_total[...] += nt(g_low, w_up[:, cut])
        acc_down[:, cut] += nn(ct_ref[...], active)
        acc_up[:, cut] += nn(h2t_ref[...], g_low)
        g_up_bias[:, cut] += column_sum(g_hidden)
        return carry

    lax.fori_loop(0, w_up.shape[1] // FF_TILE, ffn, 0)
    block_out[...] = total[...].astype(BF16)
    e = e_total[...]
    cot = cot_ref[...].astype(F32)
    g_middle = cot + norm_back(e, xhat, scale, gain)
    gm_out[...] = g_middle
    g_bias[0:1, :] += column_sum(e * xhat)
    g_bias[1:2, :] += column_sum(e)
    g_bias[2:3, :] += column_sum(cot)
    branch = g_middle.astype(BF16)
    acc_out[...] += nn(mixed.T, branch)
    g_mixed = nt(branch, w_out[...])
    gnum = (g_mixed * over).astype(BF16)
    gnum_out[...] = gnum
    gden = -by_group(lambda g, a: nn(a, ones[...]), (g_mixed * num).astype(BF16)) * (over * over)
    gden_out[...] = gden.astype(BF16)
    turned = q_seen.T
    for g in range(2):
        cut = slice(256 * g, 256 * g + 256)
        use[g] += nn(turned[cut, :], gnum[:, cut])
    use_norm[...] += column_sum(q_seen.astype(F32) * gden)

    @pl.when(t == tiles - 1)
    def _():
        mask = ones[...].astype(F32)
        pack_state([use[0] * mask, use[1] * mask], use_norm[...], use_out)

    @pl.when(final)
    def _():
        g_out[...] = acc_out[...].astype(BF16)
        g_up[...] = acc_up[...].astype(BF16)
        g_down[...] = acc_down[...].astype(BF16)


def attend_back_kernel(
    lens, off, q_ref, k_ref, v_ref, gnum_ref, gden_ref, kc_ref, states, state_in, ones,
    gq_out, dk_out, dv_out, after, after_norm,
):
    m = pl.program_id(0)
    rows, d = q_ref.shape
    size = CHUNK
    count = rows // size
    base = off[0]
    after[...] = jnp.zeros_like(after)
    after_norm[...] = jnp.zeros_like(after_norm)
    half = lane_half((1, 128))
    low = flag(half).astype(BF16)
    high = flag(jnp.logical_not(half)).astype(BF16)
    groups_in, norm_in = unpack_state(state_in[...], ones[...])

    def step(i, carry):
        c = count - 1 - i
        at = pl.ds(pl.multiple_of(c * size, size), size)
        begin = base + c * size
        q, k, v, gnum = q_ref[at, :], k_ref[at, :], v_ref[at, :], gnum_ref[at, :]
        gden = gden_ref[at, :].astype(F32)
        by_row, by_column, final = chunk_masks(lens, m, begin, size)
        places = lax.broadcasted_iota(jnp.int32, (size, size), 0)
        columns = lax.broadcasted_iota(jnp.int32, (size, size), 1)
        same = by_row[:, :size] == by_column
        allowed = flag((places >= columns) & same).astype(BF16)
        allowed2 = jnp.concatenate([allowed, allowed], axis=1)
        turned = flag((places <= columns) & same).astype(BF16)
        turned2 = jnp.concatenate([turned, turned], axis=1)
        seen = rows_of(flag(by_row < begin).astype(BF16), d)
        seen_all = flag(by_row < base)
        last = flag(by_row == final)
        keep = jnp.where(final < begin, 1.0, 0.0)
        last_low = rows_of(last.astype(BF16), d)
        g_after = [after[g].astype(BF16) for g in range(2)]
        gnum_seen = gnum * seen
        gnum_all = gnum * rows_of(seen_all.astype(BF16), d)
        k_last, v_last = k * last_low, v * last_low
        gden_q = gden * q.astype(F32)
        dk_den = nn(turned, gden_q.astype(BF16)) + rows_of(last, d) * after_norm[...]
        dq_den = gden * (kc_ref[at, :].astype(F32) + rows_of(seen_all, d) * norm_in)
        for p in range(4):
            cut = slice(128 * p, 128 * p + 128)
            g, side = p // 2, 128 * (p % 2)
            wide = slice(256 * g, 256 * g + 256)
            edge = slice(side, side + 128)
            qp, kp, vp, gp = q[:, cut], k[:, cut], v[:, cut], gnum[:, cut]
            q2, k2 = split_pair(qp, low, high), split_pair(kp, low, high)
            v2, g2 = split_pair(vp, low, high), split_pair(gp, low, high)
            s_turned = nt(kp, q2).astype(BF16) * turned2
            gs_turned = nt(vp, g2).astype(BF16) * turned2
            gs = nt(gp, v2).astype(BF16) * allowed2
            dq = nn(gs, k2) + nt(gnum_seen[:, wide], states[c, g, edge, :])
            dq = dq + nt(gnum_all[:, wide], groups_in[g][edge, :]) + dq_den[:, cut]
            gq_out[at, cut] = (jnp.minimum(qp.astype(F32), 1.0) * dq).astype(BF16)
            dk = nn(gs_turned, q2) + nt(v_last[:, wide], g_after[g][edge, :]) + dk_den[:, cut]
            dk_out[at, cut] = dk.astype(BF16)
            dv = nn(s_turned, g2) + nn(k_last[:, wide], g_after[g][:, edge])
            dv_out[at, cut] = dv.astype(BF16)
        q_turned = (q * seen).T
        mask = ones[...].astype(F32)
        for g in range(2):
            wide = slice(256 * g, 256 * g + 256)
            after[g] = keep * after[g] + nn(q_turned[wide, :], gnum[:, wide]) * mask
        after_norm[...] = keep * after_norm[...] + column_sum(gden_q * seen.astype(F32))
        return carry

    lax.fori_loop(0, count, step, 0)


def project_back_kernel(
    lens, off, gq_ref, dk_ref, dv_ref, k_ref, v_ref, x_ref, gm_ref, state_grad, ones, vec, w,
    gx_out, g_qkv, g_bias, groups, norm, acc,
):
    m, t, tiles = pl.program_id(0), pl.program_id(1), pl.num_programs(1)
    rows, d = x_ref.shape
    base = off[0]

    @pl.when((m == 0) & (t == 0))
    def _():
        acc[...] = jnp.zeros_like(acc)
        g_bias[...] = jnp.zeros_like(g_bias)

    @pl.when(t == 0)
    def _():
        parts, z = unpack_state(state_grad[...], ones[...])
        for g in range(2):
            groups[g] = parts[g]
        norm[...] = z

    k, v = k_ref[...], v_ref[...]
    final = start_of(lens, m, base + rows * tiles - 1)
    last = flag(start_of(lens, m, place_rows(base + t * rows, rows)) == final)
    last_low = rows_of(last.astype(BF16), d)
    dk = dk_ref[...].astype(F32) + rows_of(last, d) * norm[...]
    dk = dk + by_group(lambda g, a: nt(a, groups[g]), v * last_low)
    gk = (jnp.minimum(k.astype(F32), 1.0) * dk).astype(BF16)
    gv = dv_ref[...].astype(F32) + by_group(lambda g, a: nn(a, groups[g]), k * last_low)
    gv = gv.astype(BF16)
    gq = gq_ref[...]
    gain, bias = vec[0:1, :], vec[1:2, :]
    xhat, scale = normed(x_ref[...].astype(F32))
    h1t = (xhat * gain + bias).astype(BF16).T
    e = jnp.zeros((rows, d), F32)
    for j, part in enumerate((gq, gk, gv)):
        cut = slice(d * j, d * j + d)
        acc[:, cut] += nn(h1t, part)
        e = e + nt(part, w[:, cut])
    gx_out[...] = gm_ref[...] + norm_back(e, xhat, scale, gain)
    g_bias[0:1, :] += column_sum(e * xhat)
    g_bias[1:2, :] += column_sum(e)

    @pl.when((m == pl.num_programs(0) - 1) & (t == tiles - 1))
    def _():
        g_qkv[...] = acc[...].astype(BF16)


def params(count):
    return pltpu.CompilerParams(
        dimension_semantics=("arbitrary",) * count, vmem_limit_bytes=VMEM
    )


def small():
    return pl.BlockSpec(memory_space=pltpu.SMEM)


def per_device(
    block_in, cotangent, ln1_gain, ln1_bias, qkv_weight, out_weight, ln2_gain, ln2_bias,
    up_weight, up_bias, down_weight, down_bias, seq_lengths,
):
    micro, rows, d = block_in.shape[0], block_in.shape[2], block_in.shape[3]
    ff = up_weight.shape[1]
    wide, index = lax.axis_size("wide"), lax.axis_index("wide")
    lens = seq_lengths.reshape(micro, -1)
    off = (index * rows).astype(jnp.int32).reshape(1)
    x = block_in.reshape(micro, rows, d)
    cot = cotangent.reshape(micro, rows, d)

    each = d // wide
    lane = jnp.arange(256) // 64
    ones = (lane[:, None] == lane[None, :]).astype(BF16)

    tiles = rows // TILE
    token = pl.BlockSpec((None, TILE, d), lambda m, t: (m, t, 0))
    whole = lambda shape: pl.BlockSpec(shape, lambda *_: (0,) * len(shape))
    fixed = lambda shape: pl.BlockSpec(
        shape, lambda *_: (0,) * len(shape), pipeline_mode=pl.Buffered(1)
    )
    packed = pl.BlockSpec((None, 272, 128), lambda m, *_: (m, 0, 0))
    like = lambda dtype: jax.ShapeDtypeStruct((micro, rows, d), dtype)
    packed_shape = jax.ShapeDtypeStruct((micro, 272, 128), BF16)

    block = pl.BlockSpec((None, rows, d), lambda m: (m, 0, 0))
    count = rows // CHUNK
    states_spec = pl.BlockSpec((None, count, 2, 256, 256), lambda m: (m, 0, 0, 0, 0))
    steps = micro * tiles
    early = pl.BlockSpec((None, TILE, d), lambda i: (jnp.minimum(i, steps - 1) // tiles, lax.rem(jnp.minimum(i, steps - 1), tiles), 0))
    late = lambda *shape: pl.BlockSpec(
        (None,) + shape, lambda i: (jnp.maximum(i - steps, 0),) + (0,) * len(shape)
    )
    anywhere = pl.BlockSpec(memory_space=pl.ANY)
    spread = lambda a: jax.ShapeDtypeStruct((wide,) + a.shape, BF16)
    dma = pltpu.SemaphoreType.DMA
    vectors = [a.reshape(1, -1) for a in (ln1_gain, ln1_bias, ln2_gain, ln2_bias, down_bias, up_bias)]
    state_shape = (micro, state_rows(), 128)
    (q, k, v, num, kc, states, state_in, w_qkv, w_out, w_up, w_down, vec) = pl.pallas_call(
        first_kernel,
        grid=(steps + micro,),
        in_specs=[small(), small(), early] + [anywhere] * 4 + [whole(a.shape) for a in vectors] + [whole((256, 256))],
        out_specs=[early, early, early, late(rows, d), late(rows, d), late(count, 2, 256, 256), whole(state_shape)]
        + [anywhere] * 4 + [whole((16, d))],
        out_shape=[like(BF16)] * 5 + [
            jax.ShapeDtypeStruct((micro, count, 2, 256, 256), BF16), jax.ShapeDtypeStruct(state_shape, F32),
            spread(qkv_weight), spread(out_weight), spread(up_weight), spread(down_weight),
            jax.ShapeDtypeStruct((16, d), F32),
        ],
        scratch_shapes=[pltpu.VMEM((3, wide, each, d), BF16)]
        + [pltpu.VMEM((micro * rows, d), BF16)] * 3
        + [pltpu.VMEM((2, 256, 256), F32), pltpu.VMEM((1, d), F32)] * 2
        + [
            pltpu.VMEM(state_shape, BF16), pltpu.VMEM((16, 128), BF16), pltpu.VMEM((wide, 16, 128), BF16),
            dma, dma((wide,)), dma((wide,)), dma((3,)),
        ]
        + running_scratch(micro)
        + gather_sems() * 6,
        compiler_params=pltpu.CompilerParams(
            dimension_semantics=("arbitrary",), vmem_limit_bytes=VMEM, collective_id=0, has_side_effects=True
        ),
        name="first",
    )(lens, off, x, qkv_weight, out_weight, up_weight, down_weight, *vectors, ones)
    w_qkv, w_out = w_qkv.reshape(d, 3 * d), w_out.reshape(d, d)
    w_up, w_down = w_up.reshape(d, ff), w_down.reshape(ff, d)

    ends = jnp.cumsum(lens, axis=-1)
    final_places = jnp.arange(1, wide + 1, dtype=jnp.int32) * rows - 1
    finals = jnp.sum(
        jnp.where(ends[:, None, :] <= final_places[None, :, None], lens[:, None, :], 0), axis=-1
    )
    blocks = jnp.arange(wide)
    before = jnp.concatenate([jnp.full((micro, 1), -1, finals.dtype), finals[:, :-1]], axis=1)
    mine = jnp.take(finals, index, axis=1)[:, None]
    reach_up = ((blocks > index)[None] & (before == mine)).astype(F32)

    def combine(part, reach):
        every = lax.all_gather(part, "wide").astype(F32)
        return jnp.einsum("jmrl,mj->mrl", every, reach, precision=lax.Precision.HIGHEST)

    result, g_middle, gnum, gden, use, g_out, g_up, g_down, g_vec, g_up_vec = pl.pallas_call(
        middle_kernel,
        grid=(micro, tiles),
        in_specs=[small(), small()] + [token] * 5 + [packed, whole((256, 256))] + [
            fixed((d, d)), whole((16, d)), fixed((d, ff)), fixed((ff, d)),
        ],
        out_specs=[token, token, token, token, packed, whole((d, d)), whole((d, ff)), whole((d, ff)), whole((8, d)), whole((1, ff))],
        out_shape=[
            like(BF16), like(F32), like(BF16), like(BF16), packed_shape,
            jax.ShapeDtypeStruct((d, d), BF16), jax.ShapeDtypeStruct((d, ff), BF16),
            jax.ShapeDtypeStruct((d, ff), BF16), jax.ShapeDtypeStruct((8, d), F32),
            jax.ShapeDtypeStruct((1, ff), F32),
        ],
        scratch_shapes=[
            pltpu.VMEM((2, 256, 256), BF16), pltpu.VMEM((1, d), F32),
            pltpu.VMEM((2, 256, 256), F32), pltpu.VMEM((1, d), F32),
            pltpu.VMEM((d, d), F32), pltpu.VMEM((d, ff), F32), pltpu.VMEM((d, ff), F32),
            pltpu.VMEM((TILE, d), F32), pltpu.VMEM((TILE, d), F32), pltpu.VMEM((TILE, d), BF16),
            pltpu.VMEM((d, TILE), BF16), pltpu.VMEM((d, TILE), BF16),
        ],
        compiler_params=params(2),
        name="middle",
    )(lens, off, q, num, kc, x, cot, state_in, ones, w_out, vec, w_up, w_down)

    gq, dk, dv = pl.pallas_call(
        attend_back_kernel,
        grid=(micro,),
        in_specs=[small(), small()] + [block] * 6 + [states_spec, pl.BlockSpec((None, 272, 128), lambda m: (m, 0, 0)), whole((256, 256))],
        out_specs=[block] * 3,
        out_shape=[like(BF16)] * 3,
        scratch_shapes=[pltpu.VMEM((2, 256, 256), F32), pltpu.VMEM((1, d), F32)],
        compiler_params=params(1),
        name="attend_back",
    )(lens, off, q, k, v, gnum, gden, kc, states, state_in, ones)
    state_grad = combine(use, reach_up)

    grad_input, g_qkv, g_vec_one = pl.pallas_call(
        project_back_kernel,
        grid=(micro, tiles),
        in_specs=[small(), small()] + [token] * 7 + [packed, whole((256, 256)), whole((16, d)), fixed((d, 3 * d))],
        out_specs=[token, whole((d, 3 * d)), whole((8, d))],
        out_shape=[like(F32), jax.ShapeDtypeStruct((d, 3 * d), BF16), jax.ShapeDtypeStruct((8, d), F32)],
        scratch_shapes=[pltpu.VMEM((2, 256, 256), BF16), pltpu.VMEM((1, d), F32), pltpu.VMEM((d, 3 * d), F32)],
        compiler_params=params(2),
        name="project_back",
    )(lens, off, gq, dk, dv, k, v, x, g_middle, state_grad, ones, vec, w_qkv)

    def shared(grad, axis):
        part = lax.psum_scatter(grad, "wide", scatter_dimension=axis, tiled=True)
        return lax.psum(part, "dp").astype(F32)

    g_all = jnp.concatenate(
        [a.reshape(wide, -1) for a in (g_vec_one[0], g_vec_one[1], g_vec[0], g_vec[1], g_vec[2], g_up_vec[0])], axis=1
    )
    g_all = lax.psum(g_all, ("dp", "wide"))
    g_all = lax.dynamic_index_in_dim(g_all, index, 0, keepdims=False)
    piece = [g_all[each * j : each * j + each] for j in range(5)] + [g_all[5 * each :]]
    return (
        result.reshape(block_in.shape),
        grad_input.reshape(block_in.shape),
        piece[0],
        piece[1],
        shared(g_qkv, 0),
        shared(g_out, 0),
        piece[2],
        piece[3],
        shared(g_up, 0),
        piece[5],
        shared(g_down, 1).T,
        piece[4],
    )


def solution(mesh):
    tokens = P(None, "dp", "wide", None)
    vector, matrix = P("wide"), P("wide", None)
    weights = (vector, vector, matrix, matrix, vector, vector, matrix, vector, matrix, vector)
    return jax.shard_map(
        per_device,
        mesh=mesh,
        in_specs=(tokens, tokens) + weights + (P(None, "dp", None),),
        out_specs=(tokens, tokens) + weights,
        check_vma=False,
    )
```

time: 1110 us -> 579 us (0.52); the launches traced: 1090 us -> 579 us
  matrix products: 471 us -> 4 us
  Pallas kernels: 0 us -> 265 us
  local copies, waits for them, and re-layouts: 255 us -> 7 us
  waiting for transfers between devices: 18.4 us -> 241 us
  other arithmetic: 153 us -> 7.07 us
  blocking collectives: 177 us -> 39.8 us
    dot_general x54 -> x1, matrix products: 471 us -> 4 us  [combine(): jnp.einsum('jmrl,mj->mrl', every, reach, precision=lax.Precision.HIGHEST)]
    pallas_call x0 -> x4, Pallas kernels: none -> 265 us  [the longest x1 103 us: per_device(): pl.pallas_call(middle_kernel, grid=(micro, tiles), in_specs=[small(), sma...]
    reduce_scatter x4, waiting for transfers between devices: 0.03 us -> 239 us  [shared(): part = lax.psum_scatter(grad, 'wide', scatter_dimension=axis, tiled=True)]
    dynamic_update_slice x16 -> x0, local copies, waits for them, and re-layouts: 165 us -> none  [per_device(): lax.map(attend, (query_feat, key_feat, values, starts, state_low, norm_in))]
    all_gather x4 -> x0, blocking collectives: 113 us -> none  [the longest x1 33 us: per_device(): lax.all_gather(out_weight, 'wide', axis=0, tiled=True)]
    unnamed x2 -> x0, blocking collectives: 57.9 us -> none
    reduce_sum x14 -> x1, other arithmetic: 52.7 us -> 0.21 us  [per_device(): jnp.sum(jnp.where(ends[:, None, :] <= final_places[None, :, None], lens[:...]
    psum x1, blocking collectives: 5.64 us -> 39.8 us  [per_device(): g_all = lax.psum(g_all, ('dp', 'wide'))]
  transfers between devices with their start and end apart: 10 -> 6, of which waited for: 2 -> 4; matrix products, arithmetic and copies ran while one was open for 67% -> 2% of each run, Pallas kernels for 0% -> 14%
where the time goes in v1:
time: 579 us
  Pallas kernels  265 us (46%)
  waiting for transfers between devices  241 us (42%)
  blocking collectives  39.8 us (7%)
  between operations  14.2 us (2%)
  other arithmetic  7.07 us (1%)
  local copies, waits for them, and re-layouts  7 us (1%)
    reduce_scatter x4, waiting for transfers between devices, shared(): part = lax.psum_scatter(grad, 'wide', scatter_dimension=axis, tiled=True)  239 us
    pallas_call x1, Pallas kernels, per_device(): pl.pallas_call(middle_kernel, grid=(micro, tiles), in_specs=[small(), sma...  103 us
    pallas_call x1, Pallas kernels, per_device(): pl.pallas_call(first_kernel, grid=(steps + micro,), in_specs=[small(), sm...  79.8 us
    pallas_call x1, Pallas kernels, per_device(): pl.pallas_call(attend_back_kernel, grid=(micro,), in_specs=[small(), smal...  53.4 us
    psum x1, blocking collectives, per_device(): g_all = lax.psum(g_all, ('dp', 'wide'))  39.8 us
    pallas_call x1, Pallas kernels, per_device(): pl.pallas_call(project_back_kernel, grid=(micro, tiles), in_specs=[small(...  29.6 us
  transfers between devices with their start and end apart: 6, of which 4 were waited for; matrix products, arithmetic and copies ran while one was open for 2% of the time, Pallas kernels for 14%

profile of v1, /device:TPU:0, one launch (start us, length us, event | category | flops | bytes accessed | tf_op | source)
XLA Modules:
  0.0 578.5 jit_solution(1594487735944096888)
XLA Ops:
  7.2 0.8 compare_convert_fusion.refs_10_.ones
  8.0 1.2 reshape.129.refs_9_
  9.2 79.8 %first.1 = (bf16[4,1024,512]{2,1,0:T(8,128)(2,1)}, bf16[4,1024,512]{2,1,0:T(8,128)(2,1)}, bf16[4,1024,512]{2,1,0:T(8,128)(2,1)}, bf16[4,1024,512]{2,1,0:T(8,128)...) custom-call(s32[4,8]{1,0:T(4,128)} %bitcast.47, ...), custom_call_target="tpu_custom_call" | custom-call | tf_op jit(solution)/shard_map/first/pallas_call | solution.py:876
  89.0 102.5 %middle.1 = (bf16[4,1024,512]{2,1,0:T(8,128)(2,1)}, f32[4,1024,512]{2,1,0:T(8,128)}, bf16[4,1024,512]{2,1,0:T(8,128)(2,1)}, bf16[4,1024,512]{2,1,0:T(8,128)(2,1)...) custom-call(s32[4,8]{1,0:T(4,128)} %bitcast.48, ...), custom_call_target="tpu_custom_call" | custom-call | tf_op jit(solution)/shard_map/middle/pallas_call | solution.py:918
  191.6 0.7 reduce-scatter.7.cloned.1.call-update
  192.4 0.7 reduce-scatter.11.cloned.1.call-update
  193.1 0.5 reduce-scatter.9.cloned.1.call-update
  193.7 0.2 reduce-scatter.5.cloned.1.call-start
  193.9 0.2 reduce_window_sum.11
  194.1 53.4 %attend_back.1 = (bf16[4,1024,512]{2,1,0:T(8,128)(2,1)}, bf16[4,1024,512]{2,1,0:T(8,128)(2,1)}, bf16[4,1024,512]{2,1,0:T(8,128)(2,1)}) custom-call(s32[4,8]{1,0:T(4,128)} %bitcast.49, s32[1]{0:T(128)} %bitcast.1.off, bf16[4,1024,512]{2,1,0:T(8,128)(2,1)} %get-tuple-element.40.q_ref, bf16[4,1024,512]{2,1,0:T(8,128)(2,1)} %get-tuple-element.49.k_ref, ...), custom_call_target="tpu_custom_call" | custom-call | tf_op jit(solution)/shard_map/attend_back/pallas_call | solution.py:942
  247.5 0.2 select_reduce_fusion
  247.7 0.2 select_reduce_fusion.1
  248.0 4.0 fusion
  252.0 29.6 %project_back.1 = (f32[4,1024,512]{2,1,0:T(8,128)}, bf16[512,1536]{1,0:T(8,128)(2,1)}, f32[8,512]{1,0:T(8,128)}) custom-call(s32[4,8]{1,0:T(4,128)} %bitcast.50, s32[1]{0:T(128)} %bitcast.1.off, bf16[4,1024,512]{2,1,0:T(8,128)(2,1)} %get-tuple-element.54.gq_ref, bf16[4,1024,512]{2,1,0:T(8,128)(2,1)} %get-tuple-element.55.dk_ref, ...), custom_call_target="tpu_custom_call" | custom-call | tf_op jit(solution)/shard_map/project_back/pallas_call | solution.py:954
  281.7 29.2 %reduce-scatter.7.cloned.1.call-done = bf16[64,512]{1,0:T(8,128)(2,1)} async-done(((bf16[512,512]{1,0:T(8,128)(2,1)}), bf16[64,512]{1,0:T(8,128)(2,1)}) %reduce-scatter.7.cloned.1.call-update) | async-done | bytes 65552 | tf_op jit(solution)/shard_map/reduce_scatter | solution.py:966
  310.9 71.3 %reduce-scatter.11.cloned.1.call-done = bf16[512,256]{1,0:T(8,128)(2,1)} async-done(((bf16[512,2048]{1,0:T(8,128)(2,1)}), bf16[512,256]{1,0:T(8,128)(2,1)}) %reduce-scatter.11.cloned.1.call-update) | async-done | bytes 262160 | tf_op jit(solution)/shard_map/reduce_scatter | solution.py:966
  382.2 70.5 %reduce-scatter.9.cloned.1.call-done = bf16[64,2048]{1,0:T(8,128)(2,1)} async-done(((bf16[512,2048]{1,0:T(8,128)(2,1)}), bf16[64,2048]{1,0:T(8,128)(2,1)}) %reduce-scatter.9.cloned.1.call-update) | async-done | bytes 262160 | tf_op jit(solution)/shard_map/reduce_scatter | solution.py:966
  452.8 67.6 %reduce-scatter.5.cloned.1.call-done = bf16[64,1536]{1,0:T(8,128)(2,1)} async-done(((bf16[512,1536]{1,0:T(8,128)(2,1)}), bf16[64,1536]{1,0:T(8,128)(2,1)}) %reduce-scatter.5.cloned.1.call-update) | async-done | bytes 196624 | tf_op jit(solution)/shard_map/reduce_scatter | solution.py:966
  520.4 0.5 broadcast.143
  520.9 0.7 reduce.25
  521.6 0.9 slice_reduce_fusion
  522.5 0.1 reshape_squeeze.20
  522.7 0.8 slice_reduce_fusion.3
  523.5 0.1 reshape_squeeze.18
  523.7 0.1 concatenate.7
  523.8 39.8 %psum.35 = f32[8,576]{1,0:T(8,128)S(1)} all-reduce(f32[8,576]{1,0:T(8,128)S(1)} %concatenate.7), channel_id=1, replica_groups=mesh['dp'=4,'wide'=8] {'dp','wide'}, use_global_device_ids=true, to_apply=%region_2.3 | all-reduce | flops 4608 | bytes 36864 | tf_op jit(solution)/shard_map/psum | solution.py:972
  563.6 0.6 dynamic-slice.8
  564.2 0.6 dynamic-slice_bitcast_fusion
  564.8 1.8 convert_element_type.24
  566.6 1.9 copy.36
  568.5 1.7 convert_element_type.22
  570.2 1.5 convert_element_type.23
  (24 shorter events, 0.6 us)
Async XLA Ops:
  7.2 240.8 %all-gather.3.cloned.1.call-start = ((), (), s32[]{:S(2)}) async-start(), calls=%async_computation.8 | async-start | bytes 2506752 | tf_op jit(solution)/shard_map/all_gather | solution.py:915
  191.6 2.3 copy-start
  191.6 119.3 %reduce-scatter.7.cloned.1.call-start = ((), (), s32[]{:S(2)}) async-start(), calls=%async_computation.5 | async-start | bytes 589824 | tf_op jit(solution)/shard_map/reduce_scatter | solution.py:966
  192.3 189.9 %reduce-scatter.11.cloned.1.call-start = ((), (), s32[]{:S(2)}) async-start(), calls=%async_computation.7 | async-start | bytes 2359296 | tf_op jit(solution)/shard_map/reduce_scatter | solution.py:966
  193.1 259.7 %reduce-scatter.9.cloned.1.call-start = ((), (), s32[]{:S(2)}) async-start(), calls=%async_computation.6 | async-start | bytes 2359296 | tf_op jit(solution)/shard_map/reduce_scatter | solution.py:966
  193.7 326.7 %reduce-scatter.5.cloned.1.call-start = ((), (), s32[]{:S(2)}) async-start(), calls=%async_computation.4 | async-start | bytes 1769472 | tf_op jit(solution)/shard_map/reduce_scatter | solution.py:966
  194.1 53.4 %copy-start.1 = (s32[4,1,8]{2,1,0:T(1,128)S(1)}, s32[4,1,8]{2,1,0:T(1,128)}, u32[]{:S(2)}) copy-start(s32[4,1,8]{2,1,0:T(1,128)} %param.25) | copy-start | bytes 388
  252.0 268.9 %copy-start.2 = (f32[1,2048]{1,0:T(1,128)S(1)}, f32[1,2048]{1,0:T(1,128)}, u32[]{:S(2)}) copy-start(f32[1,2048]{1,0:T(1,128)} %get-tuple-element.63) | copy-start | bytes 24580
  281.6 283.2 %all-reduce.4.cloned.1.call-start = ((), (), s32[]{:S(2)}) async-start(), calls=%async_computation.9 | async-start | bytes 1572864 | tf_op jit(solution)/shard_map/psum | solution.py:967
Sparse Core Ops, SparseCore 0:
  191.7 54.7 all-gather.2
  250.4 60.4 reduce-scatter.6
  314.9 67.3 reduce-scatter.10
  386.0 66.6 reduce-scatter.8
  456.4 63.9 reduce-scatter.4
  522.8 34.1 all-reduce.3

commit v2 on v1

--- a/solution.py
+++ b/solution.py
@@ -14,7 +14,7 @@
 CHUNK = 128
 TILE = 512
 FF_TILE = 512
-VMEM = 60 * 1024 * 1024
+VMEM = 62 * 1024 * 1024
 
 
 def nn(a, b):
@@ -229,6 +229,219 @@
     n, ny = lax.axis_size("wide"), lax.axis_size("dp") // 2
     dma = pltpu.SemaphoreType.DMA
     return [dma, dma((n,)), dma((n,)), dma((ny,)), dma((ny,)), dma, dma]
+
+
+def packed_shape(rows, d):
+    unit = 16 * lax.axis_size("dp")
+    columns = d if rows % unit == 0 else 128
+    rows = rows * (d // columns)
+    return -(-rows // unit) * unit, columns
+
+
+def put(block, at, piece):
+    rows, d = piece.shape
+    columns = block.shape[1]
+    for b in range(d // columns):
+        begin = at * (d // columns) + rows * b
+        block[begin : begin + rows, :] = piece[:, columns * b : columns * b + columns]
+
+
+def fill(block, rows, d):
+    used = rows * (d // block.shape[1])
+    if block.shape[0] > used:
+        block[used:, :] = jnp.zeros((block.shape[0] - used, block.shape[1]), block.dtype)
+
+
+def get(block, at, rows, d):
+    columns = block.shape[1]
+    begin = at * (d // columns)
+    return jnp.concatenate(
+        [block[begin + rows * b : begin + rows * b + rows, :] for b in range(d // columns)], axis=1
+    )
+
+
+class Scatter:
+    def __init__(self, src, refs):
+        self.src = src
+        (self.half, self.got_core, self.got_y, self.got_wide, self.out, self.near, self.c_sem, self.y_send,
+         self.y_recv, self.w_send, self.w_recv, self.yb_send, self.yb_recv, self.cb_sem) = refs
+        self.core, self.y, self.me, self.ny, self.n = place()
+        self.dp = 2 * self.y + self.core
+        self.rows = self.out.shape[0]
+        self.each = self.rows // (2 * self.ny)
+        self.partner = 2 * self.y + 1 - self.core
+        self.part = self.got_core.at[:, 0 : self.each]
+
+    def half_rows(self, core):
+        return pl.ds(pl.multiple_of(core * (self.rows // 2), self.rows // 2), self.rows // 2)
+
+    def y_rows(self, y):
+        return pl.ds(pl.multiple_of(y * self.each, self.each), self.each)
+
+    def own_rows(self, y):
+        at = self.core * (self.rows // 2) + y * self.each
+        return pl.ds(pl.multiple_of(at, self.each), self.each)
+
+    def load(self):
+        return pltpu.make_async_copy(self.src.at[:, self.half_rows(self.core)], self.half, self.near)
+
+    def cross(self):
+        return remote(
+            self.src.at[:, self.half_rows(1 - self.core)], self.got_core, self.c_sem.at[0], self.c_sem.at[1], self.partner, self.me
+        )
+
+    def start1(self):
+        self.cross().start()
+        self.load().start()
+
+    def along_y(self, o):
+        to = lax.rem(self.y + o, self.ny)
+        return remote(
+            self.half.at[:, self.y_rows(to)], self.got_y.at[o - 1], self.y_send.at[o], self.y_recv.at[o],
+            2 * to + self.core, self.me,
+        )
+
+    def finish1_start2(self):
+        self.load().wait()
+        self.cross().wait()
+
+        def add(w, carry):
+            self.half[w] = (self.half[w].astype(F32) + self.got_core[w].astype(F32)).astype(BF16)
+            return carry
+
+        lax.fori_loop(0, self.n, add, 0)
+        others(self.ny, lambda o: self.along_y(o).start())
+
+    def along_wide(self, o):
+        to = lax.rem(self.me + o, self.n)
+        return remote(self.part.at[to], self.got_wide.at[o - 1], self.w_send.at[o], self.w_recv.at[o], self.dp, to)
+
+    def finish2_start3(self):
+        others(self.ny, lambda o: self.along_y(o).wait())
+
+        def add(w, carry):
+            total = self.half[w, self.y_rows(self.y)].astype(F32)
+            for o in range(self.ny - 1):
+                total = total + self.got_y[o, w].astype(F32)
+            self.part[w] = total.astype(BF16)
+            return carry
+
+        lax.fori_loop(0, self.n, add, 0)
+        others(self.n, lambda o: self.along_wide(o).start())
+
+    def back_y(self, o, back=False):
+        other = lax.rem(self.y + o, self.ny)
+        rows = self.own_rows(other if back else self.y)
+        ref = self.out.at[rows]
+        return remote(ref, ref, self.yb_send.at[o], self.yb_recv.at[other if back else self.y], 2 * other + self.core, self.me)
+
+    def finish3_start4(self):
+        others(self.n, lambda o: self.along_wide(o).wait())
+        total = self.part[self.me].astype(F32)
+        total = lax.fori_loop(0, self.n - 1, lambda o, t: t + self.got_wide[o].astype(F32), total)
+        self.out[self.own_rows(self.y)] = total.astype(BF16)
+        others(self.ny, lambda o: self.back_y(o).start())
+
+    def back_core(self, back=False):
+        ref = self.out.at[self.half_rows(1 - self.core if back else self.core)]
+        return remote(ref, ref, self.cb_sem.at[0], self.cb_sem.at[1], self.partner, self.me)
+
+    def finish4_start5(self):
+        others(self.ny, lambda o: self.back_y(o).wait_send())
+        others(self.ny, lambda o: self.back_y(o, True).wait_recv())
+        self.back_core().start()
+
+    def finish5(self):
+        self.back_core().wait_send()
+        self.back_core(True).wait_recv()
+
+
+def scatter_scratch(shape):
+    rows, d = shape
+    n, dp = lax.axis_size("wide"), lax.axis_size("dp")
+    ny, part = dp // 2, rows // dp
+    dma = pltpu.SemaphoreType.DMA
+    return [
+        pltpu.VMEM((n, rows // 2, d), BF16),
+        pltpu.VMEM((n, rows // 2, d), BF16),
+        pltpu.VMEM((ny - 1, n, part, d), BF16),
+        pltpu.VMEM((n - 1, part, d), BF16),
+        pltpu.VMEM((rows, d), BF16),
+        dma, dma((2,)), dma((ny,)), dma((ny,)), dma((n,)), dma((n,)), dma((ny,)), dma((ny,)), dma((2,)),
+    ]
+
+
+class VectorSum:
+    def __init__(self, refs):
+        self.tiles, self.got_core, self.got_y, self.got_wide, self.c_sem, self.y_send, self.y_recv, self.w_send, self.w_recv = refs
+        self.core, self.y, self.me, self.ny, self.n = place()
+        self.dp = 2 * self.y + self.core
+
+    def cross(self):
+        return remote(self.tiles, self.got_core, self.c_sem.at[0], self.c_sem.at[1], 2 * self.y + 1 - self.core, self.me)
+
+    def along_y(self, o):
+        to = lax.rem(self.y + o, self.ny)
+        return remote(self.tiles, self.got_y.at[o - 1], self.y_send.at[o], self.y_recv.at[o], 2 * to + self.core, self.me)
+
+    def along_wide(self, o):
+        to = lax.rem(self.me + o, self.n)
+        return remote(self.tiles.at[to], self.got_wide.at[o - 1], self.w_send.at[o], self.w_recv.at[o], self.dp, to)
+
+    def start1(self):
+        self.cross().start()
+
+    def finish1_start2(self):
+        self.cross().wait()
+        self.tiles[...] = self.tiles[...] + self.got_core[...]
+        others(self.ny, lambda o: self.along_y(o).start())
+
+    def finish2_start3(self):
+        others(self.ny, lambda o: self.along_y(o).wait())
+        total = self.tiles[...]
+        for o in range(self.ny - 1):
+            total = total + self.got_y[o]
+        self.tiles[...] = total
+        others(self.n, lambda o: self.along_wide(o).start())
+
+    def finish3(self):
+        others(self.n, lambda o: self.along_wide(o).wait())
+        return lax.fori_loop(0, self.n - 1, lambda o, t: t + self.got_wide[o], self.tiles[self.me])
+
+
+def vector_scratch():
+    n, ny = lax.axis_size("wide"), lax.axis_size("dp") // 2
+    dma = pltpu.SemaphoreType.DMA
+    return [
+        pltpu.VMEM((n, 16, 128), F32),
+        pltpu.VMEM((n, 16, 128), F32),
+        pltpu.VMEM((ny - 1, n, 16, 128), F32),
+        pltpu.VMEM((n - 1, 16, 128), F32),
+        dma((2,)), dma((ny,)), dma((ny,)), dma((n,)), dma((n,)),
+    ]
+
+
+def owner_tiles(rows, tiles, each):
+    n = tiles.shape[0]
+    d = each * n
+    per = 4 * each
+    row = lax.broadcasted_iota(jnp.int32, (16, 128), 0)
+    lane = lax.broadcasted_iota(jnp.int32, (16, 128), 1)
+    blocks = [rows[:, 128 * j : 128 * j + 128] for j in range(d // 128)]
+
+    def turned(a, by, axis):
+        by = by % a.shape[axis]
+        return pltpu.roll(a, by, axis) if by else a
+
+    for w in range(n):
+        at = each * w
+        tile = jnp.where(row < 5, turned(blocks[at // 128], -(at % 128), 1), 0.0)
+        for r in range(4):
+            at = per * w + each * r
+            from_row, begin = 5 + at // d, at % d
+            moved = turned(turned(blocks[begin // 128], -(begin % 128), 1), 5 + r - from_row, 0)
+            tile = jnp.where(row == 5 + r, moved, tile)
+        tiles[w] = jnp.where(lane < each, tile, 0.0)
 
 
 HIGH = 4
@@ -609,7 +822,7 @@
 def middle_kernel(
     lens, off, q_ref, num_ref, kc_ref, x_ref, cot_ref, state_in, ones,
     w_out, vec, w_up, w_down,
-    block_out, gm_out, gnum_out, gden_out, use_out, g_out, g_up, g_down, g_bias, g_up_bias,
+    block_out, gm_out, gnum_out, gden_out, use_out, grads, g_vec,
     groups, norm, use, use_norm, acc_out, acc_up, acc_down, total, e_total, h2_ref, h2t_ref, ct_ref,
 ):
     m, t, tiles = pl.program_id(0), pl.program_id(1), pl.num_programs(1)
@@ -623,8 +836,7 @@
         acc_out[...] = jnp.zeros_like(acc_out)
         acc_up[...] = jnp.zeros_like(acc_up)
         acc_down[...] = jnp.zeros_like(acc_down)
-        g_bias[...] = jnp.zeros_like(g_bias)
-        g_up_bias[...] = jnp.zeros_like(g_up_bias)
+        g_vec[...] = jnp.zeros_like(g_vec)
 
     @pl.when(t == 0)
     def _():
@@ -669,7 +881,7 @@
         e_total[...] += nt(g_low, w_up[:, cut])
         acc_down[:, cut] += nn(ct_ref[...], active)
         acc_up[:, cut] += nn(h2t_ref[...], g_low)
-        g_up_bias[:, cut] += column_sum(g_hidden)
+        g_vec[pl.ds(5 + f, 1), :] += column_sum(g_hidden)
         return carry
 
     lax.fori_loop(0, w_up.shape[1] // FF_TILE, ffn, 0)
@@ -677,10 +889,10 @@
     e = e_total[...]
     cot = cot_ref[...].astype(F32)
     g_middle = cot + norm_back(e, xhat, scale, gain)
-    gm_out[...] = g_middle
-    g_bias[0:1, :] += column_sum(e * xhat)
-    g_bias[1:2, :] += column_sum(e)
-    g_bias[2:3, :] += column_sum(cot)
+    gm_out[...] = g_middle.astype(BF16)
+    g_vec[2:3, :] += column_sum(e * xhat)
+    g_vec[3:4, :] += column_sum(e)
+    g_vec[4:5, :] += column_sum(cot)
     branch = g_middle.astype(BF16)
     acc_out[...] += nn(mixed.T, branch)
     g_mixed = nt(branch, w_out[...])
@@ -701,20 +913,26 @@
 
     @pl.when(final)
     def _():
-        g_out[...] = acc_out[...].astype(BF16)
-        g_up[...] = acc_up[...].astype(BF16)
-        g_down[...] = acc_down[...].astype(BF16)
-
-
-def attend_back_kernel(
-    lens, off, q_ref, k_ref, v_ref, gnum_ref, gden_ref, kc_ref, states, state_in, ones,
+        n = grads.shape[0]
+        each = d // n
+        down = acc_down[...].astype(BF16).T
+        for w in range(n):
+            at = slice(each * w, each * w + each)
+            block = grads.at[w]
+            for j in range(4):
+                put(block, each * j, acc_up[at, d * j : d * j + d].astype(BF16))
+            put(block, 4 * each, acc_out[at, :].astype(BF16))
+            put(block, 5 * each, down[4 * each * w : 4 * each * w + 4 * each, :])
+            fill(block, 9 * each, d)
+
+
+def attend_back(
+    lens, m, base, q_ref, k_ref, v_ref, gnum_ref, gden_ref, kc_ref, states, state_in, ones,
     gq_out, dk_out, dv_out, after, after_norm,
 ):
-    m = pl.program_id(0)
     rows, d = q_ref.shape
     size = CHUNK
     count = rows // size
-    base = off[0]
     after[...] = jnp.zeros_like(after)
     after_norm[...] = jnp.zeros_like(after_norm)
     half = lane_half((1, 128))
@@ -777,51 +995,180 @@
     lax.fori_loop(0, count, step, 0)
 
 
-def project_back_kernel(
-    lens, off, gq_ref, dk_ref, dv_ref, k_ref, v_ref, x_ref, gm_ref, state_grad, ones, vec, w,
-    gx_out, g_qkv, g_bias, groups, norm, acc,
+def last_kernel(lens, off, *refs):
+    (q_ref, k_ref, v_ref, gnum_ref, gden_ref, kc_ref, states, state_in, k_tile, v_tile, x_ref, use, grads, g_vec,
+     ones, vec, w,
+     gx_out, early_out, later_out, latest_out, vector_out,
+     gq_all, dk_all, dv_all, h1t_all, acc, after, after_norm, groups, norm, sums, src_kv, src_q, *rest) = refs
+    micro = use.shape[0]
+    block_rows, d = q_ref.shape
+    rows = x_ref.shape[0]
+    tiles = block_rows // rows
+    steps = micro * tiles
+    n = src_q.shape[0]
+    each = d // n
+    running = Running(use, False, rest[:13])
+    rest = rest[13:]
+    early, later, latest = Scatter(grads, rest[:14]), Scatter(src_kv, rest[14:28]), Scatter(src_q, rest[28:42])
+    vector = VectorSum(rest[42:])
+    i = pl.program_id(0)
+    base = off[0]
+    p1, p2, p3, end = micro, micro + steps, micro + steps + 1, micro + 2 * steps + 1
+
+    @pl.when(i == 0)
+    def _():
+        greet()
+        running.start1()
+        early.start1()
+        acc[...] = jnp.zeros_like(acc)
+        sums[...] = g_vec[...]
+
+    @pl.when(i == 1)
+    def _():
+        running.finish1_start2()
+        early.finish1_start2()
+
+    @pl.when(i == 2)
+    def _():
+        running.finish2_start3()
+
+    @pl.when(i == 3)
+    def _():
+        running.finish3()
+        early.finish2_start3()
+
+    @pl.when(i < p1)
+    def _():
+        at = pl.ds(pl.multiple_of(i * block_rows, block_rows), block_rows)
+        attend_back(
+            lens, i, base, q_ref, k_ref, v_ref, gnum_ref, gden_ref, kc_ref, states, state_in, ones,
+            gq_all.at[at], dk_all.at[at], dv_all.at[at], after, after_norm,
+        )
+
+    @pl.when(i == p1 + steps // 2)
+    def _():
+        early.finish3_start4()
+
+    @pl.when(i == p1 + steps - 2)
+    def _():
+        early.finish4_start5()
+
+    @pl.when((i >= p1) & (i < p2))
+    def _():
+        j = i - p1
+        m, t = j // tiles, lax.rem(j, tiles)
+
+        @pl.when(t == 0)
+        def _():
+            parts, z = unpack_state(running.result[m], ones[...])
+            for g in range(2):
+                groups[g] = parts[g]
+            norm[...] = z
+
+        at = pl.ds(pl.multiple_of(j * rows, rows), rows)
+        k, v = k_tile[...], v_tile[...]
+        final = start_of(lens, m, base + block_rows - 1)
+        last = flag(start_of(lens, m, place_rows(base + t * rows, rows)) == final)
+        last_low = rows_of(last.astype(BF16), d)
+        dk = dk_all[at, :].astype(F32) + rows_of(last, d) * norm[...]
+        dk = dk + by_group(lambda g, a: nt(a, groups[g]), v * last_low)
+        gk = (jnp.minimum(k.astype(F32), 1.0) * dk).astype(BF16)
+        dk_all[at, :] = gk
+        gv = dv_all[at, :].astype(F32) + by_group(lambda g, a: nn(a, groups[g]), k * last_low)
+        gv = gv.astype(BF16)
+        dv_all[at, :] = gv
+        xhat, _ = normed(x_ref[...].astype(F32))
+        h1t = (xhat * vec[0:1, :] + vec[1:2, :]).astype(BF16).T
+        h1t_all[:, at] = h1t
+        acc[:, d : 2 * d] += nn(h1t, gk)
+        acc[:, 2 * d :] += nn(h1t, gv)
+
+    def arrange(src, parts):
+        for w_ in range(n):
+            for j, p in enumerate(parts):
+                put(src.at[w_], each * j, acc[each * w_ : each * w_ + each, d * p : d * p + d].astype(BF16))
+            fill(src.at[w_], each * len(parts), d)
+
+    @pl.when(i == p2 - 1)
+    def _():
+        arrange(src_kv, (1, 2))
+        later.start1()
+
+    @pl.when(i == p2)
+    def _():
+        early.finish5()
+        early_out[...] = early.out[...]
+
+        def add(m, carry):
+            at = pl.ds(pl.multiple_of(m * block_rows, block_rows), block_rows)
+            acc[:, 0:d] += nn(h1t_all[:, at], gq_all[at, :])
+            return carry
+
+        lax.fori_loop(0, micro, add, 0)
+        arrange(src_q, (0,))
+        later.finish1_start2()
+        latest.start1()
+
+    @pl.when(i == p3 + 1)
+    def _():
+        latest.finish1_start2()
+
+    @pl.when(i == p3 + 3)
+    def _():
+        later.finish2_start3()
+
+    @pl.when(i == p3 + 5)
+    def _():
+        latest.finish2_start3()
+
+    @pl.when(i == end - 1)
+    def _():
+        later.finish3_start4()
+
+    @pl.when(i >= p3)
+    def _():
+        at = pl.ds(pl.multiple_of((i - p3) * rows, rows), rows)
+        e = nt(gq_all[at, :], w[:, 0:d]) + nt(dk_all[at, :], w[:, d : 2 * d]) + nt(dv_all[at, :], w[:, 2 * d :])
+        xhat, scale = normed(x_ref[...].astype(F32))
+        gx_out[...] = norm_back(e, xhat, scale, vec[0:1, :]).astype(BF16)
+        sums[0:1, :] += column_sum(e * xhat)
+        sums[1:2, :] += column_sum(e)
+
+    @pl.when(i == end - 1)
+    def _():
+        owner_tiles(sums[...], vector.tiles, each)
+        vector.start1()
+        latest.finish3_start4()
+        vector.finish1_start2()
+        later.finish4_start5()
+        latest.finish4_start5()
+        vector.finish2_start3()
+        later.finish5()
+        latest.finish5()
+        later_out[...] = later.out[...]
+        latest_out[...] = latest.out[...]
+        vector_out[...] = vector.finish3()
+
+
+def result_kernel(
+    gm_ref, part_ref, early, later, latest, vector, gx, g_qkv, g_out, g_up, g_down, v0, v1, v2, v3, v4, v5
 ):
-    m, t, tiles = pl.program_id(0), pl.program_id(1), pl.num_programs(1)
-    rows, d = x_ref.shape
-    base = off[0]
-
-    @pl.when((m == 0) & (t == 0))
-    def _():
-        acc[...] = jnp.zeros_like(acc)
-        g_bias[...] = jnp.zeros_like(g_bias)
-
-    @pl.when(t == 0)
-    def _():
-        parts, z = unpack_state(state_grad[...], ones[...])
-        for g in range(2):
-            groups[g] = parts[g]
-        norm[...] = z
-
-    k, v = k_ref[...], v_ref[...]
-    final = start_of(lens, m, base + rows * tiles - 1)
-    last = flag(start_of(lens, m, place_rows(base + t * rows, rows)) == final)
-    last_low = rows_of(last.astype(BF16), d)
-    dk = dk_ref[...].astype(F32) + rows_of(last, d) * norm[...]
-    dk = dk + by_group(lambda g, a: nt(a, groups[g]), v * last_low)
-    gk = (jnp.minimum(k.astype(F32), 1.0) * dk).astype(BF16)
-    gv = dv_ref[...].astype(F32) + by_group(lambda g, a: nn(a, groups[g]), k * last_low)
-    gv = gv.astype(BF16)
-    gq = gq_ref[...]
-    gain, bias = vec[0:1, :], vec[1:2, :]
-    xhat, scale = normed(x_ref[...].astype(F32))
-    h1t = (xhat * gain + bias).astype(BF16).T
-    e = jnp.zeros((rows, d), F32)
-    for j, part in enumerate((gq, gk, gv)):
-        cut = slice(d * j, d * j + d)
-        acc[:, cut] += nn(h1t, part)
-        e = e + nt(part, w[:, cut])
-    gx_out[...] = gm_ref[...] + norm_back(e, xhat, scale, gain)
-    g_bias[0:1, :] += column_sum(e * xhat)
-    g_bias[1:2, :] += column_sum(e)
-
-    @pl.when((m == pl.num_programs(0) - 1) & (t == tiles - 1))
-    def _():
-        g_qkv[...] = acc[...].astype(BF16)
+    gx[...] = gm_ref[...].astype(F32) + part_ref[...].astype(F32)
+
+    @pl.when((pl.program_id(0) == 0) & (pl.program_id(1) == 0))
+    def _():
+        each, d = g_out.shape
+        for j in range(4):
+            g_up[:, d * j : d * j + d] = get(early, each * j, each, d).astype(F32)
+        g_out[...] = get(early, 4 * each, each, d).astype(F32)
+        g_down[...] = get(early, 5 * each, 4 * each, d).astype(F32)
+        g_qkv[:, 0:d] = get(latest, 0, each, d).astype(F32)
+        g_qkv[:, d : 2 * d] = get(later, 0, each, d).astype(F32)
+        g_qkv[:, 2 * d :] = get(later, each, each, d).astype(F32)
+        for j, v in enumerate((v0, v1, v2, v3, v4)):
+            v[...] = vector[j : j + 1, :each]
+        for r in range(4):
+            v5[:, each * r : each * r + each] = vector[5 + r : 6 + r, :each]
 
 
 def params(count):
@@ -856,9 +1203,9 @@
     fixed = lambda shape: pl.BlockSpec(
         shape, lambda *_: (0,) * len(shape), pipeline_mode=pl.Buffered(1)
     )
-    packed = pl.BlockSpec((None, 272, 128), lambda m, *_: (m, 0, 0))
+    packed = pl.BlockSpec((None, state_rows(), 128), lambda m, *_: (m, 0, 0))
     like = lambda dtype: jax.ShapeDtypeStruct((micro, rows, d), dtype)
-    packed_shape = jax.ShapeDtypeStruct((micro, 272, 128), BF16)
+    early_shape = packed_shape(9 * each, d)
 
     block = pl.BlockSpec((None, rows, d), lambda m: (m, 0, 0))
     count = rows // CHUNK
@@ -901,32 +1248,16 @@
     w_qkv, w_out = w_qkv.reshape(d, 3 * d), w_out.reshape(d, d)
     w_up, w_down = w_up.reshape(d, ff), w_down.reshape(ff, d)
 
-    ends = jnp.cumsum(lens, axis=-1)
-    final_places = jnp.arange(1, wide + 1, dtype=jnp.int32) * rows - 1
-    finals = jnp.sum(
-        jnp.where(ends[:, None, :] <= final_places[None, :, None], lens[:, None, :], 0), axis=-1
-    )
-    blocks = jnp.arange(wide)
-    before = jnp.concatenate([jnp.full((micro, 1), -1, finals.dtype), finals[:, :-1]], axis=1)
-    mine = jnp.take(finals, index, axis=1)[:, None]
-    reach_up = ((blocks > index)[None] & (before == mine)).astype(F32)
-
-    def combine(part, reach):
-        every = lax.all_gather(part, "wide").astype(F32)
-        return jnp.einsum("jmrl,mj->mrl", every, reach, precision=lax.Precision.HIGHEST)
-
-    result, g_middle, gnum, gden, use, g_out, g_up, g_down, g_vec, g_up_vec = pl.pallas_call(
+    result, g_middle, gnum, gden, use, grads, g_vec = pl.pallas_call(
         middle_kernel,
         grid=(micro, tiles),
         in_specs=[small(), small()] + [token] * 5 + [packed, whole((256, 256))] + [
             fixed((d, d)), whole((16, d)), fixed((d, ff)), fixed((ff, d)),
         ],
-        out_specs=[token, token, token, token, packed, whole((d, d)), whole((d, ff)), whole((d, ff)), whole((8, d)), whole((1, ff))],
+        out_specs=[token, token, token, token, packed, fixed((wide,) + early_shape), whole((16, d))],
         out_shape=[
-            like(BF16), like(F32), like(BF16), like(BF16), packed_shape,
-            jax.ShapeDtypeStruct((d, d), BF16), jax.ShapeDtypeStruct((d, ff), BF16),
-            jax.ShapeDtypeStruct((d, ff), BF16), jax.ShapeDtypeStruct((8, d), F32),
-            jax.ShapeDtypeStruct((1, ff), F32),
+            like(BF16), like(BF16), like(BF16), like(BF16), jax.ShapeDtypeStruct(state_shape, BF16),
+            jax.ShapeDtypeStruct((wide,) + early_shape, BF16), jax.ShapeDtypeStruct((16, d), F32),
         ],
         scratch_shapes=[
             pltpu.VMEM((2, 256, 256), BF16), pltpu.VMEM((1, d), F32),
@@ -939,51 +1270,72 @@
         name="middle",
     )(lens, off, q, num, kc, x, cot, state_in, ones, w_out, vec, w_up, w_down)
 
-    gq, dk, dv = pl.pallas_call(
-        attend_back_kernel,
-        grid=(micro,),
-        in_specs=[small(), small()] + [block] * 6 + [states_spec, pl.BlockSpec((None, 272, 128), lambda m: (m, 0, 0)), whole((256, 256))],
-        out_specs=[block] * 3,
-        out_shape=[like(BF16)] * 3,
-        scratch_shapes=[pltpu.VMEM((2, 256, 256), F32), pltpu.VMEM((1, d), F32)],
-        compiler_params=params(1),
-        name="attend_back",
-    )(lens, off, q, k, v, gnum, gden, kc, states, state_in, ones)
-    state_grad = combine(use, reach_up)
-
-    grad_input, g_qkv, g_vec_one = pl.pallas_call(
-        project_back_kernel,
+    def first(*shape, buffers=2):
+        at = lambda i: (jnp.minimum(i, micro - 1),) + (0,) * len(shape)
+        return pl.BlockSpec((None,) + shape, at, pipeline_mode=pl.Buffered(buffers))
+
+    spare = 2 if wide <= 8 else 1
+
+    def walk(*begins):
+        def at(i):
+            j = 0
+            for b in begins:
+                j = j + jnp.where(i >= b, jnp.clip(i - b, 0, steps - 1) - j, 0)
+            return (j // tiles, lax.rem(j, tiles), 0)
+
+        return pl.BlockSpec((None, TILE, d), at)
+
+    p1, p3 = micro, micro + steps + 1
+    kv_shape, q_shape = packed_shape(2 * each, d), packed_shape(each, d)
+    vector_shapes = [(1, each)] * 5 + [(1, 4 * each)]
+    summed_shapes = [early_shape, kv_shape, q_shape, (16, 128)]
+    result_shapes = [(each, 3 * d), (each, d), (each, ff), (4 * each, d)] + vector_shapes
+    part, *summed = pl.pallas_call(
+        last_kernel,
+        grid=(micro + 2 * steps + 1,),
+        in_specs=[small(), small()] + [first(rows, d, buffers=spare)] * 6 + [first(count, 2, 256, 256, buffers=1), first(state_rows(), 128)]
+        + [walk(p1)] * 2 + [walk(p1, p3)] + [anywhere] * 2
+        + [whole((16, d)), whole((256, 256)), whole((16, d)), fixed((d, 3 * d))],
+        out_specs=[walk(p3)] + [fixed(s) for s in summed_shapes],
+        out_shape=[like(BF16)] + [jax.ShapeDtypeStruct(s, BF16) for s in summed_shapes[:3]]
+        + [jax.ShapeDtypeStruct((16, 128), F32)],
+        scratch_shapes=[pltpu.VMEM((micro * rows, d), BF16)] * 3
+        + [
+            pltpu.VMEM((d, micro * rows), BF16), pltpu.VMEM((d, 3 * d), F32),
+            pltpu.VMEM((2, 256, 256), F32), pltpu.VMEM((1, d), F32),
+            pltpu.VMEM((2, 256, 256), BF16), pltpu.VMEM((1, d), F32), pltpu.VMEM((16, d), F32),
+            pltpu.VMEM((wide,) + kv_shape, BF16), pltpu.VMEM((wide,) + q_shape, BF16),
+        ]
+        + running_scratch(micro)
+        + scatter_scratch(early_shape) + scatter_scratch(kv_shape) + scatter_scratch(q_shape)
+        + vector_scratch(),
+        compiler_params=pltpu.CompilerParams(
+            dimension_semantics=("arbitrary",), vmem_limit_bytes=VMEM, collective_id=1, has_side_effects=True
+        ),
+        name="last",
+    )(lens, off, q, k, v, gnum, gden, kc, states, state_in, k, v, x, use, grads, g_vec, ones, vec, w_qkv)
+    grad_input, g_qkv, g_out, g_up, g_down, *g_vectors = pl.pallas_call(
+        result_kernel,
         grid=(micro, tiles),
-        in_specs=[small(), small()] + [token] * 7 + [packed, whole((256, 256)), whole((16, d)), fixed((d, 3 * d))],
-        out_specs=[token, whole((d, 3 * d)), whole((8, d))],
-        out_shape=[like(F32), jax.ShapeDtypeStruct((d, 3 * d), BF16), jax.ShapeDtypeStruct((8, d), F32)],
-        scratch_shapes=[pltpu.VMEM((2, 256, 256), BF16), pltpu.VMEM((1, d), F32), pltpu.VMEM((d, 3 * d), F32)],
+        in_specs=[token, token] + [whole(s) for s in summed_shapes],
+        out_specs=[token] + [whole(s) for s in result_shapes],
+        out_shape=[like(F32)] + [jax.ShapeDtypeStruct(s, F32) for s in result_shapes],
         compiler_params=params(2),
-        name="project_back",
-    )(lens, off, gq, dk, dv, k, v, x, g_middle, state_grad, ones, vec, w_qkv)
-
-    def shared(grad, axis):
-        part = lax.psum_scatter(grad, "wide", scatter_dimension=axis, tiled=True)
-        return lax.psum(part, "dp").astype(F32)
-
-    g_all = jnp.concatenate(
-        [a.reshape(wide, -1) for a in (g_vec_one[0], g_vec_one[1], g_vec[0], g_vec[1], g_vec[2], g_up_vec[0])], axis=1
-    )
-    g_all = lax.psum(g_all, ("dp", "wide"))
-    g_all = lax.dynamic_index_in_dim(g_all, index, 0, keepdims=False)
-    piece = [g_all[each * j : each * j + each] for j in range(5)] + [g_all[5 * each :]]
+        name="result",
+    )(g_middle, part, *summed)
+    piece = [a.reshape(-1) for a in g_vectors]
     return (
         result.reshape(block_in.shape),
         grad_input.reshape(block_in.shape),
         piece[0],
         piece[1],
-        shared(g_qkv, 0),
-        shared(g_out, 0),
+        g_qkv,
+        g_out,
         piece[2],
         piece[3],
-        shared(g_up, 0),
+        g_up,
         piece[5],
-        shared(g_down, 1).T,
+        g_down,
         piece[4],
     )
 

time: 579 us -> 321 us (0.55)
  waiting for transfers between devices: 241 us -> 0 us
  Pallas kernels: 265 us -> 318 us
  blocking collectives: 39.8 us -> 0 us
  between operations: 14.2 us -> 0.83 us
  other arithmetic: 7.07 us -> 0.76 us
    reduce_scatter x4 -> x0, waiting for transfers between devices: 239 us -> none  [shared(): part = lax.psum_scatter(grad, 'wide', scatter_dimension=axis, tiled=True)]
    pallas_call x2, Pallas kernels: 83 us -> 136 us  [the longest x1 126 us: per_device(): pl.pallas_call(last_kernel, grid=(micro + 2 * steps + 1,), in_specs=[smal...]
    psum x1 -> x0, blocking collectives: 39.8 us -> none  [per_device(): g_all = lax.psum(g_all, ('dp', 'wide'))]
  transfers between devices with their start and end apart: 6 -> 0, of which waited for: 4 -> 0; matrix products, arithmetic and copies ran while one was open for 2% -> 0% of each run, Pallas kernels for 14% -> 0%
where the time goes in v2:
time: 321 us
  Pallas kernels  318 us (99%)
    pallas_call x1, Pallas kernels, per_device(): pl.pallas_call(last_kernel, grid=(micro + 2 * steps + 1,), in_specs=[smal...  126 us
    pallas_call x1, Pallas kernels, per_device(): pl.pallas_call(middle_kernel, grid=(micro, tiles), in_specs=[small(), sma...  103 us
    pallas_call x1, Pallas kernels, per_device(): pl.pallas_call(first_kernel, grid=(steps + micro,), in_specs=[small(), sm...  79.8 us
    pallas_call x1, Pallas kernels, per_device(): pl.pallas_call(result_kernel, grid=(micro, tiles), in_specs=[token, token...  9.88 us

profile of v2, /device:TPU:0, one launch (start us, length us, event | category | flops | bytes accessed | tf_op | source)
XLA Modules:
  0.0 320.9 jit_solution(8652348069927622954)
XLA Ops:
  0.6 1.2 reshape.124.refs_9_
  1.9 0.8 compare_convert_fusion.refs_10_.ones.refs_14_
  2.6 79.8 %first.1 = (bf16[4,1024,512]{2,1,0:T(8,128)(2,1)}, bf16[4,1024,512]{2,1,0:T(8,128)(2,1)}, bf16[4,1024,512]{2,1,0:T(8,128)(2,1)}, bf16[4,1024,512]{2,1,0:T(8,128)...) custom-call(s32[4,8]{1,0:T(4,128)} %bitcast.33, ...), custom_call_target="tpu_custom_call" | custom-call | tf_op jit(solution)/shard_map/first/pallas_call | solution.py:1223
  82.5 102.7 %middle.1 = (bf16[4,1024,512]{2,1,0:T(8,128)(2,1)}, bf16[4,1024,512]{2,1,0:T(8,128)(2,1)}, bf16[4,1024,512]{2,1,0:T(8,128)(2,1)}, bf16[4,1024,512]{2,1,0:T(8,128...) custom-call(s32[4,8]{1,0:T(4,128)} %bitcast.34, s32[1]{0:T(128)} %bitcast.1.off, ...), custom_call_target="tpu_custom_call" | custom-call | tf_op jit(solution)/shard_map/middle/pallas_call | solution.py:1251
  185.2 125.6 %last.1 = (bf16[4,1024,512]{2,1,0:T(8,128)(2,1)}, bf16[576,512]{1,0:T(8,128)(2,1)}, bf16[128,512]{1,0:T(8,128)(2,1)}, bf16[64,512]{1,0:T(8,128)(2,1)}, f32[16,128]{1,0:T(8,128)}) custom-call(s32[4,8]{1,0:T(4,128)} %bitcast.35, s32[1]{0:T(128)} %bitcast.1.off, bf16[4,1024,512]{2,1,0:T(8,128)(2,1)} %get-tuple-element.47.q_ref.refs_0_, ...), custom_call_target="tpu_custom_call" | custom-call | tf_op jit(solution)/shard_map/last/pallas_call | solution.py:1293
  310.9 9.9 %result.1 = (f32[4,1024,512]{2,1,0:T(8,128)}, f32[64,1536]{1,0:T(8,128)}, f32[64,512]{1,0:T(8,128)}, f32[64,2048]{1,0:T(8,128)}, f32[256,512]{1,0:T(8,128)}, /*i...) custom-call(bf16[4,1024,512]{2,1,0:T(8,128)(2,1)} %get-tuple-element, ...), custom_call_target="tpu_custom_call" | custom-call | tf_op jit(solution)/shard_map/result/pallas_call | solution.py:1317
  (1 shorter events, 0.0 us)

commit v3 on v2

--- a/solution.py
+++ b/solution.py
@@ -79,11 +79,10 @@
 
 
 def pack_state(state, norm, out):
-    folded = []
-    for s in state:
-        y = s[:, :128] + s[:, 128:]
-        folded.append(y + pltpu.roll(y, 64, 1))
-    out[0:256, :] = jnp.where(lane_half((256, 128)), folded[0], folded[1]).astype(out.dtype)
+    folded = [s + pltpu.roll(s, 64, 1) for s in state]
+    half = lane_half((128, 128))
+    for j in range(2):
+        out[128 * j : 128 * j + 128, :] = jnp.where(half, folded[j], folded[2 + j]).astype(out.dtype)
     row = lax.broadcasted_iota(jnp.int32, (16, 128), 0)
     tail = jnp.zeros((16, 128), F32)
     for j in range(4):
@@ -93,15 +92,28 @@
         out[272:, :] = jnp.zeros((out.shape[0] - 272, 128), out.dtype)
 
 
-def unpack_state(packed, ones):
-    z = packed[0:256, :]
-    turned = pltpu.roll(z, 64, 1)
-    half = lane_half((256, 128))
-    groups = []
-    for part in (jnp.where(half, z, turned), jnp.where(half, turned, z)):
-        groups.append(jnp.concatenate([part, part], axis=1).astype(BF16) * ones)
+def unpack_pairs(packed, ones):
+    half = lane_half((128, 128))
+    mask = ones[0:128, 0:128].astype(F32)
+    pairs = [None] * 4
+    for j in range(2):
+        z = packed[128 * j : 128 * j + 128, :]
+        turned = pltpu.roll(z, 64, 1)
+        pairs[j] = jnp.where(half, z, turned) * mask
+        pairs[2 + j] = jnp.where(half, turned, z) * mask
     tail = packed[256:272, :]
     norm = jnp.concatenate([tail[j : j + 1, :] for j in range(4)], axis=1)
+    return pairs, norm
+
+
+def unpack_state(packed, ones):
+    pairs, norm = unpack_pairs(packed, ones)
+    zero = jnp.zeros((128, 128), BF16)
+    groups = []
+    for g in range(2):
+        above = jnp.concatenate([pairs[2 * g].astype(BF16), zero], axis=1)
+        below = jnp.concatenate([zero, pairs[2 * g + 1].astype(BF16)], axis=1)
+        groups.append(jnp.concatenate([above, below], axis=0))
     return groups, norm
 
 
@@ -136,9 +148,8 @@
         pl.semaphore_signal(barrier, inc=1, device_id=(d, w), device_id_type=MESH)
 
     others(n, lambda o: signal(dp, lax.rem(me + o, n)))
-    others(ny, lambda o: signal(2 * lax.rem(y + o, ny) + core, me))
-    signal(2 * y + 1 - core, me)
-    pl.semaphore_wait(barrier, n - 1 + ny - 1 + 1)
+    others(2 * ny, lambda o: signal(lax.rem(dp + o, 2 * ny), me))
+    pl.semaphore_wait(barrier, n - 1 + 2 * ny - 1)
 
 
 class Gather:
@@ -264,7 +275,7 @@
     def __init__(self, src, refs):
         self.src = src
         (self.half, self.got_core, self.got_y, self.got_wide, self.out, self.near, self.c_sem, self.y_send,
-         self.y_recv, self.w_send, self.w_recv, self.yb_send, self.yb_recv, self.cb_sem) = refs
+         self.y_recv, self.w_send, self.w_recv, self.b_send, self.b_recv) = refs
         self.core, self.y, self.me, self.ny, self.n = place()
         self.dp = 2 * self.y + self.core
         self.rows = self.out.shape[0]
@@ -329,31 +340,23 @@
         lax.fori_loop(0, self.n, add, 0)
         others(self.n, lambda o: self.along_wide(o).start())
 
-    def back_y(self, o, back=False):
-        other = lax.rem(self.y + o, self.ny)
-        rows = self.own_rows(other if back else self.y)
-        ref = self.out.at[rows]
-        return remote(ref, ref, self.yb_send.at[o], self.yb_recv.at[other if back else self.y], 2 * other + self.core, self.me)
+    def back(self, o, wait=False):
+        other = lax.rem(self.dp + o, 2 * self.ny)
+        slot = other if wait else self.dp
+        at = lax.rem(slot, 2) * (self.rows // 2) + (slot // 2) * self.each
+        ref = self.out.at[pl.ds(pl.multiple_of(at, self.each), self.each)]
+        return remote(ref, ref, self.b_send.at[o], self.b_recv.at[slot], other, self.me)
 
     def finish3_start4(self):
         others(self.n, lambda o: self.along_wide(o).wait())
         total = self.part[self.me].astype(F32)
         total = lax.fori_loop(0, self.n - 1, lambda o, t: t + self.got_wide[o].astype(F32), total)
         self.out[self.own_rows(self.y)] = total.astype(BF16)
-        others(self.ny, lambda o: self.back_y(o).start())
-
-    def back_core(self, back=False):
-        ref = self.out.at[self.half_rows(1 - self.core if back else self.core)]
-        return remote(ref, ref, self.cb_sem.at[0], self.cb_sem.at[1], self.partner, self.me)
-
-    def finish4_start5(self):
-        others(self.ny, lambda o: self.back_y(o).wait_send())
-        others(self.ny, lambda o: self.back_y(o, True).wait_recv())
-        self.back_core().start()
-
-    def finish5(self):
-        self.back_core().wait_send()
-        self.back_core(True).wait_recv()
+        others(2 * self.ny, lambda o: self.back(o).start())
+
+    def finish4(self):
+        others(2 * self.ny, lambda o: self.back(o).wait_send())
+        others(2 * self.ny, lambda o: self.back(o, True).wait_recv())
 
 
 def scatter_scratch(shape):
@@ -367,7 +370,7 @@
         pltpu.VMEM((ny - 1, n, part, d), BF16),
         pltpu.VMEM((n - 1, part, d), BF16),
         pltpu.VMEM((rows, d), BF16),
-        dma, dma((2,)), dma((ny,)), dma((ny,)), dma((n,)), dma((n,)), dma((ny,)), dma((ny,)), dma((2,)),
+        dma, dma((2,)), dma((ny,)), dma((ny,)), dma((n,)), dma((n,)), dma((dp,)), dma((dp,)),
     ]
 
 
@@ -604,27 +607,23 @@
         out[:, 128 * j : 128 * j + 128] = block
 
 
-def first_kernel(
-    lens, off, x, *refs
-):
+def first_kernel(lens, off, x, *refs):
     (s_qkv, s_out, s_up, s_down, v0, v1, v2, v3, v4, v5, ones,
      q_out, k_out, v_out, num_out, kc_out, states_out, state_in, w_qkv, w_out, w_up, w_down, vec_out,
-     w_ref, q_all, k_all, v_all, acc, zacc, state, norm, local, tile, tiles_ref, tile_near, tile_send, tile_recv,
+     w_ref, h_all, q_all, k_all, v_all, state, norm, local, tile, tiles_ref, tile_near, tile_send, tile_recv,
      save_sem, *rest) = refs
     each = s_qkv.shape[0]
-    running_refs, rest = rest[:13], rest[13:]
+    micro, rows, d = x.shape
+    half = micro // 2
+    running = []
+    for j in range(2):
+        running.append(Running(local.at[half * j : half * j + half], True, rest[:13]))
+        rest = rest[13:]
     jobs = []
-    d = x.shape[1]
     for j in range(3):
         jobs.append(Gather(s_qkv.at[:, d * j : d * j + d], w_ref.at[j], rest[7 * j : 7 * j + 7]))
     for j, (src, dst) in enumerate(((s_out, w_out), (s_up, w_up), (s_down, w_down))):
         jobs.append(Gather(src, dst, rest[21 + 7 * j : 28 + 7 * j]))
-    running = Running(local, True, running_refs)
-    rows = x.shape[0]
-    micro = local.shape[0]
-    block_rows = num_out.shape[0]
-    tiles = block_rows // rows
-    steps = micro * tiles
     i = pl.program_id(0)
     core, y, me, ny, n = place()
     dp = 2 * y + core
@@ -639,6 +638,9 @@
 
     def save(j):
         return pltpu.make_async_copy(w_ref.at[j], w_qkv.at[:, :, d * j : d * j + d], save_sem.at[j])
+
+    def weights(j):
+        return w_ref[j].reshape(d, d)
 
     @pl.when(i == 0)
     def _():
@@ -648,110 +650,124 @@
         others(n, lambda o: vec_copy(o).start())
         for job in jobs[:3]:
             job.start_wide()
-
-    @pl.when(i < steps)
-    def _():
-        xhat, _ = normed(x[...].astype(F32))
-
-        @pl.when(i == 0)
-        def _():
-            vec_near().wait()
-            others(n, lambda o: vec_copy(o).wait_send())
-            others(n, lambda o: vec_copy(o, True).wait_recv())
-            spread_vectors(tiles_ref, vec_out, each)
-            for job in jobs[:3]:
-                job.finish_wide()
-                job.start_y()
-            for job in jobs[3:]:
-                job.start_wide()
-            for job in jobs[:3]:
-                job.finish_y()
-                job.start_core()
-            jobs[0].finish_core()
-
-        h1 = (xhat * vec_out[0:1, :] + vec_out[1:2, :]).astype(BF16)
-        at = pl.ds(pl.multiple_of(i * rows, rows), rows)
-
-        def weights(j):
-            return w_ref[j].reshape(d, d)
-
-        q = feature(nn(h1, weights(0))).astype(BF16)
+        vec_near().wait()
+        others(n, lambda o: vec_copy(o).wait_send())
+        others(n, lambda o: vec_copy(o, True).wait_recv())
+        spread_vectors(tiles_ref, vec_out, each)
+
+        def norm_micro(m, carry):
+            xhat, _ = normed(x[m].astype(F32))
+            h_all[m] = (xhat * vec_out[0:1, :] + vec_out[1:2, :]).astype(BF16)
+            return carry
+
+        lax.fori_loop(0, micro // 2, norm_micro, 0)
+        jobs[0].finish_wide()
+        jobs[0].start_y()
+        lax.fori_loop(micro // 2, micro, norm_micro, 0)
+        for job in jobs[1:3]:
+            job.finish_wide()
+            job.start_y()
+        for job in jobs[3:]:
+            job.start_wide()
+        jobs[0].finish_y()
+        jobs[0].start_core()
+        jobs[0].finish_core()
+
+    @pl.when(i == 1)
+    def _():
+        jobs[1].finish_y()
+        jobs[1].start_core()
+
+    @pl.when(i == 2)
+    def _():
+        jobs[2].finish_y()
+        jobs[2].start_core()
+
+    @pl.when(i < micro)
+    def _():
+        q = feature(nn(h_all[i], weights(0))).astype(BF16)
         q_out[...] = q
-        q_all[at, :] = q
-
-        @pl.when(i == 0)
-        def _():
-            jobs[1].finish_core()
-
-        k = feature(nn(h1, weights(1))).astype(BF16)
+        q_all[i] = q
+
+    @pl.when(i == micro)
+    def _():
+        jobs[1].finish_core()
+
+    @pl.when((i >= micro) & (i < 2 * micro))
+    def _():
+        m = i - micro
+        k = feature(nn(h_all[m], weights(1))).astype(BF16)
         k_out[...] = k
-        k_all[at, :] = k
-
-        @pl.when(i == 0)
-        def _():
-            jobs[2].finish_core()
-            for j in range(3):
-                save(j).start()
-
-        v = nn(h1, weights(2)).astype(BF16)
+        k_all[m] = k
+
+    @pl.when(i == 2 * micro)
+    def _():
+        jobs[2].finish_core()
+        for j in range(3):
+            save(j).start()
+
+    @pl.when((i >= 2 * micro) & (i < 3 * micro))
+    def _():
+        m = i - 2 * micro
+        v = nn(h_all[m], weights(2)).astype(BF16)
         v_out[...] = v
-        v_all[at, :] = v
-        m, t = i // tiles, lax.rem(i, tiles)
+        v_all[m] = v
         base = off[0]
-        final = start_of(lens, m, base + block_rows - 1)
-        last = flag(start_of(lens, m, place_rows(base + t * rows, rows)) == final)
-        k_last = k * rows_of(last.astype(BF16), d)
+        final = start_of(lens, m, base + rows - 1)
+        last = flag(start_of(lens, m, place_rows(base, rows)) == final)
+        k_last = k_all[m] * rows_of(last.astype(BF16), d)
         k_turned = k_last.T
-
-        @pl.when(t == 0)
-        def _():
-            acc[...] = jnp.zeros_like(acc)
-            zacc[...] = jnp.zeros_like(zacc)
-
-        for g in range(2):
-            acc[g] += nn(k_turned[256 * g : 256 * g + 256, :], v[:, 256 * g : 256 * g + 256])
-        zacc[...] += column_sum(k_last.astype(F32))
-
-        @pl.when(t == tiles - 1)
-        def _():
-            mask = ones[...].astype(F32)
-            pack_state([acc[0] * mask, acc[1] * mask], zacc[...], local.at[m])
-
-    @pl.when(i == steps - 1)
-    def _():
-        running.start1()
-
-    @pl.when(i == steps)
+        mask = ones[0:128, 0:128].astype(F32)
+        parts = [nn(k_turned[128 * p : 128 * p + 128, :], v[:, 128 * p : 128 * p + 128]) * mask for p in range(4)]
+        pack_state(parts, column_sum(k_last.astype(F32)), local.at[m])
+
+    @pl.when(i == 2 * micro + half - 1)
+    def _():
+        running[0].start1()
+
+    @pl.when(i == 2 * micro + half)
     def _():
         for job in jobs[3:5]:
             job.finish_wide()
             job.start_y()
 
-    @pl.when(i == steps + 1)
-    def _():
-        running.finish1_start2()
+    @pl.when(i == 3 * micro - 1)
+    def _():
+        running[1].start1()
+
+    @pl.when(i == 3 * micro)
+    def _():
+        running[0].finish1_start2()
+
+    @pl.when(i == 3 * micro + 1)
+    def _():
+        running[1].finish1_start2()
         jobs[5].finish_wide()
         jobs[5].start_y()
 
-    @pl.when(i == steps + 2)
-    def _():
-        running.finish2_start3()
+    @pl.when(i == 3 * micro + 2)
+    def _():
+        running[0].finish2_start3()
         for job in jobs[3:5]:
             job.finish_y()
             job.start_core()
 
-    @pl.when(i >= steps)
-    def _():
-        m = i - steps
-        at = pl.ds(pl.multiple_of(m * block_rows, block_rows), block_rows)
-        attend(lens, m, off[0], q_all.at[at], k_all.at[at], v_all.at[at], ones, num_out, kc_out, states_out, state, norm)
-
-    @pl.when(i == steps + micro - 1)
+    @pl.when(i == 3 * micro + 3)
+    def _():
+        running[1].finish2_start3()
+
+    @pl.when(i >= 3 * micro)
+    def _():
+        m = i - 3 * micro
+        attend(lens, m, off[0], q_all.at[m], k_all.at[m], v_all.at[m], ones, num_out, kc_out, states_out, state, norm)
+
+    @pl.when(i == 4 * micro - 1)
     def _():
         jobs[5].finish_y()
         jobs[5].start_core()
-        running.finish3()
-        state_in[...] = running.result[...]
+        for j in range(2):
+            running[j].finish3()
+            state_in[half * j : half * j + half] = running[j].result[...]
         for job in jobs[3:]:
             job.finish_core()
         for j in range(3):
@@ -796,27 +812,25 @@
         last = flag(by_row == final).astype(BF16)
         keep = jnp.where(final < begin, 1.0, 0.0)
         kc_out[at, :] = (nn(allowed, k) + rows_of(seen, d) * norm[...]).astype(BF16)
-        groups = [state[g].astype(BF16) for g in range(2)]
-        for g in range(2):
-            states_out[c, g] = groups[g]
         q_seen = q * rows_of(seen.astype(BF16), d)
         for p in range(4):
             cut = slice(128 * p, 128 * p + 128)
             s = nt(q[:, cut], split_pair(k[:, cut], low, high)).astype(BF16) * allowed2
             inside = nn(s, split_pair(v[:, cut], low, high))
-            g, side = p // 2, 128 * (p % 2)
-            before = nn(q_seen[:, 256 * g : 256 * g + 256], groups[g][:, side : side + 128])
+            held = state[p].astype(BF16)
+            states_out[c, p] = held
+            before = nn(q_seen[:, cut], held)
             num_out[at, cut] = (inside + before).astype(BF16)
         k_last = k * rows_of(last, d)
         k_turned = k_last.T
-        mask = ones[...].astype(F32)
-        for g in range(2):
-            cut = slice(256 * g, 256 * g + 256)
-            state[g] = keep * state[g] + nn(k_turned[cut, :], v[:, cut]) * mask
+        mask = ones[0:128, 0:128].astype(F32)
+        for p in range(4):
+            cut = slice(128 * p, 128 * p + 128)
+            state[p] = keep * state[p] + nn(k_turned[cut, :], v[:, cut]) * mask
         norm[...] = keep * norm[...] + column_sum(k_last.astype(F32))
         return carry
 
-    lax.fori_loop(0, rows // size, step, 0)
+    lax.fori_loop(0, rows // size, step, 0, unroll=8)
 
 
 def middle_kernel(
@@ -884,7 +898,7 @@
         g_vec[pl.ds(5 + f, 1), :] += column_sum(g_hidden)
         return carry
 
-    lax.fori_loop(0, w_up.shape[1] // FF_TILE, ffn, 0)
+    lax.fori_loop(0, w_up.shape[1] // FF_TILE, ffn, 0, unroll=True)
     block_out[...] = total[...].astype(BF16)
     e = e_total[...]
     cot = cot_ref[...].astype(F32)
@@ -908,8 +922,8 @@
 
     @pl.when(t == tiles - 1)
     def _():
-        mask = ones[...].astype(F32)
-        pack_state([use[0] * mask, use[1] * mask], use_norm[...], use_out)
+        mask = ones[0:128, 0:128].astype(F32)
+        pack_state([use[p // 2][128 * (p % 2) : 128 * (p % 2) + 128, 128 * (p % 2) : 128 * (p % 2) + 128] * mask for p in range(4)], use_norm[...], use_out)
 
     @pl.when(final)
     def _():
@@ -938,7 +952,7 @@
     half = lane_half((1, 128))
     low = flag(half).astype(BF16)
     high = flag(jnp.logical_not(half)).astype(BF16)
-    groups_in, norm_in = unpack_state(state_in[...], ones[...])
+    pairs_in, norm_in = unpack_pairs(state_in[...], ones[...])
 
     def step(i, carry):
         c = count - 1 - i
@@ -959,61 +973,61 @@
         last = flag(by_row == final)
         keep = jnp.where(final < begin, 1.0, 0.0)
         last_low = rows_of(last.astype(BF16), d)
-        g_after = [after[g].astype(BF16) for g in range(2)]
+        carried = jnp.where((c == 0) | (start_of(lens, m, begin - 1) < base), 1.0, 0.0)
         gnum_seen = gnum * seen
-        gnum_all = gnum * rows_of(seen_all.astype(BF16), d)
         k_last, v_last = k * last_low, v * last_low
         gden_q = gden * q.astype(F32)
         dk_den = nn(turned, gden_q.astype(BF16)) + rows_of(last, d) * after_norm[...]
         dq_den = gden * (kc_ref[at, :].astype(F32) + rows_of(seen_all, d) * norm_in)
         for p in range(4):
             cut = slice(128 * p, 128 * p + 128)
-            g, side = p // 2, 128 * (p % 2)
-            wide = slice(256 * g, 256 * g + 256)
-            edge = slice(side, side + 128)
+            held = (states[c, p].astype(F32) + carried * pairs_in[p]).astype(BF16)
+            g_after = after[p].astype(BF16)
             qp, kp, vp, gp = q[:, cut], k[:, cut], v[:, cut], gnum[:, cut]
             q2, k2 = split_pair(qp, low, high), split_pair(kp, low, high)
             v2, g2 = split_pair(vp, low, high), split_pair(gp, low, high)
             s_turned = nt(kp, q2).astype(BF16) * turned2
             gs_turned = nt(vp, g2).astype(BF16) * turned2
             gs = nt(gp, v2).astype(BF16) * allowed2
-            dq = nn(gs, k2) + nt(gnum_seen[:, wide], states[c, g, edge, :])
-            dq = dq + nt(gnum_all[:, wide], groups_in[g][edge, :]) + dq_den[:, cut]
+            dq = nn(gs, k2) + nt(gnum_seen[:, cut], held) + dq_den[:, cut]
             gq_out[at, cut] = (jnp.minimum(qp.astype(F32), 1.0) * dq).astype(BF16)
-            dk = nn(gs_turned, q2) + nt(v_last[:, wide], g_after[g][edge, :]) + dk_den[:, cut]
+            dk = nn(gs_turned, q2) + nt(v_last[:, cut], g_after) + dk_den[:, cut]
             dk_out[at, cut] = dk.astype(BF16)
-            dv = nn(s_turned, g2) + nn(k_last[:, wide], g_after[g][:, edge])
+            dv = nn(s_turned, g2) + nn(k_last[:, cut], g_after)
             dv_out[at, cut] = dv.astype(BF16)
         q_turned = (q * seen).T
-        mask = ones[...].astype(F32)
-        for g in range(2):
-            wide = slice(256 * g, 256 * g + 256)
-            after[g] = keep * after[g] + nn(q_turned[wide, :], gnum[:, wide]) * mask
+        mask = ones[0:128, 0:128].astype(F32)
+        for p in range(4):
+            cut = slice(128 * p, 128 * p + 128)
+            after[p] = keep * after[p] + nn(q_turned[cut, :], gnum[:, cut]) * mask
         after_norm[...] = keep * after_norm[...] + column_sum(gden_q * seen.astype(F32))
         return carry
 
-    lax.fori_loop(0, count, step, 0)
+    lax.fori_loop(0, count, step, 0, unroll=4)
 
 
 def last_kernel(lens, off, *refs):
-    (q_ref, k_ref, v_ref, gnum_ref, gden_ref, kc_ref, states, state_in, k_tile, v_tile, x_ref, use, grads, g_vec,
-     ones, vec, w,
-     gx_out, early_out, later_out, latest_out, vector_out,
-     gq_all, dk_all, dv_all, h1t_all, acc, after, after_norm, groups, norm, sums, src_kv, src_q, *rest) = refs
+    (q_ref, k_ref, v_ref, gnum_ref, gden_ref, kc_ref, states, state_in, x_ref, use, grads, g_vec, ones, vec, w,
+     gx_out, early_out, later_out, latest_out, final_out, vector_out,
+     gq_all, dk_all, dv_all, h1t_all, acc, after, after_norm, sums, shares, src_k, src_v, src_q, *rest) = refs
     micro = use.shape[0]
-    block_rows, d = q_ref.shape
-    rows = x_ref.shape[0]
-    tiles = block_rows // rows
-    steps = micro * tiles
+    rows, d = q_ref.shape
     n = src_q.shape[0]
     each = d // n
     running = Running(use, False, rest[:13])
     rest = rest[13:]
-    early, later, latest = Scatter(grads, rest[:14]), Scatter(src_kv, rest[14:28]), Scatter(src_q, rest[28:42])
-    vector = VectorSum(rest[42:])
+    jobs = [Scatter(src, rest[13 * j : 13 * j + 13]) for j, src in enumerate((grads, src_k, src_v, src_q))]
+    early, of_k, of_v, of_q = jobs
+    vector = VectorSum(rest[52:])
     i = pl.program_id(0)
     base = off[0]
-    p1, p2, p3, end = micro, micro + steps, micro + steps + 1, micro + 2 * steps + 1
+    p1, p2, p3, p4, end = micro, 2 * micro, 3 * micro, 3 * micro + 1, 4 * micro + 1
+
+    def at_step(step, *actions):
+        @pl.when(i == step)
+        def _():
+            for action in actions:
+                action()
 
     @pl.when(i == 0)
     def _():
@@ -1021,150 +1035,137 @@
         running.start1()
         early.start1()
         acc[...] = jnp.zeros_like(acc)
-        sums[...] = g_vec[...]
-
-    @pl.when(i == 1)
-    def _():
-        running.finish1_start2()
-        early.finish1_start2()
-
-    @pl.when(i == 2)
-    def _():
-        running.finish2_start3()
-
-    @pl.when(i == 3)
-    def _():
-        running.finish3()
-        early.finish2_start3()
+        shares[...] = jnp.zeros_like(shares)
+
+    at_step(1, running.finish1_start2, early.finish1_start2)
+    at_step(3, running.finish2_start3, early.finish2_start3)
+    at_step(p1, running.finish3)
+    at_step(p1 + 3, early.finish3_start4)
+    at_step(p2 + 1, early.finish4, of_k.finish1_start2)
+    at_step(p2 + 3, of_k.finish2_start3)
+    at_step(p4, of_k.finish3_start4)
+    at_step(p4 + 1, of_v.finish2_start3, vector.finish1_start2)
+    at_step(p4 + 2, of_k.finish4, of_q.finish2_start3)
+    at_step(p4 + 3, of_v.finish3_start4, vector.finish2_start3)
 
     @pl.when(i < p1)
     def _():
-        at = pl.ds(pl.multiple_of(i * block_rows, block_rows), block_rows)
+        at = pl.ds(pl.multiple_of(i * rows, rows), rows)
         attend_back(
             lens, i, base, q_ref, k_ref, v_ref, gnum_ref, gden_ref, kc_ref, states, state_in, ones,
             gq_all.at[at], dk_all.at[at], dv_all.at[at], after, after_norm,
         )
 
-    @pl.when(i == p1 + steps // 2)
-    def _():
-        early.finish3_start4()
-
-    @pl.when(i == p1 + steps - 2)
-    def _():
-        early.finish4_start5()
+    def block(m):
+        final = start_of(lens, m, base + rows - 1)
+        last = flag(start_of(lens, m, place_rows(base, rows)) == final)
+        groups, norm = unpack_state(running.result[m], ones[...])
+        return last, rows_of(last.astype(BF16), d), groups, norm
 
     @pl.when((i >= p1) & (i < p2))
     def _():
-        j = i - p1
-        m, t = j // tiles, lax.rem(j, tiles)
-
-        @pl.when(t == 0)
-        def _():
-            parts, z = unpack_state(running.result[m], ones[...])
-            for g in range(2):
-                groups[g] = parts[g]
-            norm[...] = z
-
-        at = pl.ds(pl.multiple_of(j * rows, rows), rows)
-        k, v = k_tile[...], v_tile[...]
-        final = start_of(lens, m, base + block_rows - 1)
-        last = flag(start_of(lens, m, place_rows(base + t * rows, rows)) == final)
-        last_low = rows_of(last.astype(BF16), d)
-        dk = dk_all[at, :].astype(F32) + rows_of(last, d) * norm[...]
-        dk = dk + by_group(lambda g, a: nt(a, groups[g]), v * last_low)
-        gk = (jnp.minimum(k.astype(F32), 1.0) * dk).astype(BF16)
+        m = i - p1
+        at = pl.ds(pl.multiple_of(m * rows, rows), rows)
+        last, last_low, groups, norm = block(m)
+        dk = dk_all[at, :].astype(F32) + rows_of(last, d) * norm
+        dk = dk + by_group(lambda g, a: nt(a, groups[g]), v_ref[...] * last_low)
+        gk = (jnp.minimum(k_ref[...].astype(F32), 1.0) * dk).astype(BF16)
         dk_all[at, :] = gk
-        gv = dv_all[at, :].astype(F32) + by_group(lambda g, a: nn(a, groups[g]), k * last_low)
-        gv = gv.astype(BF16)
-        dv_all[at, :] = gv
         xhat, _ = normed(x_ref[...].astype(F32))
         h1t = (xhat * vec[0:1, :] + vec[1:2, :]).astype(BF16).T
         h1t_all[:, at] = h1t
         acc[:, d : 2 * d] += nn(h1t, gk)
-        acc[:, 2 * d :] += nn(h1t, gv)
-
-    def arrange(src, parts):
+        shares[:, d : 2 * d] += column_sum(gk.astype(F32))
+
+    def arrange(src, part):
         for w_ in range(n):
-            for j, p in enumerate(parts):
-                put(src.at[w_], each * j, acc[each * w_ : each * w_ + each, d * p : d * p + d].astype(BF16))
-            fill(src.at[w_], each * len(parts), d)
+            put(src.at[w_], 0, acc[each * w_ : each * w_ + each, d * part : d * part + d].astype(BF16))
+            fill(src.at[w_], each, d)
 
     @pl.when(i == p2 - 1)
     def _():
-        arrange(src_kv, (1, 2))
-        later.start1()
-
-    @pl.when(i == p2)
-    def _():
-        early.finish5()
+        arrange(src_k, 1)
+        of_k.start1()
+
+    @pl.when((i >= p2) & (i < p3))
+    def _():
+        m = i - p2
+        at = pl.ds(pl.multiple_of(m * rows, rows), rows)
+        _, last_low, groups, _ = block(m)
+        gv = dv_all[at, :].astype(F32) + by_group(lambda g, a: nn(a, groups[g]), k_ref[...] * last_low)
+        gv = gv.astype(BF16)
+        dv_all[at, :] = gv
+        acc[:, 2 * d :] += nn(h1t_all[:, at], gv)
+        shares[:, 2 * d :] += column_sum(gv.astype(F32))
+
+    @pl.when(i == p3 - 1)
+    def _():
+        arrange(src_v, 2)
+        of_v.start1()
+
+    @pl.when(i == p3)
+    def _():
         early_out[...] = early.out[...]
 
         def add(m, carry):
-            at = pl.ds(pl.multiple_of(m * block_rows, block_rows), block_rows)
-            acc[:, 0:d] += nn(h1t_all[:, at], gq_all[at, :])
+            at = pl.ds(pl.multiple_of(m * rows, rows), rows)
+            gq = gq_all[at, :]
+            acc[:, 0:d] += nn(h1t_all[:, at], gq)
+            shares[:, 0:d] += column_sum(gq.astype(F32))
             return carry
 
-        lax.fori_loop(0, micro, add, 0)
-        arrange(src_q, (0,))
-        later.finish1_start2()
-        latest.start1()
-
-    @pl.when(i == p3 + 1)
-    def _():
-        latest.finish1_start2()
-
-    @pl.when(i == p3 + 3)
-    def _():
-        later.finish2_start3()
-
-    @pl.when(i == p3 + 5)
-    def _():
-        latest.finish2_start3()
-
-    @pl.when(i == end - 1)
-    def _():
-        later.finish3_start4()
-
-    @pl.when(i >= p3)
-    def _():
-        at = pl.ds(pl.multiple_of((i - p3) * rows, rows), rows)
+        lax.fori_loop(0, micro // 2, add, 0)
+        of_v.finish1_start2()
+        lax.fori_loop(micro // 2, micro, add, 0)
+        arrange(src_q, 0)
+        of_q.start1()
+        both = jnp.zeros((d, 128), F32)
+        only = jnp.zeros((d, 128), F32)
+        for j in range(3 * d // 128):
+            cut = slice(128 * j, 128 * j + 128)
+            weight = w[:, cut].astype(F32)
+            both = both + weight * acc[:, cut]
+            only = only + weight * shares[:, cut]
+        both, only = column_sum(both.T), column_sum(only.T)
+        sums[...] = g_vec[...]
+        sums[0:1, :] = (both - vec[1:2, :] * only) / vec[0:1, :]
+        sums[1:2, :] = only
+        owner_tiles(sums[...], vector.tiles, each)
+        vector.start1()
+        of_q.finish1_start2()
+
+    @pl.when(i >= p4)
+    def _():
+        at = pl.ds(pl.multiple_of((i - p4) * rows, rows), rows)
         e = nt(gq_all[at, :], w[:, 0:d]) + nt(dk_all[at, :], w[:, d : 2 * d]) + nt(dv_all[at, :], w[:, 2 * d :])
         xhat, scale = normed(x_ref[...].astype(F32))
         gx_out[...] = norm_back(e, xhat, scale, vec[0:1, :]).astype(BF16)
-        sums[0:1, :] += column_sum(e * xhat)
-        sums[1:2, :] += column_sum(e)
 
     @pl.when(i == end - 1)
     def _():
-        owner_tiles(sums[...], vector.tiles, each)
-        vector.start1()
-        latest.finish3_start4()
-        vector.finish1_start2()
-        later.finish4_start5()
-        latest.finish4_start5()
-        vector.finish2_start3()
-        later.finish5()
-        latest.finish5()
-        later_out[...] = later.out[...]
-        latest_out[...] = latest.out[...]
+        of_q.finish3_start4()
+        later_out[...] = of_k.out[...]
         vector_out[...] = vector.finish3()
+        of_v.finish4()
+        latest_out[...] = of_v.out[...]
+        of_q.finish4()
+        final_out[...] = of_q.out[...]
 
 
 def result_kernel(
-    gm_ref, part_ref, early, later, latest, vector, gx, g_qkv, g_out, g_up, g_down, v0, v1, v2, v3, v4, v5
+    gm_ref, part_ref, early, of_k, of_v, of_q, vector, gx, g_qkv, g_out, g_up, g_down, v0, v1, v2, v3, v4, v5
 ):
     gx[...] = gm_ref[...].astype(F32) + part_ref[...].astype(F32)
 
-    @pl.when((pl.program_id(0) == 0) & (pl.program_id(1) == 0))
+    @pl.when(pl.program_id(0) == 0)
     def _():
         each, d = g_out.shape
         for j in range(4):
             g_up[:, d * j : d * j + d] = get(early, each * j, each, d).astype(F32)
         g_out[...] = get(early, 4 * each, each, d).astype(F32)
         g_down[...] = get(early, 5 * each, 4 * each, d).astype(F32)
-        g_qkv[:, 0:d] = get(latest, 0, each, d).astype(F32)
-        g_qkv[:, d : 2 * d] = get(later, 0, each, d).astype(F32)
-        g_qkv[:, 2 * d :] = get(later, each, each, d).astype(F32)
+        for j, part in enumerate((of_q, of_k, of_v)):
+            g_qkv[:, d * j : d * j + d] = get(part, 0, each, d).astype(F32)
         for j, v in enumerate((v0, v1, v2, v3, v4)):
             v[...] = vector[j : j + 1, :each]
         for r in range(4):
@@ -1210,10 +1211,8 @@
     block = pl.BlockSpec((None, rows, d), lambda m: (m, 0, 0))
     count = rows // CHUNK
     states_spec = pl.BlockSpec((None, count, 2, 256, 256), lambda m: (m, 0, 0, 0, 0))
-    steps = micro * tiles
-    early = pl.BlockSpec((None, TILE, d), lambda i: (jnp.minimum(i, steps - 1) // tiles, lax.rem(jnp.minimum(i, steps - 1), tiles), 0))
-    late = lambda *shape: pl.BlockSpec(
-        (None,) + shape, lambda i: (jnp.maximum(i - steps, 0),) + (0,) * len(shape)
+    during = lambda begin, *shape: pl.BlockSpec(
+        (None,) + shape, lambda i: (jnp.clip(i - begin, 0, micro - 1),) + (0,) * len(shape)
     )
     anywhere = pl.BlockSpec(memory_space=pl.ANY)
     spread = lambda a: jax.ShapeDtypeStruct((wide,) + a.shape, BF16)
@@ -1222,23 +1221,23 @@
     state_shape = (micro, state_rows(), 128)
     (q, k, v, num, kc, states, state_in, w_qkv, w_out, w_up, w_down, vec) = pl.pallas_call(
         first_kernel,
-        grid=(steps + micro,),
-        in_specs=[small(), small(), early] + [anywhere] * 4 + [whole(a.shape) for a in vectors] + [whole((256, 256))],
-        out_specs=[early, early, early, late(rows, d), late(rows, d), late(count, 2, 256, 256), whole(state_shape)]
+        grid=(4 * micro,),
+        in_specs=[small(), small(), fixed((micro, rows, d))] + [anywhere] * 4 + [whole(a.shape) for a in vectors] + [whole((256, 256))],
+        out_specs=[during(micro * j, rows, d) for j in range(3)] + [during(3 * micro, rows, d)] * 2
+        + [during(3 * micro, count, 4, 128, 128), whole(state_shape)]
         + [anywhere] * 4 + [whole((16, d))],
         out_shape=[like(BF16)] * 5 + [
-            jax.ShapeDtypeStruct((micro, count, 2, 256, 256), BF16), jax.ShapeDtypeStruct(state_shape, F32),
+            jax.ShapeDtypeStruct((micro, count, 4, 128, 128), BF16), jax.ShapeDtypeStruct(state_shape, F32),
             spread(qkv_weight), spread(out_weight), spread(up_weight), spread(down_weight),
             jax.ShapeDtypeStruct((16, d), F32),
         ],
         scratch_shapes=[pltpu.VMEM((3, wide, each, d), BF16)]
-        + [pltpu.VMEM((micro * rows, d), BF16)] * 3
-        + [pltpu.VMEM((2, 256, 256), F32), pltpu.VMEM((1, d), F32)] * 2
+        + [pltpu.VMEM((micro, rows, d), BF16)] * 4
         + [
-            pltpu.VMEM(state_shape, BF16), pltpu.VMEM((16, 128), BF16), pltpu.VMEM((wide, 16, 128), BF16),
+            pltpu.VMEM((4, 128, 128), F32), pltpu.VMEM((1, d), F32), pltpu.VMEM(state_shape, BF16), pltpu.VMEM((16, 128), BF16), pltpu.VMEM((wide, 16, 128), BF16),
             dma, dma((wide,)), dma((wide,)), dma((3,)),
         ]
-        + running_scratch(micro)
+        + running_scratch(micro // 2) * 2
         + gather_sems() * 6,
         compiler_params=pltpu.CompilerParams(
             dimension_semantics=("arbitrary",), vmem_limit_bytes=VMEM, collective_id=0, has_side_effects=True
@@ -1276,51 +1275,52 @@
 
     spare = 2 if wide <= 8 else 1
 
-    def walk(*begins):
+    def walk(*begins, buffers=2):
         def at(i):
             j = 0
             for b in begins:
-                j = j + jnp.where(i >= b, jnp.clip(i - b, 0, steps - 1) - j, 0)
-            return (j // tiles, lax.rem(j, tiles), 0)
-
-        return pl.BlockSpec((None, TILE, d), at)
-
-    p1, p3 = micro, micro + steps + 1
-    kv_shape, q_shape = packed_shape(2 * each, d), packed_shape(each, d)
+                j = j + jnp.where(i >= b, jnp.clip(i - b, 0, micro - 1) - j, 0)
+            return (j, 0, 0)
+
+        return pl.BlockSpec((None, rows, d), at, pipeline_mode=pl.Buffered(buffers))
+
+    p1, p2, p4 = micro, 2 * micro, 3 * micro + 1
+    part_shape = packed_shape(each, d)
     vector_shapes = [(1, each)] * 5 + [(1, 4 * each)]
-    summed_shapes = [early_shape, kv_shape, q_shape, (16, 128)]
+    summed_shapes = [early_shape, part_shape, part_shape, part_shape, (16, 128)]
     result_shapes = [(each, 3 * d), (each, d), (each, ff), (4 * each, d)] + vector_shapes
     part, *summed = pl.pallas_call(
         last_kernel,
-        grid=(micro + 2 * steps + 1,),
-        in_specs=[small(), small()] + [first(rows, d, buffers=spare)] * 6 + [first(count, 2, 256, 256, buffers=1), first(state_rows(), 128)]
-        + [walk(p1)] * 2 + [walk(p1, p3)] + [anywhere] * 2
+        grid=(4 * micro + 1,),
+        in_specs=[small(), small(), first(rows, d, buffers=spare), walk(0, p1, p2, buffers=spare), walk(0, p1, buffers=spare)]
+        + [first(rows, d, buffers=spare)] * 3 + [first(count, 4, 128, 128, buffers=spare), first(state_rows(), 128)]
+        + [walk(p1, p4)] + [anywhere] * 2
         + [whole((16, d)), whole((256, 256)), whole((16, d)), fixed((d, 3 * d))],
-        out_specs=[walk(p3)] + [fixed(s) for s in summed_shapes],
-        out_shape=[like(BF16)] + [jax.ShapeDtypeStruct(s, BF16) for s in summed_shapes[:3]]
+        out_specs=[walk(p4)] + [fixed(s) for s in summed_shapes],
+        out_shape=[like(BF16)] + [jax.ShapeDtypeStruct(s, BF16) for s in summed_shapes[:4]]
         + [jax.ShapeDtypeStruct((16, 128), F32)],
         scratch_shapes=[pltpu.VMEM((micro * rows, d), BF16)] * 3
         + [
             pltpu.VMEM((d, micro * rows), BF16), pltpu.VMEM((d, 3 * d), F32),
-            pltpu.VMEM((2, 256, 256), F32), pltpu.VMEM((1, d), F32),
-            pltpu.VMEM((2, 256, 256), BF16), pltpu.VMEM((1, d), F32), pltpu.VMEM((16, d), F32),
-            pltpu.VMEM((wide,) + kv_shape, BF16), pltpu.VMEM((wide,) + q_shape, BF16),
+            pltpu.VMEM((4, 128, 128), F32), pltpu.VMEM((1, d), F32),
+            pltpu.VMEM((16, d), F32), pltpu.VMEM((1, 3 * d), F32),
         ]
+        + [pltpu.VMEM((wide,) + part_shape, BF16)] * 3
         + running_scratch(micro)
-        + scatter_scratch(early_shape) + scatter_scratch(kv_shape) + scatter_scratch(q_shape)
+        + scatter_scratch(early_shape) + scatter_scratch(part_shape) * 3
         + vector_scratch(),
         compiler_params=pltpu.CompilerParams(
             dimension_semantics=("arbitrary",), vmem_limit_bytes=VMEM, collective_id=1, has_side_effects=True
         ),
         name="last",
-    )(lens, off, q, k, v, gnum, gden, kc, states, state_in, k, v, x, use, grads, g_vec, ones, vec, w_qkv)
+    )(lens, off, q, k, v, gnum, gden, kc, states, state_in, x, use, grads, g_vec, ones, vec, w_qkv)
     grad_input, g_qkv, g_out, g_up, g_down, *g_vectors = pl.pallas_call(
         result_kernel,
-        grid=(micro, tiles),
-        in_specs=[token, token] + [whole(s) for s in summed_shapes],
-        out_specs=[token] + [whole(s) for s in result_shapes],
+        grid=(micro,),
+        in_specs=[block, block] + [whole(s) for s in summed_shapes],
+        out_specs=[block] + [whole(s) for s in result_shapes],
         out_shape=[like(F32)] + [jax.ShapeDtypeStruct(s, F32) for s in result_shapes],
-        compiler_params=params(2),
+        compiler_params=params(1),
         name="result",
     )(g_middle, part, *summed)
     piece = [a.reshape(-1) for a in g_vectors]

time: 321 us -> 282 us (0.88)
  Pallas kernels: 318 us -> 279 us
    pallas_call x3, Pallas kernels: 215 us -> 188 us  [the longest x1 110 us: per_device(): pl.pallas_call(last_kernel, grid=(4 * micro + 1,), in_specs=[small(), sma...]
    pallas_call x1, Pallas kernels: 103 us -> 91.6 us  [per_device(): pl.pallas_call(middle_kernel, grid=(micro, tiles), in_specs=[small(), sma...]
where the time goes in v3:
time: 282 us
  Pallas kernels  279 us (99%)
    pallas_call x1, Pallas kernels, per_device(): pl.pallas_call(last_kernel, grid=(4 * micro + 1,), in_specs=[small(), sma...  110 us
    pallas_call x1, Pallas kernels, per_device(): pl.pallas_call(middle_kernel, grid=(micro, tiles), in_specs=[small(), sma...  91.6 us
    pallas_call x1, Pallas kernels, per_device(): pl.pallas_call(first_kernel, grid=(4 * micro,), in_specs=[small(), small(...  69.9 us
    pallas_call x1, Pallas kernels, per_device(): pl.pallas_call(result_kernel, grid=(micro,), in_specs=[block, block] + [w...  7.97 us

profile of v3, /device:TPU:0, one launch (start us, length us, event | category | flops | bytes accessed | tf_op | source)
XLA Modules:
  0.0 282.1 jit_solution(12140031579386762245)
XLA Ops:
  0.6 1.2 reshape.124.refs_9_
  1.9 0.8 compare_convert_fusion.refs_10_.ones.refs_12_
  2.6 69.9 %first.1 = (bf16[4,1024,512]{2,1,0:T(8,128)(2,1)}, bf16[4,1024,512]{2,1,0:T(8,128)(2,1)}, bf16[4,1024,512]{2,1,0:T(8,128)(2,1)}, bf16[4,1024,512]{2,1,0:T(8,128)...) custom-call(s32[4,8]{1,0:T(4,128)} %bitcast.33, ...), custom_call_target="tpu_custom_call" | custom-call | tf_op jit(solution)/shard_map/first/pallas_call | solution.py:1222
  72.5 91.6 %middle.1 = (bf16[4,1024,512]{2,1,0:T(8,128)(2,1)}, bf16[4,1024,512]{2,1,0:T(8,128)(2,1)}, bf16[4,1024,512]{2,1,0:T(8,128)(2,1)}, bf16[4,1024,512]{2,1,0:T(8,128...) custom-call(s32[4,8]{1,0:T(4,128)} %bitcast.34, s32[1]{0:T(128)} %bitcast.1.off, ...), custom_call_target="tpu_custom_call" | custom-call | tf_op jit(solution)/shard_map/middle/pallas_call | solution.py:1250
  164.1 109.8 %last.1 = (bf16[4,1024,512]{2,1,0:T(8,128)(2,1)}, bf16[576,512]{1,0:T(8,128)(2,1)}, bf16[64,512]{1,0:T(8,128)(2,1)}, bf16[64,512]{1,0:T(8,128)(2,1)}, bf16[64,512]{1,0:T(8,128)(2,1)}, /*index=5*/f32[16,128]{1,0:T(8,128)}) custom-call(s32[4,8]{1,0:T(4,128)} %bitcast.35, s32[1]{0:T(128)} %bitcast.1.off, bf16[4,1024,512]{2,1,0:T(8,128)(2,1)} %get-tuple-element.48.q_ref.refs_0_, ...), custom_call_target="tpu_custom_call" | custom-call | tf_op jit(solution)/shard_map/last/pallas_call | solution.py:1292
  273.9 8.0 %result.1 = (f32[4,1024,512]{2,1,0:T(8,128)}, f32[64,1536]{1,0:T(8,128)}, f32[64,512]{1,0:T(8,128)}, f32[64,2048]{1,0:T(8,128)}, f32[256,512]{1,0:T(8,128)}, /*i...) custom-call(bf16[4,1024,512]{2,1,0:T(8,128)(2,1)} %get-tuple-element, ...), custom_call_target="tpu_custom_call" | custom-call | tf_op jit(solution)/shard_map/result/pallas_call | solution.py:1317
  (1 shorter events, 0.0 us)

commit v4 on v3

--- a/solution.py
+++ b/solution.py
@@ -139,7 +139,7 @@
     )
 
 
-def greet():
+def signal_all():
     core, y, me, ny, n = place()
     dp = 2 * y + core
     barrier = pltpu.get_barrier_semaphore()
@@ -149,7 +149,11 @@
 
     others(n, lambda o: signal(dp, lax.rem(me + o, n)))
     others(2 * ny, lambda o: signal(lax.rem(dp + o, 2 * ny), me))
-    pl.semaphore_wait(barrier, n - 1 + 2 * ny - 1)
+
+
+def wait_all():
+    _, _, _, ny, n = place()
+    pl.semaphore_wait(pltpu.get_barrier_semaphore(), n - 1 + 2 * ny - 1)
 
 
 class Gather:
@@ -622,7 +626,11 @@
     jobs = []
     for j in range(3):
         jobs.append(Gather(s_qkv.at[:, d * j : d * j + d], w_ref.at[j], rest[7 * j : 7 * j + 7]))
-    for j, (src, dst) in enumerate(((s_out, w_out), (s_up, w_up), (s_down, w_down))):
+    pieces = [(s_out, w_out)]
+    for src, dst in ((s_up, w_up), (s_down, w_down)):
+        columns = src.shape[1] // 2
+        pieces += [(src.at[:, c : c + columns], dst.at[:, :, c : c + columns]) for c in (0, columns)]
+    for j, (src, dst) in enumerate(pieces):
         jobs.append(Gather(src, dst, rest[21 + 7 * j : 28 + 7 * j]))
     i = pl.program_id(0)
     core, y, me, ny, n = place()
@@ -644,8 +652,9 @@
 
     @pl.when(i == 0)
     def _():
+        signal_all()
         tile[...] = vector_tile((v0, v1, v2, v3, v4, v5), each)
-        greet()
+        wait_all()
         vec_near().start()
         others(n, lambda o: vec_copy(o).start())
         for job in jobs[:3]:
@@ -725,36 +734,50 @@
     def _():
         running[0].start1()
 
-    @pl.when(i == 2 * micro + half)
-    def _():
-        for job in jobs[3:5]:
-            job.finish_wide()
-            job.start_y()
-
     @pl.when(i == 3 * micro - 1)
     def _():
         running[1].start1()
 
+    def pass_on(step, *parts):
+        @pl.when(i == step)
+        def _():
+            for job in parts:
+                job.finish_wide()
+                job.start_y()
+
+    def cross_over(step, *parts):
+        @pl.when(i == step)
+        def _():
+            for job in parts:
+                job.finish_y()
+                job.start_core()
+
+    pass_on(micro + 1, jobs[3], jobs[4])
+    pass_on(2 * micro + 1, jobs[5])
+    pass_on(3 * micro, jobs[6])
+
     @pl.when(i == 3 * micro)
     def _():
         running[0].finish1_start2()
 
+    cross_over(3 * micro, jobs[3], jobs[4])
+    pass_on(3 * micro + 1, jobs[7])
+
     @pl.when(i == 3 * micro + 1)
     def _():
         running[1].finish1_start2()
-        jobs[5].finish_wide()
-        jobs[5].start_y()
+
+    cross_over(3 * micro + 2, jobs[5], jobs[6])
 
     @pl.when(i == 3 * micro + 2)
     def _():
         running[0].finish2_start3()
-        for job in jobs[3:5]:
-            job.finish_y()
-            job.start_core()
 
     @pl.when(i == 3 * micro + 3)
     def _():
         running[1].finish2_start3()
+
+    cross_over(3 * micro + 3, jobs[7])
 
     @pl.when(i >= 3 * micro)
     def _():
@@ -763,8 +786,6 @@
 
     @pl.when(i == 4 * micro - 1)
     def _():
-        jobs[5].finish_y()
-        jobs[5].start_core()
         for j in range(2):
             running[j].finish3()
             state_in[half * j : half * j + half] = running[j].result[...]
@@ -836,7 +857,7 @@
 def middle_kernel(
     lens, off, q_ref, num_ref, kc_ref, x_ref, cot_ref, state_in, ones,
     w_out, vec, w_up, w_down,
-    block_out, gm_out, gnum_out, gden_out, use_out, grads, g_vec,
+    block_out, gm_out, gnum_out, gden_out, use_out, grads_up, grads_down, g_vec,
     groups, norm, use, use_norm, acc_out, acc_up, acc_down, total, e_total, h2_ref, h2t_ref, ct_ref,
 ):
     m, t, tiles = pl.program_id(0), pl.program_id(1), pl.num_programs(1)
@@ -927,28 +948,26 @@
 
     @pl.when(final)
     def _():
-        n = grads.shape[0]
+        n = grads_up.shape[0]
         each = d // n
         down = acc_down[...].astype(BF16).T
         for w in range(n):
             at = slice(each * w, each * w + each)
-            block = grads.at[w]
             for j in range(4):
-                put(block, each * j, acc_up[at, d * j : d * j + d].astype(BF16))
-            put(block, 4 * each, acc_out[at, :].astype(BF16))
-            put(block, 5 * each, down[4 * each * w : 4 * each * w + 4 * each, :])
-            fill(block, 9 * each, d)
+                put(grads_up.at[w], each * j, acc_up[at, d * j : d * j + d].astype(BF16))
+            put(grads_up.at[w], 4 * each, acc_out[at, :].astype(BF16))
+            fill(grads_up.at[w], 5 * each, d)
+            put(grads_down.at[w], 0, down[4 * each * w : 4 * each * w + 4 * each, :])
+            fill(grads_down.at[w], 4 * each, d)
 
 
 def attend_back(
-    lens, m, base, q_ref, k_ref, v_ref, gnum_ref, gden_ref, kc_ref, states, state_in, ones,
+    lens, m, base, lead, q_ref, k_ref, v_ref, gnum_ref, gden_ref, kc_ref, states, state_in, ones,
     gq_out, dk_out, dv_out, after, after_norm,
 ):
     rows, d = q_ref.shape
     size = CHUNK
     count = rows // size
-    after[...] = jnp.zeros_like(after)
-    after_norm[...] = jnp.zeros_like(after_norm)
     half = lane_half((1, 128))
     low = flag(half).astype(BF16)
     high = flag(jnp.logical_not(half)).astype(BF16)
@@ -957,7 +976,7 @@
     def step(i, carry):
         c = count - 1 - i
         at = pl.ds(pl.multiple_of(c * size, size), size)
-        begin = base + c * size
+        begin = lead + c * size
         q, k, v, gnum = q_ref[at, :], k_ref[at, :], v_ref[at, :], gnum_ref[at, :]
         gden = gden_ref[at, :].astype(F32)
         by_row, by_column, final = chunk_masks(lens, m, begin, size)
@@ -973,7 +992,7 @@
         last = flag(by_row == final)
         keep = jnp.where(final < begin, 1.0, 0.0)
         last_low = rows_of(last.astype(BF16), d)
-        carried = jnp.where((c == 0) | (start_of(lens, m, begin - 1) < base), 1.0, 0.0)
+        carried = jnp.where((begin == base) | (start_of(lens, m, begin - 1) < base), 1.0, 0.0)
         gnum_seen = gnum * seen
         k_last, v_last = k * last_low, v * last_low
         gden_q = gden * q.astype(F32)
@@ -1007,21 +1026,28 @@
 
 
 def last_kernel(lens, off, *refs):
-    (q_ref, k_ref, v_ref, gnum_ref, gden_ref, kc_ref, states, state_in, x_ref, use, grads, g_vec, ones, vec, w,
-     gx_out, early_out, later_out, latest_out, final_out, vector_out,
+    (q_ref, k_half, v_half, gnum_ref, gden_ref, kc_ref, states, state_in, k_ref, v_ref, x_ref,
+     use, grads_up, grads_down, g_vec, ones, vec, w,
+     gx_out, up_out, down_out, k_out, v_out, q_out, vector_out,
      gq_all, dk_all, dv_all, h1t_all, acc, after, after_norm, sums, shares, src_k, src_v, src_q, *rest) = refs
     micro = use.shape[0]
-    rows, d = q_ref.shape
+    rows, d = k_ref.shape
+    part_rows = q_ref.shape[0]
+    halves = rows // part_rows
     n = src_q.shape[0]
     each = d // n
     running = Running(use, False, rest[:13])
     rest = rest[13:]
-    jobs = [Scatter(src, rest[13 * j : 13 * j + 13]) for j, src in enumerate((grads, src_k, src_v, src_q))]
-    early, of_k, of_v, of_q = jobs
-    vector = VectorSum(rest[52:])
+    jobs = [
+        Scatter(src, rest[13 * j : 13 * j + 13]) for j, src in enumerate((grads_up, grads_down, src_k, src_v, src_q))
+    ]
+    of_up, of_down, of_k, of_v, of_q = jobs
+    vector = VectorSum(rest[65:])
     i = pl.program_id(0)
     base = off[0]
-    p1, p2, p3, p4, end = micro, 2 * micro, 3 * micro, 3 * micro + 1, 4 * micro + 1
+    p1 = halves * micro
+    p2, p3 = p1 + micro, p1 + 2 * micro
+    p4, end = p3 + 1, p3 + 1 + micro
 
     def at_step(step, *actions):
         @pl.when(i == step)
@@ -1031,28 +1057,39 @@
 
     @pl.when(i == 0)
     def _():
-        greet()
+        signal_all()
+        wait_all()
+        of_up.start1()
+        of_down.start1()
         running.start1()
-        early.start1()
         acc[...] = jnp.zeros_like(acc)
         shares[...] = jnp.zeros_like(shares)
 
-    at_step(1, running.finish1_start2, early.finish1_start2)
-    at_step(3, running.finish2_start3, early.finish2_start3)
-    at_step(p1, running.finish3)
-    at_step(p1 + 3, early.finish3_start4)
-    at_step(p2 + 1, early.finish4, of_k.finish1_start2)
-    at_step(p2 + 3, of_k.finish2_start3)
-    at_step(p4, of_k.finish3_start4)
-    at_step(p4 + 1, of_v.finish2_start3, vector.finish1_start2)
-    at_step(p4 + 2, of_k.finish4, of_q.finish2_start3)
-    at_step(p4 + 3, of_v.finish3_start4, vector.finish2_start3)
+    at_step(1, of_up.finish1_start2, of_down.finish1_start2)
+    at_step(2, running.finish1_start2)
+    at_step(p1 - 2, of_up.finish2_start3)
+    at_step(p1 - 1, running.finish2_start3)
+    at_step(p1, running.finish3, of_down.finish2_start3)
+    at_step(p1 + 3, of_up.finish3_start4)
+    at_step(p2 + 1, of_up.finish4, of_k.finish1_start2)
+    at_step(p4, of_down.finish3_start4)
+    at_step(p4 + 1, of_k.finish3_start4, of_v.finish2_start3, vector.finish1_start2)
+    at_step(p4 + 2, of_down.finish4, of_q.finish2_start3)
+    at_step(p4 + 3, of_k.finish4, vector.finish2_start3)
 
     @pl.when(i < p1)
     def _():
-        at = pl.ds(pl.multiple_of(i * rows, rows), rows)
+        m, t = i // halves, halves - 1 - lax.rem(i, halves)
+
+        @pl.when(t == halves - 1)
+        def _():
+            after[...] = jnp.zeros_like(after)
+            after_norm[...] = jnp.zeros_like(after_norm)
+
+        lead = t * part_rows
+        at = pl.ds(pl.multiple_of(m * rows + lead, part_rows), part_rows)
         attend_back(
-            lens, i, base, q_ref, k_ref, v_ref, gnum_ref, gden_ref, kc_ref, states, state_in, ones,
+            lens, m, base, base + lead, q_ref, k_half, v_half, gnum_ref, gden_ref, kc_ref, states, state_in, ones,
             gq_all.at[at], dk_all.at[at], dv_all.at[at], after, after_norm,
         )
 
@@ -1105,7 +1142,7 @@
 
     @pl.when(i == p3)
     def _():
-        early_out[...] = early.out[...]
+        up_out[...] = of_up.out[...]
 
         def add(m, carry):
             at = pl.ds(pl.multiple_of(m * rows, rows), rows)
@@ -1115,6 +1152,7 @@
             return carry
 
         lax.fori_loop(0, micro // 2, add, 0)
+        of_k.finish2_start3()
         of_v.finish1_start2()
         lax.fori_loop(micro // 2, micro, add, 0)
         arrange(src_q, 0)
@@ -1143,17 +1181,19 @@
 
     @pl.when(i == end - 1)
     def _():
+        of_v.finish3_start4()
         of_q.finish3_start4()
-        later_out[...] = of_k.out[...]
+        down_out[...] = of_down.out[...]
+        k_out[...] = of_k.out[...]
         vector_out[...] = vector.finish3()
         of_v.finish4()
-        latest_out[...] = of_v.out[...]
+        v_out[...] = of_v.out[...]
         of_q.finish4()
-        final_out[...] = of_q.out[...]
+        q_out[...] = of_q.out[...]
 
 
 def result_kernel(
-    gm_ref, part_ref, early, of_k, of_v, of_q, vector, gx, g_qkv, g_out, g_up, g_down, v0, v1, v2, v3, v4, v5
+    gm_ref, part_ref, of_up, of_down, of_k, of_v, of_q, vector, gx, g_qkv, g_out, g_up, g_down, v0, v1, v2, v3, v4, v5
 ):
     gx[...] = gm_ref[...].astype(F32) + part_ref[...].astype(F32)
 
@@ -1161,9 +1201,9 @@
     def _():
         each, d = g_out.shape
         for j in range(4):
-            g_up[:, d * j : d * j + d] = get(early, each * j, each, d).astype(F32)
-        g_out[...] = get(early, 4 * each, each, d).astype(F32)
-        g_down[...] = get(early, 5 * each, 4 * each, d).astype(F32)
+            g_up[:, d * j : d * j + d] = get(of_up, each * j, each, d).astype(F32)
+        g_out[...] = get(of_up, 4 * each, each, d).astype(F32)
+        g_down[...] = get(of_down, 0, 4 * each, d).astype(F32)
         for j, part in enumerate((of_q, of_k, of_v)):
             g_qkv[:, d * j : d * j + d] = get(part, 0, each, d).astype(F32)
         for j, v in enumerate((v0, v1, v2, v3, v4)):
@@ -1206,7 +1246,7 @@
     )
     packed = pl.BlockSpec((None, state_rows(), 128), lambda m, *_: (m, 0, 0))
     like = lambda dtype: jax.ShapeDtypeStruct((micro, rows, d), dtype)
-    early_shape = packed_shape(9 * each, d)
+    up_shape, down_shape = packed_shape(5 * each, d), packed_shape(4 * each, d)
 
     block = pl.BlockSpec((None, rows, d), lambda m: (m, 0, 0))
     count = rows // CHUNK
@@ -1238,7 +1278,7 @@
             dma, dma((wide,)), dma((wide,)), dma((3,)),
         ]
         + running_scratch(micro // 2) * 2
-        + gather_sems() * 6,
+        + gather_sems() * 8,
         compiler_params=pltpu.CompilerParams(
             dimension_semantics=("arbitrary",), vmem_limit_bytes=VMEM, collective_id=0, has_side_effects=True
         ),
@@ -1247,16 +1287,17 @@
     w_qkv, w_out = w_qkv.reshape(d, 3 * d), w_out.reshape(d, d)
     w_up, w_down = w_up.reshape(d, ff), w_down.reshape(ff, d)
 
-    result, g_middle, gnum, gden, use, grads, g_vec = pl.pallas_call(
+    result, g_middle, gnum, gden, use, grads_up, grads_down, g_vec = pl.pallas_call(
         middle_kernel,
         grid=(micro, tiles),
         in_specs=[small(), small()] + [token] * 5 + [packed, whole((256, 256))] + [
             fixed((d, d)), whole((16, d)), fixed((d, ff)), fixed((ff, d)),
         ],
-        out_specs=[token, token, token, token, packed, fixed((wide,) + early_shape), whole((16, d))],
+        out_specs=[token, token, token, token, packed, fixed((wide,) + up_shape), fixed((wide,) + down_shape), whole((16, d))],
         out_shape=[
             like(BF16), like(BF16), like(BF16), like(BF16), jax.ShapeDtypeStruct(state_shape, BF16),
-            jax.ShapeDtypeStruct((wide,) + early_shape, BF16), jax.ShapeDtypeStruct((16, d), F32),
+            jax.ShapeDtypeStruct((wide,) + up_shape, BF16), jax.ShapeDtypeStruct((wide,) + down_shape, BF16),
+            jax.ShapeDtypeStruct((16, d), F32),
         ],
         scratch_shapes=[
             pltpu.VMEM((2, 256, 256), BF16), pltpu.VMEM((1, d), F32),
@@ -1269,11 +1310,17 @@
         name="middle",
     )(lens, off, q, num, kc, x, cot, state_in, ones, w_out, vec, w_up, w_down)
 
-    def first(*shape, buffers=2):
-        at = lambda i: (jnp.minimum(i, micro - 1),) + (0,) * len(shape)
-        return pl.BlockSpec((None,) + shape, at, pipeline_mode=pl.Buffered(buffers))
-
     spare = 2 if wide <= 8 else 1
+    halves = rows // TILE
+    p1 = halves * micro
+    p2, p4 = p1 + micro, p1 + 2 * micro + 1
+
+    def backward(*shape):
+        def at(i):
+            i = jnp.minimum(i, p1 - 1)
+            return (i // halves, halves - 1 - lax.rem(i, halves)) + (0,) * (len(shape) - 1)
+
+        return pl.BlockSpec((None,) + shape, at)
 
     def walk(*begins, buffers=2):
         def at(i):
@@ -1284,20 +1331,19 @@
 
         return pl.BlockSpec((None, rows, d), at, pipeline_mode=pl.Buffered(buffers))
 
-    p1, p2, p4 = micro, 2 * micro, 3 * micro + 1
     part_shape = packed_shape(each, d)
     vector_shapes = [(1, each)] * 5 + [(1, 4 * each)]
-    summed_shapes = [early_shape, part_shape, part_shape, part_shape, (16, 128)]
+    summed_shapes = [up_shape, down_shape, part_shape, part_shape, part_shape, (16, 128)]
     result_shapes = [(each, 3 * d), (each, d), (each, ff), (4 * each, d)] + vector_shapes
     part, *summed = pl.pallas_call(
         last_kernel,
-        grid=(4 * micro + 1,),
-        in_specs=[small(), small(), first(rows, d, buffers=spare), walk(0, p1, p2, buffers=spare), walk(0, p1, buffers=spare)]
-        + [first(rows, d, buffers=spare)] * 3 + [first(count, 4, 128, 128, buffers=spare), first(state_rows(), 128)]
-        + [walk(p1, p4)] + [anywhere] * 2
+        grid=(p4 + micro,),
+        in_specs=[small(), small()] + [backward(TILE, d)] * 6 + [backward(count // halves, 4, 128, 128)]
+        + [pl.BlockSpec((None, state_rows(), 128), lambda i: (jnp.minimum(i // halves, micro - 1), 0, 0))]
+        + [walk(p1, p2, buffers=spare), walk(p1, buffers=spare), walk(p1, p4, buffers=spare)] + [anywhere] * 3
         + [whole((16, d)), whole((256, 256)), whole((16, d)), fixed((d, 3 * d))],
         out_specs=[walk(p4)] + [fixed(s) for s in summed_shapes],
-        out_shape=[like(BF16)] + [jax.ShapeDtypeStruct(s, BF16) for s in summed_shapes[:4]]
+        out_shape=[like(BF16)] + [jax.ShapeDtypeStruct(s, BF16) for s in summed_shapes[:5]]
         + [jax.ShapeDtypeStruct((16, 128), F32)],
         scratch_shapes=[pltpu.VMEM((micro * rows, d), BF16)] * 3
         + [
@@ -1307,13 +1353,13 @@
         ]
         + [pltpu.VMEM((wide,) + part_shape, BF16)] * 3
         + running_scratch(micro)
-        + scatter_scratch(early_shape) + scatter_scratch(part_shape) * 3
+        + scatter_scratch(up_shape) + scatter_scratch(down_shape) + scatter_scratch(part_shape) * 3
         + vector_scratch(),
         compiler_params=pltpu.CompilerParams(
             dimension_semantics=("arbitrary",), vmem_limit_bytes=VMEM, collective_id=1, has_side_effects=True
         ),
         name="last",
-    )(lens, off, q, k, v, gnum, gden, kc, states, state_in, x, use, grads, g_vec, ones, vec, w_qkv)
+    )(lens, off, q, k, v, gnum, gden, kc, states, state_in, k, v, x, use, grads_up, grads_down, g_vec, ones, vec, w_qkv)
     grad_input, g_qkv, g_out, g_up, g_down, *g_vectors = pl.pallas_call(
         result_kernel,
         grid=(micro,),

time: 282 us -> 264 us (0.936)
  Pallas kernels: 279 us -> 261 us
    pallas_call x1, Pallas kernels: 110 us -> 95.8 us  [per_device(): pl.pallas_call(last_kernel, grid=(p4 + micro,), in_specs=[small(), small(...]
    pallas_call x1, Pallas kernels: 69.9 us -> 65.9 us  [per_device(): pl.pallas_call(first_kernel, grid=(4 * micro,), in_specs=[small(), small(...]
where the time goes in v4:
time: 264 us
  Pallas kernels  261 us (99%)
    pallas_call x1, Pallas kernels, per_device(): pl.pallas_call(last_kernel, grid=(p4 + micro,), in_specs=[small(), small(...  95.8 us
    pallas_call x1, Pallas kernels, per_device(): pl.pallas_call(middle_kernel, grid=(micro, tiles), in_specs=[small(), sma...  91.6 us
    pallas_call x1, Pallas kernels, per_device(): pl.pallas_call(first_kernel, grid=(4 * micro,), in_specs=[small(), small(...  65.9 us
    pallas_call x1, Pallas kernels, per_device(): pl.pallas_call(result_kernel, grid=(micro,), in_specs=[block, block] + [w...  7.95 us

profile of v4, /device:TPU:0, one launch (start us, length us, event | category | flops | bytes accessed | tf_op | source)
XLA Modules:
  0.0 264.1 jit_solution(9053650432984694785)
XLA Ops:
  0.6 1.2 reshape.124.refs_9_
  1.9 0.8 compare_convert_fusion.refs_10_.ones.refs_15_
  2.6 65.9 %first.1 = (bf16[4,1024,512]{2,1,0:T(8,128)(2,1)}, bf16[4,1024,512]{2,1,0:T(8,128)(2,1)}, bf16[4,1024,512]{2,1,0:T(8,128)(2,1)}, bf16[4,1024,512]{2,1,0:T(8,128)...) custom-call(s32[4,8]{1,0:T(4,128)} %bitcast.33, ...), custom_call_target="tpu_custom_call" | custom-call | tf_op jit(solution)/shard_map/first/pallas_call | solution.py:1262
  68.6 91.6 %middle.1 = (bf16[4,1024,512]{2,1,0:T(8,128)(2,1)}, bf16[4,1024,512]{2,1,0:T(8,128)(2,1)}, bf16[4,1024,512]{2,1,0:T(8,128)(2,1)}, bf16[4,1024,512]{2,1,0:T(8,128...) custom-call(s32[4,8]{1,0:T(4,128)} %bitcast.34, ...), custom_call_target="tpu_custom_call" | custom-call | tf_op jit(solution)/shard_map/middle/pallas_call | solution.py:1290
  160.2 95.8 %last.1 = (bf16[4,1024,512]{2,1,0:T(8,128)(2,1)}, bf16[320,512]{1,0:T(8,128)(2,1)}, bf16[256,512]{1,0:T(8,128)(2,1)}, bf16[64,512]{1,0:T(8,128)(2,1)}, bf16[64,5...) custom-call(s32[4,8]{1,0:T(4,128)} %bitcast.35, s32[1]{0:T(128)} %bitcast.1.off, ...), custom_call_target="tpu_custom_call" | custom-call | tf_op jit(solution)/shard_map/last/pallas_call | solution.py:1338
  256.0 8.0 %result.1 = (f32[4,1024,512]{2,1,0:T(8,128)}, f32[64,1536]{1,0:T(8,128)}, f32[64,512]{1,0:T(8,128)}, f32[64,2048]{1,0:T(8,128)}, f32[256,512]{1,0:T(8,128)}, /*i...) custom-call(bf16[4,1024,512]{2,1,0:T(8,128)(2,1)} %get-tuple-element, ...), custom_call_target="tpu_custom_call" | custom-call | tf_op jit(solution)/shard_map/result/pallas_call | solution.py:1363
  (1 shorter events, 0.0 us)

commit v5 on v4

--- a/solution.py
+++ b/solution.py
@@ -801,10 +801,6 @@
     by_column = start_of(lens, m, lane)[0:1, :]
     final = start_of(lens, m, begin + size - 1)
     return by_row, by_column, final
-
-
-def pair_mask():
-    return flag(lane_half((16, 128))).astype(BF16)[0:1, :]
 
 
 def split_pair(a, low, high):
@@ -872,6 +868,7 @@
         acc_up[...] = jnp.zeros_like(acc_up)
         acc_down[...] = jnp.zeros_like(acc_down)
         g_vec[...] = jnp.zeros_like(g_vec)
+        h2t_ref[d:, :] = jnp.ones((16, rows), BF16)
 
     @pl.when(t == 0)
     def _():
@@ -895,7 +892,7 @@
     xhat, scale = normed(middle)
     h2 = (xhat * gain + bias).astype(BF16)
     h2_ref[...] = h2
-    h2t_ref[...] = h2.T
+    h2t_ref[0:d, :] = h2.T
     ct_ref[...] = cot_ref[...].T
     total[...] = middle + down_bias
     e_total[...] = jnp.zeros_like(e_total)
@@ -909,14 +906,12 @@
         th = jnp.tanh(hidden * (c0 + (c0 * c1) * square))
         half_up = 0.5 + 0.5 * th
         active = (hidden * half_up).astype(BF16)
-        slope = half_up + (0.5 * hidden) * (1.0 - th * th) * (c0 + (3.0 * c0 * c1) * square)
-        g_hidden = slope * pulled
-        g_low = g_hidden.astype(BF16)
+        slope = half_up + hidden * (1.0 - th * th) * (0.5 * c0 + (1.5 * c0 * c1) * square)
+        g_low = (slope * pulled).astype(BF16)
         total[...] += nn(active, w_down[cut, :])
         e_total[...] += nt(g_low, w_up[:, cut])
         acc_down[:, cut] += nn(ct_ref[...], active)
         acc_up[:, cut] += nn(h2t_ref[...], g_low)
-        g_vec[pl.ds(5 + f, 1), :] += column_sum(g_hidden)
         return carry
 
     lax.fori_loop(0, w_up.shape[1] // FF_TILE, ffn, 0, unroll=True)
@@ -948,6 +943,8 @@
 
     @pl.when(final)
     def _():
+        for j in range(4):
+            g_vec[5 + j : 6 + j, :] = acc_up[d : d + 1, d * j : d * j + d]
         n = grads_up.shape[0]
         each = d // n
         down = acc_down[...].astype(BF16).T
@@ -1058,15 +1055,12 @@
     @pl.when(i == 0)
     def _():
         signal_all()
-        wait_all()
-        of_up.start1()
-        of_down.start1()
-        running.start1()
         acc[...] = jnp.zeros_like(acc)
         shares[...] = jnp.zeros_like(shares)
 
-    at_step(1, of_up.finish1_start2, of_down.finish1_start2)
-    at_step(2, running.finish1_start2)
+    at_step(1, wait_all, of_up.start1, of_down.start1, running.start1)
+    at_step(2, of_up.finish1_start2, of_down.finish1_start2)
+    at_step(3, running.finish1_start2)
     at_step(p1 - 2, of_up.finish2_start3)
     at_step(p1 - 1, running.finish2_start3)
     at_step(p1, running.finish3, of_down.finish2_start3)
@@ -1302,9 +1296,9 @@
         scratch_shapes=[
             pltpu.VMEM((2, 256, 256), BF16), pltpu.VMEM((1, d), F32),
             pltpu.VMEM((2, 256, 256), F32), pltpu.VMEM((1, d), F32),
-            pltpu.VMEM((d, d), F32), pltpu.VMEM((d, ff), F32), pltpu.VMEM((d, ff), F32),
+            pltpu.VMEM((d, d), F32), pltpu.VMEM((d + 16, ff), F32), pltpu.VMEM((d, ff), F32),
             pltpu.VMEM((TILE, d), F32), pltpu.VMEM((TILE, d), F32), pltpu.VMEM((TILE, d), BF16),
-            pltpu.VMEM((d, TILE), BF16), pltpu.VMEM((d, TILE), BF16),
+            pltpu.VMEM((d + 16, TILE), BF16), pltpu.VMEM((d, TILE), BF16),
         ],
         compiler_params=params(2),
         name="middle",

time: 264 us -> 260 us (0.985)
  Pallas kernels: 261 us -> 257 us
    pallas_call x1, Pallas kernels: 95.8 us -> 93.1 us  [per_device(): pl.pallas_call(last_kernel, grid=(p4 + micro,), in_specs=[small(), small(...]
where the time goes in v5:
time: 260 us
  Pallas kernels  257 us (99%)
    pallas_call x1, Pallas kernels, per_device(): pl.pallas_call(last_kernel, grid=(p4 + micro,), in_specs=[small(), small(...  93.1 us
    pallas_call x1, Pallas kernels, per_device(): pl.pallas_call(middle_kernel, grid=(micro, tiles), in_specs=[small(), sma...  89.8 us
    pallas_call x1, Pallas kernels, per_device(): pl.pallas_call(first_kernel, grid=(4 * micro,), in_specs=[small(), small(...  65.9 us
    pallas_call x1, Pallas kernels, per_device(): pl.pallas_call(result_kernel, grid=(micro,), in_specs=[block, block] + [w...  7.95 us

profile of v5, /device:TPU:0, one launch (start us, length us, event | category | flops | bytes accessed | tf_op | source)
XLA Modules:
  0.0 259.7 jit_solution(4243875015120600217)
XLA Ops:
  0.6 1.2 reshape.124.refs_9_
  1.9 0.8 compare_convert_fusion.refs_10_.ones.refs_15_
  2.6 65.9 %first.1 = (bf16[4,1024,512]{2,1,0:T(8,128)(2,1)}, bf16[4,1024,512]{2,1,0:T(8,128)(2,1)}, bf16[4,1024,512]{2,1,0:T(8,128)(2,1)}, bf16[4,1024,512]{2,1,0:T(8,128)...) custom-call(s32[4,8]{1,0:T(4,128)} %bitcast.33, ...), custom_call_target="tpu_custom_call" | custom-call | tf_op jit(solution)/shard_map/first/pallas_call | solution.py:1256
  68.6 89.8 %middle.1 = (bf16[4,1024,512]{2,1,0:T(8,128)(2,1)}, bf16[4,1024,512]{2,1,0:T(8,128)(2,1)}, bf16[4,1024,512]{2,1,0:T(8,128)(2,1)}, bf16[4,1024,512]{2,1,0:T(8,128...) custom-call(s32[4,8]{1,0:T(4,128)} %bitcast.34, ...), custom_call_target="tpu_custom_call" | custom-call | tf_op jit(solution)/shard_map/middle/pallas_call | solution.py:1284
  158.4 93.1 %last.1 = (bf16[4,1024,512]{2,1,0:T(8,128)(2,1)}, bf16[320,512]{1,0:T(8,128)(2,1)}, bf16[256,512]{1,0:T(8,128)(2,1)}, bf16[64,512]{1,0:T(8,128)(2,1)}, bf16[64,5...) custom-call(s32[4,8]{1,0:T(4,128)} %bitcast.35, s32[1]{0:T(128)} %bitcast.1.off, ...), custom_call_target="tpu_custom_call" | custom-call | tf_op jit(solution)/shard_map/last/pallas_call | solution.py:1332
  251.5 8.0 %result.1 = (f32[4,1024,512]{2,1,0:T(8,128)}, f32[64,1536]{1,0:T(8,128)}, f32[64,512]{1,0:T(8,128)}, f32[64,2048]{1,0:T(8,128)}, f32[256,512]{1,0:T(8,128)}, /*i...) custom-call(bf16[4,1024,512]{2,1,0:T(8,128)(2,1)} %get-tuple-element, ...), custom_call_target="tpu_custom_call" | custom-call | tf_op jit(solution)/shard_map/result/pallas_call | solution.py:1357
  (1 shorter events, 0.0 us)

commit v6 on v5

--- a/solution.py
+++ b/solution.py
@@ -854,7 +854,7 @@
     lens, off, q_ref, num_ref, kc_ref, x_ref, cot_ref, state_in, ones,
     w_out, vec, w_up, w_down,
     block_out, gm_out, gnum_out, gden_out, use_out, grads_up, grads_down, g_vec,
-    groups, norm, use, use_norm, acc_out, acc_up, acc_down, total, e_total, h2_ref, h2t_ref, ct_ref,
+    groups, norm, use, use_norm, acc_out, acc_up, acc_down, active_all, g_low_all, h2_ref, h2t_ref, ct_ref,
 ):
     m, t, tiles = pl.program_id(0), pl.program_id(1), pl.num_programs(1)
     rows, d = x_ref.shape
@@ -894,8 +894,6 @@
     h2_ref[...] = h2
     h2t_ref[0:d, :] = h2.T
     ct_ref[...] = cot_ref[...].T
-    total[...] = middle + down_bias
-    e_total[...] = jnp.zeros_like(e_total)
 
     def ffn(f, carry):
         cut = pl.ds(pl.multiple_of(f * FF_TILE, FF_TILE), FF_TILE)
@@ -908,15 +906,15 @@
         active = (hidden * half_up).astype(BF16)
         slope = half_up + hidden * (1.0 - th * th) * (0.5 * c0 + (1.5 * c0 * c1) * square)
         g_low = (slope * pulled).astype(BF16)
-        total[...] += nn(active, w_down[cut, :])
-        e_total[...] += nt(g_low, w_up[:, cut])
+        active_all[:, cut] = active
+        g_low_all[:, cut] = g_low
         acc_down[:, cut] += nn(ct_ref[...], active)
         acc_up[:, cut] += nn(h2t_ref[...], g_low)
         return carry
 
     lax.fori_loop(0, w_up.shape[1] // FF_TILE, ffn, 0, unroll=True)
-    block_out[...] = total[...].astype(BF16)
-    e = e_total[...]
+    block_out[...] = (middle + down_bias + nn(active_all[...], w_down[...])).astype(BF16)
+    e = nt(g_low_all[...], w_up[...])
     cot = cot_ref[...].astype(F32)
     g_middle = cot + norm_back(e, xhat, scale, gain)
     gm_out[...] = g_middle.astype(BF16)
@@ -1297,7 +1295,7 @@
             pltpu.VMEM((2, 256, 256), BF16), pltpu.VMEM((1, d), F32),
             pltpu.VMEM((2, 256, 256), F32), pltpu.VMEM((1, d), F32),
             pltpu.VMEM((d, d), F32), pltpu.VMEM((d + 16, ff), F32), pltpu.VMEM((d, ff), F32),
-            pltpu.VMEM((TILE, d), F32), pltpu.VMEM((TILE, d), F32), pltpu.VMEM((TILE, d), BF16),
+            pltpu.VMEM((TILE, ff), BF16), pltpu.VMEM((TILE, ff), BF16), pltpu.VMEM((TILE, d), BF16),
             pltpu.VMEM((d + 16, TILE), BF16), pltpu.VMEM((d, TILE), BF16),
         ],
         compiler_params=params(2),

time: 260 us -> 261 us (level)
  no operation moved by 1% of the time
where the time goes in v6:
time: 261 us
  Pallas kernels  258 us (99%)
    pallas_call x1, Pallas kernels, per_device(): pl.pallas_call(last_kernel, grid=(p4 + micro,), in_specs=[small(), small(...  93 us
    pallas_call x1, Pallas kernels, per_device(): pl.pallas_call(middle_kernel, grid=(micro, tiles), in_specs=[small(), sma...  91.5 us
    pallas_call x1, Pallas kernels, per_device(): pl.pallas_call(first_kernel, grid=(4 * micro,), in_specs=[small(), small(...  65.9 us
    pallas_call x1, Pallas kernels, per_device(): pl.pallas_call(result_kernel, grid=(micro,), in_specs=[block, block] + [w...  7.95 us

profile of v6, /device:TPU:0, one launch (start us, length us, event | category | flops | bytes accessed | tf_op | source)
XLA Modules:
  0.0 261.2 jit_solution(17513164567031593885)
XLA Ops:
  0.6 1.2 reshape.124.refs_9_
  1.9 0.8 compare_convert_fusion.refs_10_.ones.refs_15_
  2.6 65.9 %first.1 = (bf16[4,1024,512]{2,1,0:T(8,128)(2,1)}, bf16[4,1024,512]{2,1,0:T(8,128)(2,1)}, bf16[4,1024,512]{2,1,0:T(8,128)(2,1)}, bf16[4,1024,512]{2,1,0:T(8,128)...) custom-call(s32[4,8]{1,0:T(4,128)} %bitcast.33, ...), custom_call_target="tpu_custom_call" | custom-call | tf_op jit(solution)/shard_map/first/pallas_call | solution.py:1254
  68.6 91.5 %middle.1 = (bf16[4,1024,512]{2,1,0:T(8,128)(2,1)}, bf16[4,1024,512]{2,1,0:T(8,128)(2,1)}, bf16[4,1024,512]{2,1,0:T(8,128)(2,1)}, bf16[4,1024,512]{2,1,0:T(8,128...) custom-call(s32[4,8]{1,0:T(4,128)} %bitcast.34, ...), custom_call_target="tpu_custom_call" | custom-call | tf_op jit(solution)/shard_map/middle/pallas_call | solution.py:1282
  160.1 93.0 %last.1 = (bf16[4,1024,512]{2,1,0:T(8,128)(2,1)}, bf16[320,512]{1,0:T(8,128)(2,1)}, bf16[256,512]{1,0:T(8,128)(2,1)}, bf16[64,512]{1,0:T(8,128)(2,1)}, bf16[64,5...) custom-call(s32[4,8]{1,0:T(4,128)} %bitcast.35, s32[1]{0:T(128)} %bitcast.1.off, ...), custom_call_target="tpu_custom_call" | custom-call | tf_op jit(solution)/shard_map/last/pallas_call | solution.py:1330
  253.1 8.0 %result.1 = (f32[4,1024,512]{2,1,0:T(8,128)}, f32[64,1536]{1,0:T(8,128)}, f32[64,512]{1,0:T(8,128)}, f32[64,2048]{1,0:T(8,128)}, f32[256,512]{1,0:T(8,128)}, /*i...) custom-call(bf16[4,1024,512]{2,1,0:T(8,128)(2,1)} %get-tuple-element, ...), custom_call_target="tpu_custom_call" | custom-call | tf_op jit(solution)/shard_map/result/pallas_call | solution.py:1355
  (1 shorter events, 0.0 us)
